TPU v7x, 256 devices: a whole 4x4x8 slice. The times are simulated.
256 devices in a mesh: dp: 16 (over x, y), tensor: 16 (over z, core).
Axes of the slice: x: 4, y: 4, z: 8, core: 2. Of those that a mesh axis runs over, the one named last changes fastest.
Arguments:
- activations: bfloat16 [32, 1024, 4096], P('dp', 'tensor'), may hold values from -6 to 6
- out_grads: bfloat16 [32, 1024, 8192], P('dp', None, 'tensor')
- lengths: int32 [32], P('dp'), may hold values from 128 to 1024, as said below
- clip_bound: float32 [1], replicated, may hold values from 2867.2 to 6389.76
- noise: float32 [4096, 8192], P('dp', 'tensor'), may hold values from -4 to 4
Outputs:
- private_grad: float32 [4096, 8192], P('dp', 'tensor')
Inputs may be any that keep to these rules, and one draw needn't show every extreme that they name: `lengths`: at least one example uses all 1024 positions.
All inputs are finite; a program needn't handle non-finite values.
Results may differ from a plain program's by a relative error of at most 0.0003.
Values may be sent and summed in bfloat16 or wider, within the bound.
No kernel may reach another device: no remote copies, remote signals or barrier semaphores. Data moves between devices by JAX's collectives and lax.ppermute only.
A program may use at most 128 MiB of HBM per device.

v0:
```python
import jax
import jax.numpy as jnp
from jax import lax
from jax.sharding import PartitionSpec as P


def per_device(activations, out_grads, lengths, clip_bound, noise):
    gathered = lax.all_gather(activations, "tensor", axis=1, tiled=True)
    positions = lax.broadcasted_iota(jnp.int32, (1, out_grads.shape[1], 1), 1)
    masked = jnp.where(positions < lengths[:, None, None], out_grads, jnp.zeros_like(out_grads))
    clip_value = clip_bound[0]
    grads_gram = jnp.einsum("bsf,btf->bst", masked, masked, preferred_element_type=jnp.float32)
    gram_share = lax.psum_scatter(grads_gram, "tensor", scatter_dimension=1, tiled=True)
    acts_share = jnp.einsum(
        "bsd,btd->bst", activations, gathered, preferred_element_type=jnp.float32
    )
    partial_sq = jnp.sum(acts_share * gram_share, axis=(1, 2))
    scaling = clip_value / jnp.maximum(jnp.sqrt(lax.psum(partial_sq, "tensor")), clip_value)
    products = jnp.einsum("btd,btf->bdf", gathered, masked, preferred_element_type=jnp.float32)
    summed = lax.psum_scatter(
        jnp.sum(scaling[:, None, None] * products, axis=0), "dp", scatter_dimension=0, tiled=True
    )
    example_total = activations.shape[0] * lax.axis_size("dp")
    return summed / jnp.sqrt(jnp.float32(example_total)) + noise


def solution(mesh):
    in_specs = (P("dp", "tensor", None), P("dp", None, "tensor"), P("dp"), P(), P("dp", "tensor"))
    out_specs = P("dp", "tensor")
    return jax.shard_map(
        per_device, mesh=mesh, in_specs=in_specs, out_specs=out_specs, check_vma=False
    )
```

profile of v0, /device:TPU:32, one launch (start us, length us, event | category | flops | bytes accessed | tf_op | source)
XLA Modules:
  0.0 337.4 jit_solution(3799856885796036029)
XLA Ops:
  6.5 0.0 reduce-scatter.3.cloned.1.call-start
  6.5 0.7 iota_compare_fusion
  7.3 0.0 copy-start
  7.3 8.0 %fusion = f32[2,1024,1024]{2,1,0:T(8,128)} fusion(bf16[2,1024,512]{2,1,0:T(8,128)(2,1)} %param.6, pred[2,1024]{1,0:T(4,128)(4,1)S(1)} %iota_compare_fusion), kind=kOutput, calls=%fused_computation.2 | convolution fusion | flops 2148532224 | bytes 10487808 | tf_op jit(solution)/shard_map/bsf,btf->bst/dot_general | solution.py:12
  15.3 0.0 reduce-scatter.3.cloned.1.call-update
  15.3 0.0 all-gather.2.cloned.1.call-start
  15.3 0.7 all-gather.2.cloned.1.call-update
  16.0 0.0 copy-start.2
  16.0 0.0 reduce-scatter.5.cloned.1.call-start
  16.1 69.0 %reduce-scatter.3.cloned.1.call-done = f32[2,64,1024]{2,1,0:T(8,128)} async-done(((f32[2,1024,1024]{2,1,0:T(8,128)}), f32[2,64,1024]{2,1,0:T(8,128)}) %reduce-scatter.3.cloned.1.call-update) | async-done | bytes 524304 | tf_op jit(solution)/shard_map/reduce_scatter | solution.py:13
  85.0 97.7 %all-gather.2.cloned.1.call-done = bf16[2,1024,4096]{2,1,0:T(8,128)(2,1)} async-done(((bf16[2,64,4096]{2,1,0:T(8,128)(2,1)}), bf16[2,1024,4096]{2,1,0:T(8,128)(2,1)}) %all-gather.2.cloned.1.call-update) | async-done | bytes 16777232 | tf_op jit(solution)/shard_map/all_gather | solution.py:8
  182.8 0.0 copy-done
  182.8 11.1 %fusion.1 = f32[2]{0:T(128)S(1)} fusion(f32[2,64,1024]{2,1,0:T(8,128)} %reduce-scatter.3.cloned.1.call-done, bf16[2,64,4096]{2,1,0:T(8,128)(2,1)S(1)} %copy-done, bf16[2,1024,4096]{2,1,0:T(8,128)(2,1)} %all-gather.2.cloned.1.call-done), kind=kOutput, calls=%fused_computation.4 | convolution fusion | flops 1074003968 | bytes 18350088 | tf_op jit(solution)/shard_map/bsd,btd->bst/dot_general | solution.py:14
  194.5 23.9 %psum.7 = f32[2]{0:T(128)S(1)} all-reduce(f32[2]{0:T(128)S(1)} %fusion.1), channel_id=1, replica_groups=mesh['dp'=16,'tensor'=16] {'tensor'}, use_global_device_ids=true, to_apply=%region_2.3 | all-reduce | flops 2 | bytes 16 | tf_op jit(solution)/shard_map/psum | solution.py:18
  218.4 0.0 copy-done.2
  218.4 17.4 %multiply_reduce_fusion = f32[512,4096]{1,0:T(8,128)} fusion(f32[2]{0:T(128)S(1)} %maximum_divide_fusion, bf16[2,1024,4096]{2,1,0:T(8,128)(2,1)} %all-gather.2.cloned.1.call-done, bf16[2,1024,512]{2,1,0:T(8,128)(2,1)S(1)} %copy-done.2, pred[2,1024]{1,0:T(4,128)(4,1)S(1)} %iota_compare_fusion), kind=kOutput, calls=%fused_computation | convolution fusion | flops 8597274624 | bytes 27265032 | tf_op jit(solution)/shard_map/btd,btf->bdf/dot_general | solution.py:19
  235.8 0.0 copy-start.1
  235.8 0.0 reduce-scatter.5.cloned.1.call-update
  235.8 1.0 copy-done.1
  236.8 0.2 copy.8
  237.0 91.7 %reduce-scatter.5.cloned.1.call-done = f32[256,512]{0,1:T(8,128)} async-done(((f32[4096,512]{0,1:T(8,128)}), f32[256,512]{0,1:T(8,128)}) %reduce-scatter.5.cloned.1.call-update) | async-done | bytes 524304 | tf_op jit(solution)/shard_map/reduce_scatter | solution.py:20
  328.7 1.1 multiply_add_fusion
  329.8 1.0 copy.9
  (1 shorter events, 0.0 us)
Async XLA Ops:
  6.5 78.5 %reduce-scatter.3.cloned.1.call-start = ((), (), s32[]{:S(2)}) async-start(), calls=%async_computation.3 | async-start | bytes 8912896 | tf_op jit(solution)/shard_map/reduce_scatter | solution.py:13
  7.3 175.5 %copy-start = (bf16[2,64,4096]{2,1,0:T(8,128)(2,1)S(1)}, bf16[2,64,4096]{2,1,0:T(8,128)(2,1)}, u32[]{:S(2)}) copy-start(bf16[2,64,4096]{2,1,0:T(8,128)(2,1)} %param.5) | copy-start | bytes 3145732
  15.3 167.5 %all-gather.2.cloned.1.call-start = ((), (), s32[]{:S(2)}) async-start(), calls=%async_computation.2 | async-start | bytes 17825792 | tf_op jit(solution)/shard_map/all_gather | solution.py:8
  16.0 202.4 %copy-start.2 = (bf16[2,1024,512]{2,1,0:T(8,128)(2,1)S(1)}, bf16[2,1024,512]{2,1,0:T(8,128)(2,1)}, u32[]{:S(2)}) copy-start(bf16[2,1024,512]{2,1,0:T(8,128)(2,1)} %param.6) | copy-start | bytes 6291460
  16.0 312.7 %reduce-scatter.5.cloned.1.call-start = ((), (), s32[]{:S(2)}) async-start(), calls=%async_computation.4 | async-start | bytes 8912896 | tf_op jit(solution)/shard_map/reduce_scatter | solution.py:20
  235.8 1.0 copy-start.1
Sparse Core Ops, SparseCore 0:
  15.4 69.5 reduce-scatter.2
  86.9 95.8 all-gather.1
  235.9 92.7 reduce-scatter.4
where the time goes:
time: 338 us; the launch traced here: 337 us
  waiting for transfers between devices  259 us (77%)
  matrix products  36.5 us (11%)
  blocking collectives  23.9 us (7%)
  between operations  13.8 us (4%)
    all_gather x1, waiting for transfers between devices, per_device(): gathered = lax.all_gather(activations, 'tensor', axis=1, tiled=True)  97.7 us
    reduce_scatter x1, waiting for transfers between devices, per_device(): lax.psum_scatter(jnp.sum(scaling[:, None, None] * products, axis=0), 'dp'...  91.7 us
    reduce_scatter x1, waiting for transfers between devices, per_device(): lax.psum_scatter(grads_gram, 'tensor', scatter_dimension=1, tiled=True)  69 us
    psum x1, blocking collectives, per_device(): lax.psum(partial_sq, 'tensor')  23.9 us
    dot_general x1, matrix products, per_device(): jnp.einsum('btd,btf->bdf', gathered, masked, preferred_element_type=jnp.f...  17.4 us
    dot_general x1, matrix products, per_device(): jnp.einsum('bsd,btd->bst', activations, gathered, preferred_element_type=...  11.1 us
    dot_general x1, matrix products, per_device(): jnp.einsum('bsf,btf->bst', masked, masked, preferred_element_type=jnp.flo...  7.99 us
  transfers between devices with their start and end apart: 3, of which 3 were waited for; matrix products, arithmetic and copies ran while one was open for 0% of the time, Pallas kernels for 0%

commit v1 on v0

v1 whole, which is shorter than its diff:
```python
import functools

import jax
import jax.numpy as jnp
from jax import lax
from jax.experimental import pallas as pl
from jax.experimental.pallas import tpu as pltpu
from jax.sharding import PartitionSpec as P

LANES = 128
EXTRA = 16
TOGETHER = 4
LEAST = 1e-33
PARAMS = pltpu.CompilerParams(vmem_limit_bytes=56 * 1024 * 1024)
RAW = ((0, 64), (64, 32))
CLIPPED = ((128, 128), (96, 32))
OWNED = sum(width for _, width in RAW + CLIPPED)
ARRIVALS = (0, -1, 1, -2, 2, -3, 3, 4)
SMALL = pl.CostEstimate(flops=1, bytes_accessed=1, transcendentals=0)


def part_kernel(parts, acts_ref, part_ref):
    at = 0
    for first, width in parts:
        for tile in range(acts_ref.shape[1] // OWNED * width // LANES):
            owners = range(tile * LANES // width, (tile + 1) * LANES // width)
            pieces = [acts_ref[:, o * OWNED + first : o * OWNED + first + width] for o in owners]
            part_ref[:, at : at + LANES] = jnp.concatenate(pieces, axis=1) if len(pieces) > 1 else pieces[0]
            at += LANES


def part_features(acts, parts):
    examples, shard, features = acts.shape
    taken = features // OWNED * sum(width for _, width in parts)
    return pl.pallas_call(
        functools.partial(part_kernel, parts),
        out_shape=jax.ShapeDtypeStruct((examples * shard, taken), acts.dtype),
        compiler_params=PARAMS,
    )(acts.reshape(examples * shard, features)).reshape(examples, shard, taken)


def coded(values):
    top = jnp.maximum(jnp.max(jnp.abs(values), axis=0, keepdims=True), LEAST)
    exponent = jnp.ceil(jnp.log2(top) - 14.99)
    return jnp.round(values * jnp.exp2(-exponent)), exponent


def narrow(units):
    return units.astype(jnp.int32).astype(jnp.int16)


def packed(tile, owners):
    if owners == 1:
        return [tile]
    width, rows = LANES // owners, tile.shape[0] // owners
    lane = lax.broadcasted_iota(jnp.int32, (rows, LANES), 1)
    out = []
    for owner in range(owners):
        total = None
        for group in range(owners):
            piece = tile[group * rows : (group + 1) * rows]
            shift = (group - owner) * width % LANES
            piece = pltpu.roll(piece, shift, 1) if shift else piece
            total = piece if total is None else jnp.where(lane >= group * width, piece, total)
        out.append(total)
    return out


def packed_row(row, owners):
    return [t[0:1] for t in packed(jnp.broadcast_to(row, (8 * owners, LANES)), owners)]


def lane_sums(product):
    rows = jnp.sum(product * product, axis=0, keepdims=True)
    return sum(rows[:, at : at + LANES] for at in range(0, rows.shape[1], LANES))


def raw_kernel(order_ref, *refs):
    pieces, (grads_ref, coded_ref, exponent_ref, squares_ref, acts, grads, sems) = refs[:-7], refs[-7:]
    example = pl.program_id(0)
    depth = pieces[0].shape[1]

    def copies(e):
        far = pieces[-4 + 2 * e : len(pieces) - 2 + 2 * e]
        sources = [p.at[e] for p in pieces[:-4]] + [p.at[0] for p in far]
        made = [pltpu.make_async_copy(grads_ref.at[e], grads.at[e], sems.at[e, len(sources)])]
        for k, source in enumerate(sources):
            place = pl.ds(pl.multiple_of(order_ref[k] * depth, depth), depth)
            made.append(pltpu.make_async_copy(source, acts.at[e, place], sems.at[e, k]))
        return made

    @pl.when(example == 0)
    def _():
        for copy in copies(0) + copies(1):
            copy.start()
        for copy in copies(0):
            copy.wait()

    @pl.when(example == 1)
    def _():
        for copy in copies(1):
            copy.wait()

    product = jnp.dot(grads[example], acts[example], preferred_element_type=jnp.float32)
    squares_ref[0] = lane_sums(product)
    at = row = 0
    for h, (_, width) in enumerate(RAW):
        together = LANES // width
        rows = product.shape[0] // together
        for tile in range(coded_ref.shape[0] // together):
            units, exponent = coded(product[:, at : at + LANES])
            exponents = packed_row(exponent, together)
            for k, block in enumerate(packed(units, together)):
                coded_ref[tile * together + k, 0, row : row + rows] = narrow(block)
                exponent_ref[tile * together + k, 0, h : h + 1] = exponents[k]
            at += LANES
        row += rows


def raw_products(order, pieces, grads):
    examples, shard, features = pieces[0].shape
    _, columns, positions = grads.shape
    owners = features // sum(width for _, width in RAW)
    rows = columns * features // owners // LANES
    return pl.pallas_call(
        raw_kernel,
        grid=(examples,),
        in_specs=[pl.BlockSpec(memory_space=pltpu.SMEM)]
        + [pl.BlockSpec(memory_space=pltpu.HBM)] * (len(pieces) + 1),
        out_specs=[
            pl.BlockSpec((owners, 1, rows, LANES), lambda e: (0, e, 0, 0)),
            pl.BlockSpec((owners, 1, 8, LANES), lambda e: (0, e, 0, 0)),
            pl.BlockSpec((1, 1, LANES), lambda e: (e, 0, 0)),
        ],
        out_shape=[
            jax.ShapeDtypeStruct((owners, examples, rows, LANES), jnp.int16),
            jax.ShapeDtypeStruct((owners, examples, 8, LANES), jnp.float32),
            jax.ShapeDtypeStruct((examples, 1, LANES), jnp.float32),
        ],
        scratch_shapes=[
            pltpu.VMEM((examples, positions, features), pieces[0].dtype),
            pltpu.VMEM(grads.shape, grads.dtype),
            pltpu.SemaphoreType.DMA((examples, len(order) + 1)),
        ],
        compiler_params=PARAMS,
    )(order, *pieces, grads)


def plain_kernel(acts_ref, grads_ref, squares_ref, product_ref, share_ref):
    devices, _, shard, width = acts_ref.shape
    acts = acts_ref[...].reshape(devices * shard, width)
    product = jnp.dot(grads_ref[0], acts, preferred_element_type=jnp.float32)
    product_ref[0] = product

    @pl.when(pl.program_id(1) == 0)
    def _():
        share_ref[...] = squares_ref[...]

    share_ref[0] += lane_sums(product)


def plain_products(acts, grads, squares):
    devices, examples, shard, features = acts.shape
    _, columns, positions = grads.shape
    width = features // 2
    row = pl.BlockSpec((1, 1, LANES), lambda e, i: (e, 0, 0))
    return pl.pallas_call(
        plain_kernel,
        grid=(examples, features // width),
        in_specs=[
            pl.BlockSpec((devices, 1, shard, width), lambda e, i: (0, e, 0, i)),
            pl.BlockSpec((1, columns, positions), lambda e, i: (e, 0, 0)),
            row,
        ],
        out_specs=[pl.BlockSpec((1, columns, width), lambda e, i: (e, 0, i)), row],
        out_shape=[
            jax.ShapeDtypeStruct((examples, columns, features), jnp.float32),
            jax.ShapeDtypeStruct((examples, 1, LANES), jnp.float32),
        ],
        cost_estimate=SMALL,
        compiler_params=PARAMS,
    )(acts, grads, squares)


def clipped_kernel(clip_ref, shares_ref, wide_ref, thin_ref, exponent_ref, coded_ref):
    examples, columns, _ = wide_ref.shape
    owners = coded_ref.shape[0]
    clip = clip_ref[0]
    blank = jnp.zeros((1, LANES), jnp.float32)
    wide, thin, extra = 0.0, 0.0, [[] for _ in range(owners)]
    for e in range(examples):
        square = jnp.sum(shares_ref[e], axis=1, keepdims=True)
        factor = clip / jnp.maximum(jnp.sqrt(square), clip)
        wide = wide + factor * wide_ref[e]
        thin = thin + factor * thin_ref[e]
        power = jnp.floor(jnp.log2(jnp.maximum(factor, LEAST))) + 1.0
        scaled = factor * jnp.exp2(-power) * 16384.0
        high = jnp.floor(scaled)
        low = jnp.round((scaled - high) * 16384.0)
        for k in range(owners):
            extra[k] += [blank + high, blank + low]
            extra[k] += [exponent_ref[k, e, h : h + 1] + power for h in range(len(RAW))]
    thin_units, exponent = coded(thin)
    thin_units, thin_exponents = packed(thin_units, owners), packed_row(exponent, owners)
    for k in range(owners):
        units, exponent = coded(wide[:, k * LANES : (k + 1) * LANES])
        rows = extra[k] + [exponent, thin_exponents[k]]
        rows = jnp.concatenate(rows + [blank] * (EXTRA - len(rows)), axis=0)
        coded_ref[k, :columns] = narrow(units)
        coded_ref[k, columns : coded_ref.shape[1] - EXTRA] = narrow(thin_units[k])
        coded_ref[k, coded_ref.shape[1] - EXTRA :] = narrow(rows)


def clipped_sums(clip_bound, shares, products, exponents):
    examples, columns, features = products.shape
    owners = exponents.shape[0]
    together = LANES // CLIPPED[1][1]
    rows = columns * features // owners // LANES + EXTRA
    return pl.pallas_call(
        clipped_kernel,
        grid=(owners // together,),
        in_specs=[
            pl.BlockSpec(memory_space=pltpu.SMEM),
            pl.BlockSpec(shares.shape, lambda i: (0, 0, 0)),
            pl.BlockSpec((examples, columns, together * LANES), lambda i: (0, 0, i)),
            pl.BlockSpec((examples, columns, LANES), lambda i: (0, 0, owners + i)),
            pl.BlockSpec((together, examples, 8, LANES), lambda i: (i, 0, 0, 0)),
        ],
        out_specs=pl.BlockSpec((together, rows, LANES), lambda i: (i, 0, 0)),
        out_shape=jax.ShapeDtypeStruct((owners, rows, LANES), jnp.int16),
        cost_estimate=SMALL,
        compiler_params=PARAMS,
    )(clip_bound, shares, products, products, exponents)


def finish_kernel(scale, raw_ref, clipped_ref, noise_ref, out_ref, raw_sum, clipped_sum):
    _, examples, _, _ = raw_ref.shape
    columns = out_ref.shape[1]
    group = pl.program_id(0)

    @pl.when(group == 0)
    def _():
        raw_sum[...] = jnp.zeros_like(raw_sum)
        clipped_sum[...] = jnp.zeros_like(clipped_sum)

    kinds = len(RAW)
    bottom = clipped_sum.shape[0]
    extra = [clipped_ref[g, bottom:].astype(jnp.float32) for g in range(TOGETHER)]
    at = 0
    for h, (_, width) in enumerate(RAW):
        rows = columns * width // LANES
        total = raw_sum[at : at + rows]
        for g in range(TOGETHER):
            row = lambda k: extra[g][k : k + 1]
            for e in range(examples):
                base = e * (2 + kinds)
                weight = (row(base) + row(base + 1) * (1.0 / 16384.0)) * (1.0 / 16384.0) * jnp.exp2(row(base + 2 + h))
                total = total + weight * raw_ref[g, e, at : at + rows].astype(jnp.float32)
        raw_sum[at : at + rows] = total
        at += rows
    at = 0
    for h, (_, width) in enumerate(CLIPPED):
        rows = columns * width // LANES
        total = clipped_sum[at : at + rows]
        for g in range(TOGETHER):
            k = examples * (2 + kinds) + h
            total = total + jnp.exp2(extra[g][k : k + 1]) * clipped_ref[g, at : at + rows].astype(jnp.float32)
        clipped_sum[at : at + rows] = total
        at += rows

    @pl.when(group == pl.num_programs(0) - 1)
    def _():
        for sums, parts in ((raw_sum, RAW), (clipped_sum, CLIPPED)):
            at = 0
            for first, width in parts:
                together = LANES // width
                rows = columns // together
                turned = sums[at : at + rows].T
                for k in range(together):
                    here = (slice(first, first + width), slice(k * rows, (k + 1) * rows))
                    out_ref[here] = turned[k * width : (k + 1) * width] * scale + noise_ref[here]
                at += rows


def finish(raw, clipped, noise, scale):
    groups, examples, raw_rows, _ = raw.shape
    rows = clipped.shape[1]
    whole = pl.BlockSpec(noise.shape, lambda g: (0, 0))
    return pl.pallas_call(
        functools.partial(finish_kernel, scale),
        grid=(groups // TOGETHER,),
        in_specs=[
            pl.BlockSpec((TOGETHER, examples, raw_rows, LANES), lambda g: (g, 0, 0, 0)),
            pl.BlockSpec((TOGETHER, rows, LANES), lambda g: (g, 0, 0)),
            whole,
        ],
        out_specs=whole,
        out_shape=jax.ShapeDtypeStruct(noise.shape, jnp.float32),
        scratch_shapes=[pltpu.VMEM((raw_rows, LANES), jnp.float32), pltpu.VMEM((rows - EXTRA, LANES), jnp.float32)],
        compiler_params=PARAMS,
    )(raw, clipped, noise)


def per_device(activations, out_grads, lengths, clip_bound, noise):
    owners = lax.axis_size("dp")
    devices = lax.axis_size("tensor")
    examples = activations.shape[0]
    here = lax.axis_index("tensor")

    def along_z(x, k):
        return lax.ppermute(x, "tensor", [(t, (t + 2 * k) % devices) for t in range(devices)])

    def crossed(x, k):
        return lax.ppermute(x, "tensor", [(t, t ^ k) for t in range(devices)])

    own = part_features(activations, RAW)
    second = part_features(activations, CLIPPED)
    positions = lax.broadcasted_iota(jnp.int32, (1, out_grads.shape[1], 1), 1)
    masked = jnp.where(positions < lengths[:, None, None], out_grads, jnp.zeros_like(out_grads))
    masked = jnp.swapaxes(masked, 1, 2)

    up1, down1 = along_z(own, 1), along_z(own, -1)
    up1, down1, second = lax.optimization_barrier((up1, down1, second))
    second = lax.all_gather(second, "tensor")
    up2, down2 = along_z(up1, 1), along_z(down1, -1)
    up2, down2, masked = lax.optimization_barrier((up2, down2, masked))
    up3, down3 = along_z(up2, 1), along_z(down2, -1)
    up4, down4 = along_z(up3[:1], 1), along_z(down3[1:], -1)
    pieces = []
    for piece in (own, up1, down1, up2, down2, up3, down3):
        pieces += [piece, crossed(piece, 1)]
    pieces += [up4, crossed(up4, 1), down4, crossed(down4, 1)]
    step = jnp.array([2 * k for k in ARRIVALS for _ in range(2)], jnp.int32)
    second_core = jnp.array([0, 1] * len(ARRIVALS), jnp.int32)
    order = ((here & ~1) + step + ((here & 1) ^ second_core)) & (devices - 1)

    raw, exponents, squares = raw_products(order, pieces, masked)
    raw = lax.all_to_all(raw, "dp", 0, 0)
    products, share = plain_products(second, masked, squares)
    share = share + crossed(share, 1) + crossed(share, 2) + crossed(share, 3)
    share = share + crossed(share, 4) + crossed(share, 8) + crossed(share, 12)
    clipped = clipped_sums(clip_bound, share, products, exponents)
    clipped, raw = lax.optimization_barrier((clipped, raw))
    clipped = lax.all_to_all(clipped, "dp", 0, 0)
    return finish(raw, clipped, noise, float((examples * owners) ** -0.5))


def solution(mesh):
    in_specs = (P("dp", "tensor", None), P("dp", None, "tensor"), P("dp"), P(), P("dp", "tensor"))
    out_specs = P("dp", "tensor")
    return jax.shard_map(
        per_device, mesh=mesh, in_specs=in_specs, out_specs=out_specs, check_vma=False
    )
```

time: 338 us -> 190 us (0.56)
  waiting for transfers between devices: 259 us -> 60.6 us
  Pallas kernels: 0 us -> 38.7 us
  matrix products: 36.5 us -> 0 us
  starting transfers between devices: 0.08 us -> 25.9 us
  blocking collectives: 23.9 us -> 41.4 us
    reduce_scatter x2 -> x0, waiting for transfers between devices: 161 us -> none  [the longest x1 91.7 us: per_device(): lax.psum_scatter(jnp.sum(scaling[:, None, None] * products, axis=0), 'dp'...]
    all_gather x1, waiting for transfers between devices: 97.7 us -> 9.74 us  [per_device(): second = lax.all_gather(second, 'tensor')]
    ppermute x0 -> x23, waiting for transfers between devices: none -> 50.8 us  [the longest x8 43.7 us: along_z(): lax.ppermute(x, 'tensor', [(t, (t + 2 * k) % devices) for t in range(devi...]
    all_to_all x0 -> x1, blocking collectives: none -> 41.4 us  [per_device(): clipped = lax.all_to_all(clipped, 'dp', 0, 0)]
    pallas_call x0 -> x6, Pallas kernels: none -> 38.7 us  [the longest x1 11.9 us: plain_products(): pl.pallas_call(plain_kernel, grid=(examples, features // width), in_specs...]
    dot_general x3 -> x0, matrix products: 36.5 us -> none  [the longest x1 17.4 us: per_device(): jnp.einsum('btd,btf->bdf', gathered, masked, preferred_element_type=jnp.f...]
    psum x1 -> x0, blocking collectives: 23.9 us -> none  [per_device(): lax.psum(partial_sq, 'tensor')]
    ppermute x0 -> x23, starting transfers between devices: none -> 18.8 us  [the longest x15 9.56 us: crossed(): return lax.ppermute(x, 'tensor', [(t, t ^ k) for t in range(devices)])]
  transfers between devices with their start and end apart: 3 -> 25, of which waited for: 3 -> 14; matrix products, arithmetic and copies ran while one was open for 0% -> 4% of each run, Pallas kernels for 0% -> 17%
where the time goes in v1:
time: 190 us; the launch traced here: 189 us
  waiting for transfers between devices  60.6 us (32%)
  blocking collectives  41.4 us (22%)
  Pallas kernels  38.7 us (20%)
  starting transfers between devices  25.9 us (14%)
  between operations  14.2 us (7%)
  local copies, waits for them, and re-layouts  5.24 us (3%)
  other arithmetic  3.38 us (2%)
    ppermute x8, waiting for transfers between devices, along_z(): lax.ppermute(x, 'tensor', [(t, (t + 2 * k) % devices) for t in range(devi...  43.7 us
    all_to_all x1, blocking collectives, per_device(): clipped = lax.all_to_all(clipped, 'dp', 0, 0)  41.4 us
    pallas_call x1, Pallas kernels, plain_products(): pl.pallas_call(plain_kernel, grid=(examples, features // width), in_specs...  11.9 us
    pallas_call x1, Pallas kernels, raw_products(): pl.pallas_call(raw_kernel, grid=(examples,), in_specs=[pl.BlockSpec(memor...  9.99 us
    all_gather x1, waiting for transfers between devices, per_device(): second = lax.all_gather(second, 'tensor')  9.74 us
    ppermute x15, starting transfers between devices, crossed(): return lax.ppermute(x, 'tensor', [(t, t ^ k) for t in range(devices)])  9.56 us
    ppermute x8, starting transfers between devices, along_z(): lax.ppermute(x, 'tensor', [(t, (t + 2 * k) % devices) for t in range(devi...  9.29 us
    ppermute x15, waiting for transfers between devices, crossed(): return lax.ppermute(x, 'tensor', [(t, t ^ k) for t in range(devices)])  7.16 us
  transfers between devices with their start and end apart: 25, of which 14 were waited for; matrix products, arithmetic and copies ran while one was open for 4% of the time, Pallas kernels for 17%

profile of v1, /device:TPU:32, one launch (start us, length us, event | category | flops | bytes accessed | tf_op | source)
XLA Modules:
  0.0 189.4 jit_solution(14566243784200453070)
XLA Ops:
  6.5 2.2 %shard_map.73 = bf16[128,1536]{1,0:T(8,128)(2,1)} custom-call(bf16[128,4096]{1,0:T(8,128)(2,1)} %bitcast.7), custom_call_target="tpu_custom_call" | custom-call | tf_op jit(solution)/shard_map/pallas_call | solution.py:35
  8.8 1.9 %collective-permute-start = (bf16[2,64,1536]{2,1,0:T(8,128)(2,1)}, bf16[2,64,1536]{2,1,0:T(8,128)(2,1)S(1)}, u32[]{:S(2)}, u32[]{:S(2)}) collective-permute-start(bf16[2,64,1536]{2,1,0:T(8,128)(2,1)} %bitcast.10), channel_id=1, source_target_pairs={{0,2},{1,3},{2,4},{3,5},{4,6},{5,7},{6,8},{7,9},{8,10},{9,11},{10,... | collective-permute-start | bytes 1179656 | tf_op jit(solution)/shard_map/ppermute | solution.py:311
  10.7 0.1 collective-permute-start.1
  10.8 2.3 %shard_map.74 = bf16[128,2560]{1,0:T(8,128)(2,1)} custom-call(bf16[128,4096]{1,0:T(8,128)(2,1)} %bitcast.8), custom_call_target="tpu_custom_call" | custom-call | tf_op jit(solution)/shard_map/pallas_call | solution.py:35
  13.1 6.8 %collective-permute-done.refs_2_ = bf16[2,64,1536]{2,1,0:T(8,128)(2,1)S(1)} collective-permute-done((bf16[2,64,1536]{2,1,0:T(8,128)(2,1)}, bf16[2,64,1536]{2,1,0:T(8,128)(2,1)S(1)}, u32[]{:S(2)}, u32[]{:S(2)}) %collective-permute-start) | collective-permute-done | bytes 393248 | tf_op jit(solution)/shard_map/ppermute | solution.py:311
  19.8 1.8 collective-permute-done.1.refs_4_
  21.7 3.2 %collective-permute-start.2 = (bf16[2,64,1536]{2,1,0:T(8,128)(2,1)S(1)}, bf16[2,64,1536]{2,1,0:T(8,128)(2,1)}, u32[]{:S(2)}, u32[]{:S(2)}) collective-permute-start(bf16[2,64,1536]{2,1,0:T(8,128)(2,1)S(1)} %collective-permute-done.refs_2_), channel_id=1, source_target_pairs={{0,2},{1,3},{2,4},{3,5},{4,6},{5,7},{6,8},{7,9},{8,10},{9,11},{10,... | collective-permute-start | bytes 1179656 | tf_op jit(solution)/shard_map/ppermute | solution.py:311
  25.0 3.0 %copy.9 = bf16[2,1024,512]{1,2,0:T(8,128)(2,1)S(1)} copy(bf16[2,1024,512]{2,1,0:T(8,128)(2,1)} %param.8) | data formatting | bytes 4194304 | tf_op args[1]
  28.0 1.5 select_bitcast_fusion.refs_18_.grads_ref
  29.6 3.3 %collective-permute-done.2.refs_6_ = bf16[2,64,1536]{2,1,0:T(8,128)(2,1)} collective-permute-done((bf16[2,64,1536]{2,1,0:T(8,128)(2,1)S(1)}, bf16[2,64,1536]{2,1,0:T(8,128)(2,1)}, u32[]{:S(2)}, u32[]{:S(2)}) %collective-permute-start.2) | collective-permute-done | bytes 393248 | tf_op jit(solution)/shard_map/ppermute | solution.py:311
  32.8 2.7 %collective-permute-done.3.refs_8_ = bf16[2,64,1536]{2,1,0:T(8,128)(2,1)} collective-permute-done((bf16[2,64,1536]{2,1,0:T(8,128)(2,1)S(1)}, bf16[2,64,1536]{2,1,0:T(8,128)(2,1)}, u32[]{:S(2)}, u32[]{:S(2)}) %collective-permute-start.3) | collective-permute-done | bytes 393248 | tf_op jit(solution)/shard_map/ppermute | solution.py:311
  35.6 1.7 collective-permute-start.9
  37.3 0.3 collective-permute-start.11
  37.6 0.5 collective-permute-start.5
  38.1 0.1 collective-permute-start.6
  38.2 16.7 %collective-permute-done.9.refs_10_ = bf16[2,64,1536]{2,1,0:T(8,128)(2,1)S(1)} collective-permute-done((bf16[2,64,1536]{2,1,0:T(8,128)(2,1)}, bf16[2,64,1536]{2,1,0:T(8,128)(2,1)S(1)}, u32[]{:S(2)}, u32[]{:S(2)}) %collective-permute-start.9) | collective-permute-done | bytes 393248 | tf_op jit(solution)/shard_map/ppermute | solution.py:311
  54.9 1.8 collective-permute-done.11.refs_12_
  56.7 1.7 collective-permute-start.13
  58.4 0.7 slice.9
  59.1 0.3 collective-permute-start.15
  59.5 0.5 collective-permute-start.10
  59.9 0.1 collective-permute-start.12
  60.1 8.0 %collective-permute-done.13.refs_14_ = bf16[1,64,1536]{2,1,0:T(8,128)(2,1)} collective-permute-done((bf16[1,64,1536]{2,1,0:T(8,128)(2,1)S(1)}, bf16[1,64,1536]{2,1,0:T(8,128)(2,1)}, u32[]{:S(2)}, u32[]{:S(2)}) %collective-permute-start.13) | collective-permute-done | bytes 196640 | tf_op jit(solution)/shard_map/ppermute | solution.py:311
  68.0 2.6 %collective-permute-done.15.refs_16_ = bf16[1,64,1536]{2,1,0:T(8,128)(2,1)} collective-permute-done((bf16[1,64,1536]{2,1,0:T(8,128)(2,1)}, bf16[1,64,1536]{2,1,0:T(8,128)(2,1)}, u32[]{:S(2)}, u32[]{:S(2)}) %collective-permute-start.15) | collective-permute-done | bytes 196640 | tf_op jit(solution)/shard_map/ppermute | solution.py:311
  70.7 0.5 add_and_fusion.order_ref
  71.2 1.1 collective-permute-done.16.refs_17_
  72.4 0.6 copy-done.13
  73.0 0.1 copy-done.10
  73.1 0.8 copy-done.11
  73.9 10.0 %shard_map.75 = (s16[16,2,384,128]{3,2,1,0:T(8,128)(2,1)}, f32[16,2,8,128]{3,2,1,0:T(8,128)}, f32[2,1,128]{2,1,0:T(1,128)}) custom-call(s32[16]{0:T(128)} %add_and_fusion.order_ref, bf16[2,64,1536]{2,1,0:T(8,128)(2,1)} %bitcast.12, bf16[2,64,1536]{2,1,0:T(8,128)(2,1)} %copy-done.6, bf16[2,64,1536]{2,1,0:T(8,128)(2,1)} %copy-done.4, ...), custom_call_target="tpu_custom_call" | custom-call | tf_op jit(solution)/shard_map/pallas_call | solution.py:125
  83.9 7.1 %all-to-all-start = ((s16[16,2,384,128]{3,2,1,0:T(8,128)(2,1)}), s16[16,2,384,128]{3,2,1,0:T(8,128)(2,1)S(1)}, u32[]{:S(2)}, u32[]{:S(2)}) async-start(s16[16,2,384,128]{3,2,1,0:T(8,128)(2,1)} %get-tuple-element.28), calls=%async_computation | async-start | bytes 6291456 | tf_op jit(solution)/shard_map/all_to_all | solution.py:338
  90.9 9.7 %all-gather.3.cloned.1.call-done = bf16[32,64,2560]{2,1,0:T(8,128)(2,1)} async-done(((bf16[2,64,2560]{2,1,0:T(8,128)(2,1)}), bf16[32,64,2560]{2,1,0:T(8,128)(2,1)}) %all-gather.3.cloned.1.call-update) | async-done | bytes 10485776 | tf_op jit(solution)/shard_map/all_gather | solution.py:324
  100.7 11.9 %shard_map.76 = (f32[2,512,2560]{2,1,0:T(8,128)}, f32[2,1,128]{2,1,0:T(1,128)}) custom-call(bf16[16,2,64,2560]{3,2,1,0:T(8,128)(2,1)} %bitcast.6, bf16[2,512,1024]{2,1,0:T(8,128)(2,1)} %select_bitcast_fusion.refs_18_.grads_ref, f32[2,1,128]{2,1,0:T(1,128)} %get-tuple-element.24.squares_ref), custom_call_target="tpu_custom_call" | custom-call | flops 1 | bytes 1 | tf_op jit(solution)/shard_map/pallas_call | solution.py:167
  112.6 0.3 collective-permute-start.17
  112.9 1.0 collective-permute-start.18
  113.9 0.6 collective-permute-start.19
  114.5 2.2 %collective-permute-done.18 = f32[2,1,128]{2,1,0:T(1,128)S(1)} collective-permute-done((f32[2,1,128]{2,1,0:T(1,128)}, f32[2,1,128]{2,1,0:T(1,128)S(1)}, u32[]{:S(2)}, u32[]{:S(2)}) %collective-permute-start.18) | collective-permute-done | bytes 1056 | tf_op jit(solution)/shard_map/ppermute | solution.py:314
  116.7 0.5 collective-permute-done.19
  117.1 0.7 add_add_fusion.1
  117.8 2.9 %collective-permute-start.20 = (f32[2,1,128]{2,1,0:T(1,128)S(1)}, f32[2,1,128]{2,1,0:T(1,128)S(1)}, u32[]{:S(2)}, u32[]{:S(2)}) collective-permute-start(f32[2,1,128]{2,1,0:T(1,128)S(1)} %add_add_fusion.1), channel_id=1, source_target_pairs={{0,4},{1,5},{2,6},{3,7},{4,0},{5,1},{6,2},{7,3},{8,12},{9,13},{10,... | collective-permute-start | bytes 3080 | tf_op jit(solution)/shard_map/ppermute | solution.py:314
  120.7 2.0 %collective-permute-start.21 = (f32[2,1,128]{2,1,0:T(1,128)S(1)}, f32[2,1,128]{2,1,0:T(1,128)S(1)}, u32[]{:S(2)}, u32[]{:S(2)}) collective-permute-start(f32[2,1,128]{2,1,0:T(1,128)S(1)} %add_add_fusion.1), channel_id=1, source_target_pairs={{0,8},{1,9},{2,10},{3,11},{4,12},{5,13},{6,14},{7,15},{8,0},{9,1},... | collective-permute-start | bytes 3080 | tf_op jit(solution)/shard_map/ppermute | solution.py:314
  122.7 1.6 collective-permute-start.22
  125.0 3.2 %collective-permute-done.21 = f32[2,1,128]{2,1,0:T(1,128)S(1)} collective-permute-done((f32[2,1,128]{2,1,0:T(1,128)S(1)}, f32[2,1,128]{2,1,0:T(1,128)S(1)}, u32[]{:S(2)}, u32[]{:S(2)}) %collective-permute-start.21) | collective-permute-done | bytes 1056 | tf_op jit(solution)/shard_map/ppermute | solution.py:314
  128.2 0.2 collective-permute-done.22
  128.4 0.6 add_add_fusion.shares_ref
  128.9 7.1 %shard_map.77 = s16[16,656,128]{2,1,0:T(8,128)(2,1)} custom-call(f32[1]{0:T(128)S(6)} %copy.10.clip_ref, f32[2,1,128]{2,1,0:T(1,128)} %add_add_fusion.shares_ref, f32[2,512,2560]{2,1,0:T(8,128)} %get-tuple-element.26.wide_ref.thin_ref, f32[2,512,2560]{2,1,0:T(8,128)} %get-tuple-element.26.wide_ref.thin_ref, f32[16,2,8,128]{3,2,1,0:T(8,128)} %get-tuple-element.27.exponent_ref), custom_call_target="tpu_custom_call" | custom-call | flops 1 | bytes 1 | tf_op jit(solution)/shard_map/pallas_call | solution.py:219
  136.0 41.4 %all_to_all.10.clipped_ref = s16[16,656,128]{2,1,0:T(8,128)(2,1)} all-to-all(s16[16,656,128]{2,1,0:T(8,128)(2,1)} %shard_map.77), channel_id=1, replica_groups=mesh['dp'=16,'tensor'=16] {'dp'}, dimensions={0} | all-to-all | bytes 5373952 | tf_op jit(solution)/shard_map/all_to_all | solution.py:344
  177.4 5.2 %shard_map.78 = f32[256,512]{1,0:T(8,128)} custom-call(s16[16,2,384,128]{3,2,1,0:T(8,128)(2,1)} %copy-done, s16[16,656,128]{2,1,0:T(8,128)(2,1)} %all_to_all.10.clipped_ref, f32[256,512]{1,0:T(8,128)} %noise_ref.1), custom_call_target="tpu_custom_call" | custom-call | tf_op jit(solution)/shard_map/pallas_call | solution.py:289
  (52 shorter events, 0.2 us)
Async XLA Ops:
  6.5 18.4 %copy-start.14 = (s32[2]{0:T(128)S(1)}, s32[2]{0:T(128)}, u32[]{:S(2)}) copy-start(s32[2]{0:T(128)} %param.9) | copy-start | bytes 28
  6.5 94.1 %all-gather.3.cloned.1.call-start = ((), (), s32[]{:S(2)}) async-start(), calls=%async_computation.2 | async-start | bytes 11141120 | tf_op jit(solution)/shard_map/all_gather | solution.py:324
  8.8 11.1 %collective-permute-start = (bf16[2,64,1536]{2,1,0:T(8,128)(2,1)}, bf16[2,64,1536]{2,1,0:T(8,128)(2,1)S(1)}, u32[]{:S(2)}, u32[]{:S(2)}) collective-permute-start(bf16[2,64,1536]{2,1,0:T(8,128)(2,1)} %bitcast.10), channel_id=1, source_target_pairs={{0,2},{1,3},{2,4},{3,5},{4,6},{5,7},{6,8},{7,9},{8,10},{9,11},{10,... | collective-permute-start | bytes 1179656 | tf_op jit(solution)/shard_map/ppermute | solution.py:311
  10.7 11.0 %collective-permute-start.1 = (bf16[2,64,1536]{2,1,0:T(8,128)(2,1)}, bf16[2,64,1536]{2,1,0:T(8,128)(2,1)S(1)}, u32[]{:S(2)}, u32[]{:S(2)}) collective-permute-start(bf16[2,64,1536]{2,1,0:T(8,128)(2,1)} %bitcast.11), channel_id=1, source_target_pairs={{0,14},{1,15},{2,0},{3,1},{4,2},{5,3},{6,4},{7,5},{8,6},{9,7},{10,... | collective-permute-start | bytes 1179656 | tf_op jit(solution)/shard_map/ppermute | solution.py:311
  19.8 17.8 %copy-start.4 = (bf16[2,64,1536]{2,1,0:T(8,128)(2,1)}, bf16[2,64,1536]{2,1,0:T(8,128)(2,1)S(1)}, u32[]{:S(2)}) copy-start(bf16[2,64,1536]{2,1,0:T(8,128)(2,1)S(1)} %collective-permute-done.refs_2_) | copy-start | bytes 1179652
  21.7 16.4 %copy-start.5 = (bf16[2,64,1536]{2,1,0:T(8,128)(2,1)}, bf16[2,64,1536]{2,1,0:T(8,128)(2,1)S(1)}, u32[]{:S(2)}) copy-start(bf16[2,64,1536]{2,1,0:T(8,128)(2,1)S(1)} %collective-permute-done.1.refs_4_) | copy-start | bytes 1179652
  21.7 11.1 %collective-permute-start.2 = (bf16[2,64,1536]{2,1,0:T(8,128)(2,1)S(1)}, bf16[2,64,1536]{2,1,0:T(8,128)(2,1)}, u32[]{:S(2)}, u32[]{:S(2)}) collective-permute-start(bf16[2,64,1536]{2,1,0:T(8,128)(2,1)S(1)} %collective-permute-done.refs_2_), channel_id=1, source_target_pairs={{0,2},{1,3},{2,4},{3,5},{4,6},{5,7},{6,8},{7,9},{8,10},{9,11},{10,... | collective-permute-start | bytes 1179656 | tf_op jit(solution)/shard_map/ppermute | solution.py:311
  24.9 10.7 %collective-permute-start.3 = (bf16[2,64,1536]{2,1,0:T(8,128)(2,1)S(1)}, bf16[2,64,1536]{2,1,0:T(8,128)(2,1)}, u32[]{:S(2)}, u32[]{:S(2)}) collective-permute-start(bf16[2,64,1536]{2,1,0:T(8,128)(2,1)S(1)} %collective-permute-done.1.refs_4_), channel_id=1, source_target_pairs={{0,14},{1,15},{2,0},{3,1},{4,2},{5,3},{6,4},{7,5},{8,6},{9,7},{10,... | collective-permute-start | bytes 1179656 | tf_op jit(solution)/shard_map/ppermute | solution.py:311
  28.0 9.6 %copy-start.1 = (bf16[128,1536]{1,0:T(8,128)(2,1)S(1)}, bf16[128,1536]{1,0:T(8,128)(2,1)}, u32[]{:S(2)}) copy-start(bf16[128,1536]{1,0:T(8,128)(2,1)} %shard_map.73) | copy-start | bytes 1179652
  28.0 42.7 %copy-start.15 = (s32[16]{0:T(128)S(1)}, s32[16]{0:T(128)}, u32[]{:S(2)}) copy-start(s32[16]{0:T(128)} %constant.16.clone) | copy-start | bytes 196
  28.0 42.7 %copy-start.16 = (s32[16]{0:T(128)S(1)}, s32[16]{0:T(128)}, u32[]{:S(2)}) copy-start(s32[16]{0:T(128)} %constant.17.clone) | copy-start | bytes 196
  35.6 19.3 %collective-permute-start.9 = (bf16[2,64,1536]{2,1,0:T(8,128)(2,1)}, bf16[2,64,1536]{2,1,0:T(8,128)(2,1)S(1)}, u32[]{:S(2)}, u32[]{:S(2)}) collective-permute-start(bf16[2,64,1536]{2,1,0:T(8,128)(2,1)} %collective-permute-done.2.refs_6_), channel_id=1, source_target_pairs={{0,2},{1,3},{2,4},{3,5},{4,6},{5,7},{6,8},{7,9},{8,10},{9,11},{10,... | collective-permute-start | bytes 1179656 | tf_op jit(solution)/shard_map/ppermute | solution.py:311
  37.3 19.4 %collective-permute-start.11 = (bf16[2,64,1536]{2,1,0:T(8,128)(2,1)}, bf16[2,64,1536]{2,1,0:T(8,128)(2,1)S(1)}, u32[]{:S(2)}, u32[]{:S(2)}) collective-permute-start(bf16[2,64,1536]{2,1,0:T(8,128)(2,1)} %collective-permute-done.3.refs_8_), channel_id=1, source_target_pairs={{0,14},{1,15},{2,0},{3,1},{4,2},{5,3},{6,4},{7,5},{8,6},{9,7},{10,... | collective-permute-start | bytes 1179656 | tf_op jit(solution)/shard_map/ppermute | solution.py:311
  37.6 21.5 %collective-permute-start.4 = (bf16[2,64,1536]{2,1,0:T(8,128)(2,1)S(1)}, bf16[2,64,1536]{2,1,0:T(8,128)(2,1)S(1)}, u32[]{:S(2)}, u32[]{:S(2)}) collective-permute-start(bf16[2,64,1536]{2,1,0:T(8,128)(2,1)S(1)} %bitcast.13), channel_id=1, source_target_pairs={{0,1},{1,0},{2,3},{3,2},{4,5},{5,4},{6,7},{7,6},{8,9},{9,8},{10,11... | collective-permute-start | bytes 1179656 | tf_op jit(solution)/shard_map/ppermute | solution.py:314
  37.6 21.8 %collective-permute-start.5 = (bf16[2,64,1536]{2,1,0:T(8,128)(2,1)S(1)}, bf16[2,64,1536]{2,1,0:T(8,128)(2,1)S(1)}, u32[]{:S(2)}, u32[]{:S(2)}) collective-permute-start(bf16[2,64,1536]{2,1,0:T(8,128)(2,1)S(1)} %collective-permute-done.refs_2_), channel_id=1, source_target_pairs={{0,1},{1,0},{2,3},{3,2},{4,5},{5,4},{6,7},{7,6},{8,9},{9,8},{10,11... | collective-permute-start | bytes 1179656 | tf_op jit(solution)/shard_map/ppermute | solution.py:314
  38.1 21.3 %collective-permute-start.6 = (bf16[2,64,1536]{2,1,0:T(8,128)(2,1)S(1)}, bf16[2,64,1536]{2,1,0:T(8,128)(2,1)S(1)}, u32[]{:S(2)}, u32[]{:S(2)}) collective-permute-start(bf16[2,64,1536]{2,1,0:T(8,128)(2,1)S(1)} %collective-permute-done.1.refs_4_), channel_id=1, source_target_pairs={{0,1},{1,0},{2,3},{3,2},{4,5},{5,4},{6,7},{7,6},{8,9},{9,8},{10,11... | collective-permute-start | bytes 1179656 | tf_op jit(solution)/shard_map/ppermute | solution.py:314
  54.9 17.4 %copy-start.2 = (bf16[2,64,1536]{2,1,0:T(8,128)(2,1)}, bf16[2,64,1536]{2,1,0:T(8,128)(2,1)S(1)}, u32[]{:S(2)}) copy-start(bf16[2,64,1536]{2,1,0:T(8,128)(2,1)S(1)} %collective-permute-done.9.refs_10_) | copy-start | bytes 1179652
  54.9 5.0 %collective-permute-start.7 = (bf16[2,64,1536]{2,1,0:T(8,128)(2,1)}, bf16[2,64,1536]{2,1,0:T(8,128)(2,1)}, u32[]{:S(2)}, u32[]{:S(2)}) collective-permute-start(bf16[2,64,1536]{2,1,0:T(8,128)(2,1)} %collective-permute-done.2.refs_6_), channel_id=1, source_target_pairs={{0,1},{1,0},{2,3},{3,2},{4,5},{5,4},{6,7},{7,6},{8,9},{9,8},{10,11... | collective-permute-start | bytes 1179656 | tf_op jit(solution)/shard_map/ppermute | solution.py:314
  56.7 15.6 %copy-start.3 = (bf16[2,64,1536]{2,1,0:T(8,128)(2,1)}, bf16[2,64,1536]{2,1,0:T(8,128)(2,1)S(1)}, u32[]{:S(2)}) copy-start(bf16[2,64,1536]{2,1,0:T(8,128)(2,1)S(1)} %collective-permute-done.11.refs_12_) | copy-start | bytes 1179652
  56.7 11.3 %collective-permute-start.13 = (bf16[1,64,1536]{2,1,0:T(8,128)(2,1)S(1)}, bf16[1,64,1536]{2,1,0:T(8,128)(2,1)}, u32[]{:S(2)}, u32[]{:S(2)}) collective-permute-start(bf16[1,64,1536]{2,1,0:T(8,128)(2,1)S(1)} %slice.8), channel_id=1, source_target_pairs={{0,2},{1,3},{2,4},{3,5},{4,6},{5,7},{6,8},{7,9},{8,10},{9,11},{10,... | collective-permute-start | bytes 589832 | tf_op jit(solution)/shard_map/ppermute | solution.py:311
  59.1 13.2 %copy-start.6 = (bf16[2,64,1536]{2,1,0:T(8,128)(2,1)}, bf16[2,64,1536]{2,1,0:T(8,128)(2,1)S(1)}, u32[]{:S(2)}) copy-start(bf16[2,64,1536]{2,1,0:T(8,128)(2,1)S(1)} %collective-permute-done.4.refs_1_) | copy-start | bytes 1179652
  59.1 11.5 %collective-permute-start.15 = (bf16[1,64,1536]{2,1,0:T(8,128)(2,1)}, bf16[1,64,1536]{2,1,0:T(8,128)(2,1)}, u32[]{:S(2)}, u32[]{:S(2)}) collective-permute-start(bf16[1,64,1536]{2,1,0:T(8,128)(2,1)} %slice.9), channel_id=1, source_target_pairs={{0,14},{1,15},{2,0},{3,1},{4,2},{5,3},{6,4},{7,5},{8,6},{9,7},{10,... | collective-permute-start | bytes 589832 | tf_op jit(solution)/shard_map/ppermute | solution.py:311
  59.4 12.9 %copy-start.7 = (bf16[2,64,1536]{2,1,0:T(8,128)(2,1)}, bf16[2,64,1536]{2,1,0:T(8,128)(2,1)S(1)}, u32[]{:S(2)}) copy-start(bf16[2,64,1536]{2,1,0:T(8,128)(2,1)S(1)} %collective-permute-done.5.refs_3_) | copy-start | bytes 1179652
  59.4 11.8 %collective-permute-start.8 = (bf16[2,64,1536]{2,1,0:T(8,128)(2,1)}, bf16[2,64,1536]{2,1,0:T(8,128)(2,1)S(1)}, u32[]{:S(2)}, u32[]{:S(2)}) collective-permute-start(bf16[2,64,1536]{2,1,0:T(8,128)(2,1)} %collective-permute-done.3.refs_8_), channel_id=1, source_target_pairs={{0,1},{1,0},{2,3},{3,2},{4,5},{5,4},{6,7},{7,6},{8,9},{9,8},{10,11... | collective-permute-start | bytes 1179656 | tf_op jit(solution)/shard_map/ppermute | solution.py:314
  59.4 12.9 %copy-start.8 = (bf16[2,64,1536]{2,1,0:T(8,128)(2,1)}, bf16[2,64,1536]{2,1,0:T(8,128)(2,1)S(1)}, u32[]{:S(2)}) copy-start(bf16[2,64,1536]{2,1,0:T(8,128)(2,1)S(1)} %collective-permute-done.6.refs_5_) | copy-start | bytes 1179652
  59.5 12.9 %collective-permute-start.10 = (bf16[2,64,1536]{2,1,0:T(8,128)(2,1)S(1)}, bf16[2,64,1536]{2,1,0:T(8,128)(2,1)S(1)}, u32[]{:S(2)}, u32[]{:S(2)}) collective-permute-start(bf16[2,64,1536]{2,1,0:T(8,128)(2,1)S(1)} %collective-permute-done.9.refs_10_), channel_id=1, source_target_pairs={{0,1},{1,0},{2,3},{3,2},{4,5},{5,4},{6,7},{7,6},{8,9},{9,8},{10,11... | collective-permute-start | bytes 1179656 | tf_op jit(solution)/shard_map/ppermute | solution.py:314
  59.9 12.4 %collective-permute-start.12 = (bf16[2,64,1536]{2,1,0:T(8,128)(2,1)S(1)}, bf16[2,64,1536]{2,1,0:T(8,128)(2,1)S(1)}, u32[]{:S(2)}, u32[]{:S(2)}) collective-permute-start(bf16[2,64,1536]{2,1,0:T(8,128)(2,1)S(1)} %collective-permute-done.11.refs_12_), channel_id=1, source_target_pairs={{0,1},{1,0},{2,3},{3,2},{4,5},{5,4},{6,7},{7,6},{8,9},{9,8},{10,11... | collective-permute-start | bytes 1179656 | tf_op jit(solution)/shard_map/ppermute | solution.py:314
  68.0 3.1 %collective-permute-start.14 = (bf16[1,64,1536]{2,1,0:T(8,128)(2,1)}, bf16[1,64,1536]{2,1,0:T(8,128)(2,1)S(1)}, u32[]{:S(2)}, u32[]{:S(2)}) collective-permute-start(bf16[1,64,1536]{2,1,0:T(8,128)(2,1)} %collective-permute-done.13.refs_14_), channel_id=1, source_target_pairs={{0,1},{1,0},{2,3},{3,2},{4,5},{5,4},{6,7},{7,6},{8,9},{9,8},{10,11... | collective-permute-start | bytes 589832 | tf_op jit(solution)/shard_map/ppermute | solution.py:314
  70.7 1.7 collective-permute-start.16
  71.2 1.2 copy-start.9
  71.2 1.2 copy-start.12
  72.3 0.7 copy-start.13
  72.3 0.8 copy-start.10
  73.1 0.8 copy-start.11
  83.9 52.1 %all-to-all-start = ((s16[16,2,384,128]{3,2,1,0:T(8,128)(2,1)}), s16[16,2,384,128]{3,2,1,0:T(8,128)(2,1)S(1)}, u32[]{:S(2)}, u32[]{:S(2)}) async-start(s16[16,2,384,128]{3,2,1,0:T(8,128)(2,1)} %get-tuple-element.28), calls=%async_computation | async-start | bytes 6291456 | tf_op jit(solution)/shard_map/all_to_all | solution.py:338
  112.6 1.9 collective-permute-start.17
  112.9 3.8 %collective-permute-start.18 = (f32[2,1,128]{2,1,0:T(1,128)}, f32[2,1,128]{2,1,0:T(1,128)S(1)}, u32[]{:S(2)}, u32[]{:S(2)}) collective-permute-start(f32[2,1,128]{2,1,0:T(1,128)} %get-tuple-element.25), channel_id=1, source_target_pairs={{0,2},{1,3},{2,0},{3,1},{4,6},{5,7},{6,4},{7,5},{8,10},{9,11},{10,... | collective-permute-start | bytes 3080 | tf_op jit(solution)/shard_map/ppermute | solution.py:314
  113.9 3.2 %collective-permute-start.19 = (f32[2,1,128]{2,1,0:T(1,128)}, f32[2,1,128]{2,1,0:T(1,128)S(1)}, u32[]{:S(2)}, u32[]{:S(2)}) collective-permute-start(f32[2,1,128]{2,1,0:T(1,128)} %get-tuple-element.25), channel_id=1, source_target_pairs={{0,3},{1,2},{2,1},{3,0},{4,7},{5,6},{6,5},{7,4},{8,11},{9,10},{10,... | collective-permute-start | bytes 3080 | tf_op jit(solution)/shard_map/ppermute | solution.py:314
  117.8 7.2 %collective-permute-start.20 = (f32[2,1,128]{2,1,0:T(1,128)S(1)}, f32[2,1,128]{2,1,0:T(1,128)S(1)}, u32[]{:S(2)}, u32[]{:S(2)}) collective-permute-start(f32[2,1,128]{2,1,0:T(1,128)S(1)} %add_add_fusion.1), channel_id=1, source_target_pairs={{0,4},{1,5},{2,6},{3,7},{4,0},{5,1},{6,2},{7,3},{8,12},{9,13},{10,... | collective-permute-start | bytes 3080 | tf_op jit(solution)/shard_map/ppermute | solution.py:314
  120.7 7.5 %collective-permute-start.21 = (f32[2,1,128]{2,1,0:T(1,128)S(1)}, f32[2,1,128]{2,1,0:T(1,128)S(1)}, u32[]{:S(2)}, u32[]{:S(2)}) collective-permute-start(f32[2,1,128]{2,1,0:T(1,128)S(1)} %add_add_fusion.1), channel_id=1, source_target_pairs={{0,8},{1,9},{2,10},{3,11},{4,12},{5,13},{6,14},{7,15},{8,0},{9,1},... | collective-permute-start | bytes 3080 | tf_op jit(solution)/shard_map/ppermute | solution.py:314
  122.7 5.7 %collective-permute-start.22 = (f32[2,1,128]{2,1,0:T(1,128)S(1)}, f32[2,1,128]{2,1,0:T(1,128)S(1)}, u32[]{:S(2)}, u32[]{:S(2)}) collective-permute-start(f32[2,1,128]{2,1,0:T(1,128)S(1)} %add_add_fusion.1), channel_id=1, source_target_pairs={{0,12},{1,13},{2,14},{3,15},{4,8},{5,9},{6,10},{7,11},{8,4},{9,5},... | collective-permute-start | bytes 3080 | tf_op jit(solution)/shard_map/ppermute | solution.py:314
  136.0 41.4 %copy-start = (s16[16,2,384,128]{3,2,1,0:T(8,128)(2,1)}, s16[16,2,384,128]{3,2,1,0:T(8,128)(2,1)S(1)}, u32[]{:S(2)}) copy-start(s16[16,2,384,128]{3,2,1,0:T(8,128)(2,1)S(1)} %all-to-all-done.raw_ref) | copy-start | bytes 9437188
Sparse Core Ops, SparseCore 0:
  21.8 78.8 all-gather.2

commit v2 on v1

--- a/solution.py
+++ b/solution.py
@@ -9,9 +9,10 @@
 
 LANES = 128
 EXTRA = 16
-TOGETHER = 4
+TOGETHER = 2
 LEAST = 1e-33
 PARAMS = pltpu.CompilerParams(vmem_limit_bytes=56 * 1024 * 1024)
+LESS = pltpu.CompilerParams(vmem_limit_bytes=28 * 1024 * 1024)
 RAW = ((0, 64), (64, 32))
 CLIPPED = ((128, 128), (96, 32))
 OWNED = sum(width for _, width in RAW + CLIPPED)
@@ -39,9 +40,12 @@
     )(acts.reshape(examples * shard, features)).reshape(examples, shard, taken)
 
 
-def coded(values):
-    top = jnp.maximum(jnp.max(jnp.abs(values), axis=0, keepdims=True), LEAST)
-    exponent = jnp.ceil(jnp.log2(top) - 14.99)
+def tops(values):
+    return jnp.max(jnp.abs(values), axis=0, keepdims=True)
+
+
+def coded(values, top):
+    exponent = jnp.ceil(jnp.log2(jnp.maximum(top, LEAST)) - 14.99)
     return jnp.round(values * jnp.exp2(-exponent)), exponent
 
 
@@ -108,7 +112,8 @@
         together = LANES // width
         rows = product.shape[0] // together
         for tile in range(coded_ref.shape[0] // together):
-            units, exponent = coded(product[:, at : at + LANES])
+            tile_values = product[:, at : at + LANES]
+            units, exponent = coded(tile_values, tops(tile_values))
             exponents = packed_row(exponent, together)
             for k, block in enumerate(packed(units, together)):
                 coded_ref[tile * together + k, 0, row : row + rows] = narrow(block)
@@ -146,13 +151,40 @@
     )(order, *pieces, grads)
 
 
-def plain_kernel(acts_ref, grads_ref, squares_ref, product_ref, share_ref):
-    devices, _, shard, width = acts_ref.shape
-    acts = acts_ref[...].reshape(devices * shard, width)
-    product = jnp.dot(grads_ref[0], acts, preferred_element_type=jnp.float32)
-    product_ref[0] = product
-
-    @pl.when(pl.program_id(1) == 0)
+def plain_kernel(acts_ref, grads_ref, squares_ref, product_ref, top_ref, share_ref, acts, grads, acts_sems, grads_sems):
+    devices, examples, shard, _ = acts_ref.shape
+    width = product_ref.shape[2]
+    tiles = acts_ref.shape[3] // width
+    example, tile = pl.program_id(0), pl.program_id(1)
+
+    def acts_copy(step):
+        here = pl.ds(step % tiles * width, width)
+        source = acts_ref.at[:, step // tiles, :, here]
+        return pltpu.make_async_copy(source, acts.at[step % 2], acts_sems.at[step % 2])
+
+    def grads_copy(e):
+        return pltpu.make_async_copy(grads_ref.at[e], grads.at[e], grads_sems.at[e])
+
+    for step in range(examples * tiles):
+
+        @pl.when(example * tiles + tile == step)
+        def _():
+            if step == 0:
+                acts_copy(0).start()
+                for e in range(examples):
+                    grads_copy(e).start()
+            if step + 1 < examples * tiles:
+                acts_copy(step + 1).start()
+            acts_copy(step).wait()
+            if step % tiles == 0:
+                grads_copy(step // tiles).wait()
+            rows = acts[step % 2].reshape(devices * shard, width)
+            product_ref[0] = jnp.dot(grads[step // tiles], rows, preferred_element_type=jnp.float32)
+
+    product = product_ref[0]
+    top_ref[0] = tops(product)
+
+    @pl.when(tile == 0)
     def _():
         share_ref[...] = squares_ref[...]
 
@@ -161,38 +193,48 @@
 
 def plain_products(acts, grads, squares):
     devices, examples, shard, features = acts.shape
-    _, columns, positions = grads.shape
+    _, columns, _ = grads.shape
     width = features // 2
     row = pl.BlockSpec((1, 1, LANES), lambda e, i: (e, 0, 0))
+    hbm = pl.BlockSpec(memory_space=pltpu.HBM)
     return pl.pallas_call(
         plain_kernel,
         grid=(examples, features // width),
-        in_specs=[
-            pl.BlockSpec((devices, 1, shard, width), lambda e, i: (0, e, 0, i)),
-            pl.BlockSpec((1, columns, positions), lambda e, i: (e, 0, 0)),
+        in_specs=[hbm, hbm, row],
+        out_specs=[
+            pl.BlockSpec((1, columns, width), lambda e, i: (e, 0, i)),
+            pl.BlockSpec((1, 1, width), lambda e, i: (e, 0, i)),
             row,
         ],
-        out_specs=[pl.BlockSpec((1, columns, width), lambda e, i: (e, 0, i)), row],
         out_shape=[
             jax.ShapeDtypeStruct((examples, columns, features), jnp.float32),
+            jax.ShapeDtypeStruct((examples, 1, features), jnp.float32),
             jax.ShapeDtypeStruct((examples, 1, LANES), jnp.float32),
         ],
+        scratch_shapes=[
+            pltpu.VMEM((2, devices, shard, width), acts.dtype),
+            pltpu.VMEM(grads.shape, grads.dtype),
+            pltpu.SemaphoreType.DMA((2,)),
+            pltpu.SemaphoreType.DMA((examples,)),
+        ],
         cost_estimate=SMALL,
-        compiler_params=PARAMS,
-    )(acts, grads, squares)
-
-
-def clipped_kernel(clip_ref, shares_ref, wide_ref, thin_ref, exponent_ref, coded_ref):
+        compiler_params=LESS,
+    )(*(pltpu.with_memory_space_constraint(a, pltpu.HBM) for a in (acts, grads, squares)))
+
+
+def clipped_kernel(clip_ref, shares_ref, wide_ref, thin_ref, wide_top_ref, thin_top_ref, exponent_ref, coded_ref):
     examples, columns, _ = wide_ref.shape
     owners = coded_ref.shape[0]
     clip = clip_ref[0]
     blank = jnp.zeros((1, LANES), jnp.float32)
-    wide, thin, extra = 0.0, 0.0, [[] for _ in range(owners)]
+    wide, thin, wide_top, thin_top, extra = 0.0, 0.0, 0.0, 0.0, [[] for _ in range(owners)]
     for e in range(examples):
         square = jnp.sum(shares_ref[e], axis=1, keepdims=True)
         factor = clip / jnp.maximum(jnp.sqrt(square), clip)
         wide = wide + factor * wide_ref[e]
         thin = thin + factor * thin_ref[e]
+        wide_top = wide_top + factor * wide_top_ref[e]
+        thin_top = thin_top + factor * thin_top_ref[e]
         power = jnp.floor(jnp.log2(jnp.maximum(factor, LEAST))) + 1.0
         scaled = factor * jnp.exp2(-power) * 16384.0
         high = jnp.floor(scaled)
@@ -200,10 +242,11 @@
         for k in range(owners):
             extra[k] += [blank + high, blank + low]
             extra[k] += [exponent_ref[k, e, h : h + 1] + power for h in range(len(RAW))]
-    thin_units, exponent = coded(thin)
+    thin_units, exponent = coded(thin, thin_top)
     thin_units, thin_exponents = packed(thin_units, owners), packed_row(exponent, owners)
     for k in range(owners):
-        units, exponent = coded(wide[:, k * LANES : (k + 1) * LANES])
+        here = slice(k * LANES, (k + 1) * LANES)
+        units, exponent = coded(wide[:, here], wide_top[:, here])
         rows = extra[k] + [exponent, thin_exponents[k]]
         rows = jnp.concatenate(rows + [blank] * (EXTRA - len(rows)), axis=0)
         coded_ref[k, :columns] = narrow(units)
@@ -211,7 +254,7 @@
         coded_ref[k, coded_ref.shape[1] - EXTRA :] = narrow(rows)
 
 
-def clipped_sums(clip_bound, shares, products, exponents):
+def clipped_sums(clip_bound, shares, products, top, exponents):
     examples, columns, features = products.shape
     owners = exponents.shape[0]
     together = LANES // CLIPPED[1][1]
@@ -224,13 +267,15 @@
             pl.BlockSpec(shares.shape, lambda i: (0, 0, 0)),
             pl.BlockSpec((examples, columns, together * LANES), lambda i: (0, 0, i)),
             pl.BlockSpec((examples, columns, LANES), lambda i: (0, 0, owners + i)),
+            pl.BlockSpec((examples, 1, together * LANES), lambda i: (0, 0, i)),
+            pl.BlockSpec((examples, 1, LANES), lambda i: (0, 0, owners + i)),
             pl.BlockSpec((together, examples, 8, LANES), lambda i: (i, 0, 0, 0)),
         ],
         out_specs=pl.BlockSpec((together, rows, LANES), lambda i: (i, 0, 0)),
         out_shape=jax.ShapeDtypeStruct((owners, rows, LANES), jnp.int16),
         cost_estimate=SMALL,
-        compiler_params=PARAMS,
-    )(clip_bound, shares, products, products, exponents)
+        compiler_params=LESS,
+    )(clip_bound, shares, products, products, top, top, exponents)
 
 
 def finish_kernel(scale, raw_ref, clipped_ref, noise_ref, out_ref, raw_sum, clipped_sum):
@@ -336,10 +381,10 @@
 
     raw, exponents, squares = raw_products(order, pieces, masked)
     raw = lax.all_to_all(raw, "dp", 0, 0)
-    products, share = plain_products(second, masked, squares)
+    products, top, share = plain_products(second, masked, squares)
     share = share + crossed(share, 1) + crossed(share, 2) + crossed(share, 3)
     share = share + crossed(share, 4) + crossed(share, 8) + crossed(share, 12)
-    clipped = clipped_sums(clip_bound, share, products, exponents)
+    clipped = clipped_sums(clip_bound, share, products, top, exponents)
     clipped, raw = lax.optimization_barrier((clipped, raw))
     clipped = lax.all_to_all(clipped, "dp", 0, 0)
     return finish(raw, clipped, noise, float((examples * owners) ** -0.5))

time: 190 us -> 191 us (level)
  waiting for transfers between devices: 60.6 us -> 63.5 us
  Pallas kernels: 38.7 us -> 35.9 us
  blocking collectives: 41.4 us -> 43.7 us
    pallas_call x1, Pallas kernels: 7.08 us -> 3.24 us  [clipped_sums(): pl.pallas_call(clipped_kernel, grid=(owners // together,), in_specs=[pl.B...]
    all_to_all x1, waiting for transfers between devices: 0.01 us -> 3.29 us  [per_device(): raw = lax.all_to_all(raw, 'dp', 0, 0)]
    all_to_all x1, blocking collectives: 41.4 us -> 43.7 us  [per_device(): clipped = lax.all_to_all(clipped, 'dp', 0, 0)]
  transfers between devices with their start and end apart: 25 -> 25, of which waited for: 14 -> 15; matrix products, arithmetic and copies ran while one was open for 4% -> 3% of each run, Pallas kernels for 17% -> 14%
where the time goes in v2:
time: 191 us
  waiting for transfers between devices  63.5 us (33%)
  blocking collectives  43.7 us (23%)
  Pallas kernels  35.9 us (19%)
  starting transfers between devices  26.2 us (14%)
  between operations  14.2 us (7%)
  local copies, waits for them, and re-layouts  5.25 us (3%)
  other arithmetic  2.12 us (1%)
    ppermute x8, waiting for transfers between devices, along_z(): lax.ppermute(x, 'tensor', [(t, (t + 2 * k) % devices) for t in range(devi...  43.7 us
    all_to_all x1, blocking collectives, per_device(): clipped = lax.all_to_all(clipped, 'dp', 0, 0)  43.7 us
    pallas_call x1, Pallas kernels, plain_products(): pl.pallas_call(plain_kernel, grid=(examples, features // width), in_specs...  11.4 us
    pallas_call x1, Pallas kernels, raw_products(): pl.pallas_call(raw_kernel, grid=(examples,), in_specs=[pl.BlockSpec(memor...  10 us
    ppermute x15, starting transfers between devices, crossed(): return lax.ppermute(x, 'tensor', [(t, t ^ k) for t in range(devices)])  9.84 us
    all_gather x1, waiting for transfers between devices, per_device(): second = lax.all_gather(second, 'tensor')  9.65 us
    ppermute x8, starting transfers between devices, along_z(): lax.ppermute(x, 'tensor', [(t, (t + 2 * k) % devices) for t in range(devi...  9.29 us
    all_to_all x1, starting transfers between devices, per_device(): raw = lax.all_to_all(raw, 'dp', 0, 0)  7.1 us
  transfers between devices with their start and end apart: 25, of which 15 were waited for; matrix products, arithmetic and copies ran while one was open for 3% of the time, Pallas kernels for 14%

profile of v2, /device:TPU:32, one launch (start us, length us, event | category | flops | bytes accessed | tf_op | source)
XLA Modules:
  0.0 190.9 jit_solution(17470827470537130864)
XLA Ops:
  6.5 2.2 %shard_map.73 = bf16[128,1536]{1,0:T(8,128)(2,1)} custom-call(bf16[128,4096]{1,0:T(8,128)(2,1)} %bitcast.7), custom_call_target="tpu_custom_call" | custom-call | tf_op jit(solution)/shard_map/pallas_call | solution.py:36
  8.8 1.9 %collective-permute-start = (bf16[2,64,1536]{2,1,0:T(8,128)(2,1)}, bf16[2,64,1536]{2,1,0:T(8,128)(2,1)S(1)}, u32[]{:S(2)}, u32[]{:S(2)}) collective-permute-start(bf16[2,64,1536]{2,1,0:T(8,128)(2,1)} %bitcast.10), channel_id=1, source_target_pairs={{0,2},{1,3},{2,4},{3,5},{4,6},{5,7},{6,8},{7,9},{8,10},{9,11},{10,... | collective-permute-start | bytes 1179656 | tf_op jit(solution)/shard_map/ppermute | solution.py:356
  10.7 0.1 collective-permute-start.1
  10.8 2.3 %shard_map.74 = bf16[128,2560]{1,0:T(8,128)(2,1)} custom-call(bf16[128,4096]{1,0:T(8,128)(2,1)} %bitcast.8), custom_call_target="tpu_custom_call" | custom-call | tf_op jit(solution)/shard_map/pallas_call | solution.py:36
  13.1 6.8 %collective-permute-done.refs_2_ = bf16[2,64,1536]{2,1,0:T(8,128)(2,1)S(1)} collective-permute-done((bf16[2,64,1536]{2,1,0:T(8,128)(2,1)}, bf16[2,64,1536]{2,1,0:T(8,128)(2,1)S(1)}, u32[]{:S(2)}, u32[]{:S(2)}) %collective-permute-start) | collective-permute-done | bytes 393248 | tf_op jit(solution)/shard_map/ppermute | solution.py:356
  19.8 1.8 collective-permute-done.1.refs_4_
  21.7 3.2 %collective-permute-start.2 = (bf16[2,64,1536]{2,1,0:T(8,128)(2,1)S(1)}, bf16[2,64,1536]{2,1,0:T(8,128)(2,1)}, u32[]{:S(2)}, u32[]{:S(2)}) collective-permute-start(bf16[2,64,1536]{2,1,0:T(8,128)(2,1)S(1)} %collective-permute-done.refs_2_), channel_id=1, source_target_pairs={{0,2},{1,3},{2,4},{3,5},{4,6},{5,7},{6,8},{7,9},{8,10},{9,11},{10,... | collective-permute-start | bytes 1179656 | tf_op jit(solution)/shard_map/ppermute | solution.py:356
  24.9 0.1 iota_compare_fusion
  25.0 3.0 %copy.9 = bf16[2,1024,512]{1,2,0:T(8,128)(2,1)S(1)} copy(bf16[2,1024,512]{2,1,0:T(8,128)(2,1)} %param.8) | data formatting | bytes 4194304 | tf_op args[1]
  28.0 1.5 select_bitcast_fusion.refs_18_.grads_ref
  29.5 3.3 %collective-permute-done.2.refs_6_ = bf16[2,64,1536]{2,1,0:T(8,128)(2,1)} collective-permute-done((bf16[2,64,1536]{2,1,0:T(8,128)(2,1)S(1)}, bf16[2,64,1536]{2,1,0:T(8,128)(2,1)}, u32[]{:S(2)}, u32[]{:S(2)}) %collective-permute-start.2) | collective-permute-done | bytes 393248 | tf_op jit(solution)/shard_map/ppermute | solution.py:356
  32.8 2.7 %collective-permute-done.3.refs_8_ = bf16[2,64,1536]{2,1,0:T(8,128)(2,1)} collective-permute-done((bf16[2,64,1536]{2,1,0:T(8,128)(2,1)S(1)}, bf16[2,64,1536]{2,1,0:T(8,128)(2,1)}, u32[]{:S(2)}, u32[]{:S(2)}) %collective-permute-start.3) | collective-permute-done | bytes 393248 | tf_op jit(solution)/shard_map/ppermute | solution.py:356
  35.6 1.7 collective-permute-start.9
  37.3 0.3 collective-permute-start.11
  37.6 0.5 collective-permute-start.5
  38.1 0.1 collective-permute-start.6
  38.2 16.7 %collective-permute-done.9.refs_10_ = bf16[2,64,1536]{2,1,0:T(8,128)(2,1)S(1)} collective-permute-done((bf16[2,64,1536]{2,1,0:T(8,128)(2,1)}, bf16[2,64,1536]{2,1,0:T(8,128)(2,1)S(1)}, u32[]{:S(2)}, u32[]{:S(2)}) %collective-permute-start.9) | collective-permute-done | bytes 393248 | tf_op jit(solution)/shard_map/ppermute | solution.py:356
  54.9 1.8 collective-permute-done.11.refs_12_
  56.7 1.7 collective-permute-start.13
  58.4 0.7 slice.9
  59.1 0.3 collective-permute-start.15
  59.4 0.5 collective-permute-start.10
  59.9 0.1 collective-permute-start.12
  60.0 8.0 %collective-permute-done.13.refs_14_ = bf16[1,64,1536]{2,1,0:T(8,128)(2,1)} collective-permute-done((bf16[1,64,1536]{2,1,0:T(8,128)(2,1)S(1)}, bf16[1,64,1536]{2,1,0:T(8,128)(2,1)}, u32[]{:S(2)}, u32[]{:S(2)}) %collective-permute-start.13) | collective-permute-done | bytes 196640 | tf_op jit(solution)/shard_map/ppermute | solution.py:356
  68.0 2.6 %collective-permute-done.15.refs_16_ = bf16[1,64,1536]{2,1,0:T(8,128)(2,1)} collective-permute-done((bf16[1,64,1536]{2,1,0:T(8,128)(2,1)}, bf16[1,64,1536]{2,1,0:T(8,128)(2,1)}, u32[]{:S(2)}, u32[]{:S(2)}) %collective-permute-start.15) | collective-permute-done | bytes 196640 | tf_op jit(solution)/shard_map/ppermute | solution.py:356
  70.7 0.5 add_and_fusion.order_ref
  71.2 1.1 collective-permute-done.16.refs_17_
  72.4 0.6 copy-done.13
  73.0 0.2 copy-done.10
  73.1 0.7 copy-done.11
  73.9 10.0 %shard_map.75 = (s16[16,2,384,128]{3,2,1,0:T(8,128)(2,1)}, f32[16,2,8,128]{3,2,1,0:T(8,128)}, f32[2,1,128]{2,1,0:T(1,128)}) custom-call(s32[16]{0:T(128)} %add_and_fusion.order_ref, bf16[2,64,1536]{2,1,0:T(8,128)(2,1)} %bitcast.12, bf16[2,64,1536]{2,1,0:T(8,128)(2,1)} %copy-done.6, bf16[2,64,1536]{2,1,0:T(8,128)(2,1)} %copy-done.4, ...), custom_call_target="tpu_custom_call" | custom-call | tf_op jit(solution)/shard_map/pallas_call | solution.py:130
  83.9 7.1 %all-to-all-start = ((s16[16,2,384,128]{3,2,1,0:T(8,128)(2,1)}), s16[16,2,384,128]{3,2,1,0:T(8,128)(2,1)}, u32[]{:S(2)}, u32[]{:S(2)}) async-start(s16[16,2,384,128]{3,2,1,0:T(8,128)(2,1)} %get-tuple-element.30), calls=%async_computation | async-start | bytes 6291456 | tf_op jit(solution)/shard_map/all_to_all | solution.py:383
  91.0 9.7 %all-gather.3.cloned.1.call-done = bf16[32,64,2560]{2,1,0:T(8,128)(2,1)} async-done(((bf16[2,64,2560]{2,1,0:T(8,128)(2,1)}), bf16[32,64,2560]{2,1,0:T(8,128)(2,1)}) %all-gather.3.cloned.1.call-update) | async-done | bytes 10485776 | tf_op jit(solution)/shard_map/all_gather | solution.py:369
  100.7 11.4 %shard_map.76 = (f32[2,512,2560]{2,1,0:T(8,128)S(1)}, f32[2,1,2560]{2,1,0:T(1,128)S(1)}, f32[2,1,128]{2,1,0:T(1,128)S(1)}) custom-call(bf16[16,2,64,2560]{3,2,1,0:T(8,128)(2,1)} %bitcast.6, bf16[2,512,1024]{2,1,0:T(8,128)(2,1)} %select_bitcast_fusion.refs_18_.grads_ref, f32[2,1,128]{2,1,0:T(1,128)} %get-tuple-element.25.squares_ref), custom_call_target="tpu_custom_call" | custom-call | flops 1 | bytes 1 | tf_op jit(solution)/shard_map/pallas_call | solution.py:200
  112.1 0.3 collective-permute-start.17
  112.4 1.0 collective-permute-start.18
  113.4 0.6 collective-permute-start.19
  114.0 1.9 %collective-permute-done.18 = f32[2,1,128]{2,1,0:T(1,128)S(1)} collective-permute-done((f32[2,1,128]{2,1,0:T(1,128)S(1)}, f32[2,1,128]{2,1,0:T(1,128)S(1)}, u32[]{:S(2)}, u32[]{:S(2)}) %collective-permute-start.18) | collective-permute-done | bytes 1056 | tf_op jit(solution)/shard_map/ppermute | solution.py:359
  116.0 0.5 collective-permute-done.19
  116.4 3.0 %collective-permute-start.20 = (f32[2,1,128]{2,1,0:T(1,128)S(1)}, f32[2,1,128]{2,1,0:T(1,128)S(1)}, u32[]{:S(2)}, u32[]{:S(2)}) collective-permute-start(f32[2,1,128]{2,1,0:T(1,128)S(1)} %add_add_fusion.1), channel_id=1, source_target_pairs={{0,4},{1,5},{2,6},{3,7},{4,0},{5,1},{6,2},{7,3},{8,12},{9,13},{10,... | collective-permute-start | bytes 3080 | tf_op jit(solution)/shard_map/ppermute | solution.py:359
  119.5 1.9 collective-permute-start.21
  121.4 1.8 collective-permute-start.22
  123.8 3.1 %collective-permute-done.21 = f32[2,1,128]{2,1,0:T(1,128)S(1)} collective-permute-done((f32[2,1,128]{2,1,0:T(1,128)S(1)}, f32[2,1,128]{2,1,0:T(1,128)S(1)}, u32[]{:S(2)}, u32[]{:S(2)}) %collective-permute-start.21) | collective-permute-done | bytes 1056 | tf_op jit(solution)/shard_map/ppermute | solution.py:359
  126.9 0.1 collective-permute-done.22
  127.1 3.2 %shard_map.77 = s16[16,656,128]{2,1,0:T(8,128)(2,1)S(1)} custom-call(f32[1]{0:T(128)S(6)} %copy.10.clip_ref, f32[2,1,128]{2,1,0:T(1,128)S(1)} %add_add_fusion.shares_ref, f32[2,512,2560]{2,1,0:T(8,128)S(1)} %get-tuple-element.27.wide_ref.thin_ref, f32[2,512,2560]{2,1,0:T(8,128)S(1)} %get-tuple-element.27.wide_ref.thin_ref, ...), custom_call_target="tpu_custom_call" | custom-call | flops 1 | bytes 1 | tf_op jit(solution)/shard_map/pallas_call | solution.py:262
  130.3 3.3 %all-to-all-done.raw_ref = s16[16,2,384,128]{3,2,1,0:T(8,128)(2,1)} async-done(((s16[16,2,384,128]{3,2,1,0:T(8,128)(2,1)}), s16[16,2,384,128]{3,2,1,0:T(8,128)(2,1)}, u32[]{:S(2)}, u32[]{:S(2)}) %all-to-all-start) | async-done | bytes 3145760 | tf_op jit(solution)/shard_map/all_to_all | solution.py:383
  133.6 43.7 %all_to_all.10.clipped_ref = s16[16,656,128]{2,1,0:T(8,128)(2,1)} all-to-all(s16[16,656,128]{2,1,0:T(8,128)(2,1)S(1)} %shard_map.77), channel_id=1, replica_groups=mesh['dp'=16,'tensor'=16] {'dp'}, dimensions={0} | all-to-all | bytes 5373952 | tf_op jit(solution)/shard_map/all_to_all | solution.py:389
  177.3 6.8 %shard_map.78 = f32[256,512]{1,0:T(8,128)} custom-call(s16[16,2,384,128]{3,2,1,0:T(8,128)(2,1)} %all-to-all-done.raw_ref, s16[16,656,128]{2,1,0:T(8,128)(2,1)} %all_to_all.10.clipped_ref, f32[256,512]{1,0:T(8,128)} %noise_ref.1), custom_call_target="tpu_custom_call" | custom-call | tf_op jit(solution)/shard_map/pallas_call | solution.py:334
  (52 shorter events, 0.2 us)
Async XLA Ops:
  6.5 18.4 %copy-start.14 = (s32[2]{0:T(128)S(1)}, s32[2]{0:T(128)}, u32[]{:S(2)}) copy-start(s32[2]{0:T(128)} %param.9) | copy-start | bytes 28
  6.5 94.1 %all-gather.3.cloned.1.call-start = ((), (), s32[]{:S(2)}) async-start(), calls=%async_computation.2 | async-start | bytes 11141120 | tf_op jit(solution)/shard_map/all_gather | solution.py:369
  8.8 11.1 %collective-permute-start = (bf16[2,64,1536]{2,1,0:T(8,128)(2,1)}, bf16[2,64,1536]{2,1,0:T(8,128)(2,1)S(1)}, u32[]{:S(2)}, u32[]{:S(2)}) collective-permute-start(bf16[2,64,1536]{2,1,0:T(8,128)(2,1)} %bitcast.10), channel_id=1, source_target_pairs={{0,2},{1,3},{2,4},{3,5},{4,6},{5,7},{6,8},{7,9},{8,10},{9,11},{10,... | collective-permute-start | bytes 1179656 | tf_op jit(solution)/shard_map/ppermute | solution.py:356
  10.7 11.0 %collective-permute-start.1 = (bf16[2,64,1536]{2,1,0:T(8,128)(2,1)}, bf16[2,64,1536]{2,1,0:T(8,128)(2,1)S(1)}, u32[]{:S(2)}, u32[]{:S(2)}) collective-permute-start(bf16[2,64,1536]{2,1,0:T(8,128)(2,1)} %bitcast.11), channel_id=1, source_target_pairs={{0,14},{1,15},{2,0},{3,1},{4,2},{5,3},{6,4},{7,5},{8,6},{9,7},{10,... | collective-permute-start | bytes 1179656 | tf_op jit(solution)/shard_map/ppermute | solution.py:356
  19.8 17.8 %copy-start.4 = (bf16[2,64,1536]{2,1,0:T(8,128)(2,1)}, bf16[2,64,1536]{2,1,0:T(8,128)(2,1)S(1)}, u32[]{:S(2)}) copy-start(bf16[2,64,1536]{2,1,0:T(8,128)(2,1)S(1)} %collective-permute-done.refs_2_) | copy-start | bytes 1179652
  21.7 16.4 %copy-start.5 = (bf16[2,64,1536]{2,1,0:T(8,128)(2,1)}, bf16[2,64,1536]{2,1,0:T(8,128)(2,1)S(1)}, u32[]{:S(2)}) copy-start(bf16[2,64,1536]{2,1,0:T(8,128)(2,1)S(1)} %collective-permute-done.1.refs_4_) | copy-start | bytes 1179652
  21.7 11.1 %collective-permute-start.2 = (bf16[2,64,1536]{2,1,0:T(8,128)(2,1)S(1)}, bf16[2,64,1536]{2,1,0:T(8,128)(2,1)}, u32[]{:S(2)}, u32[]{:S(2)}) collective-permute-start(bf16[2,64,1536]{2,1,0:T(8,128)(2,1)S(1)} %collective-permute-done.refs_2_), channel_id=1, source_target_pairs={{0,2},{1,3},{2,4},{3,5},{4,6},{5,7},{6,8},{7,9},{8,10},{9,11},{10,... | collective-permute-start | bytes 1179656 | tf_op jit(solution)/shard_map/ppermute | solution.py:356
  24.9 10.7 %collective-permute-start.3 = (bf16[2,64,1536]{2,1,0:T(8,128)(2,1)S(1)}, bf16[2,64,1536]{2,1,0:T(8,128)(2,1)}, u32[]{:S(2)}, u32[]{:S(2)}) collective-permute-start(bf16[2,64,1536]{2,1,0:T(8,128)(2,1)S(1)} %collective-permute-done.1.refs_4_), channel_id=1, source_target_pairs={{0,14},{1,15},{2,0},{3,1},{4,2},{5,3},{6,4},{7,5},{8,6},{9,7},{10,... | collective-permute-start | bytes 1179656 | tf_op jit(solution)/shard_map/ppermute | solution.py:356
  28.0 9.6 %copy-start.1 = (bf16[128,1536]{1,0:T(8,128)(2,1)S(1)}, bf16[128,1536]{1,0:T(8,128)(2,1)}, u32[]{:S(2)}) copy-start(bf16[128,1536]{1,0:T(8,128)(2,1)} %shard_map.73) | copy-start | bytes 1179652
  28.0 42.7 %copy-start.15 = (s32[16]{0:T(128)S(1)}, s32[16]{0:T(128)}, u32[]{:S(2)}) copy-start(s32[16]{0:T(128)} %constant.16.clone) | copy-start | bytes 196
  28.0 42.7 %copy-start.16 = (s32[16]{0:T(128)S(1)}, s32[16]{0:T(128)}, u32[]{:S(2)}) copy-start(s32[16]{0:T(128)} %constant.17.clone) | copy-start | bytes 196
  35.6 19.3 %collective-permute-start.9 = (bf16[2,64,1536]{2,1,0:T(8,128)(2,1)}, bf16[2,64,1536]{2,1,0:T(8,128)(2,1)S(1)}, u32[]{:S(2)}, u32[]{:S(2)}) collective-permute-start(bf16[2,64,1536]{2,1,0:T(8,128)(2,1)} %collective-permute-done.2.refs_6_), channel_id=1, source_target_pairs={{0,2},{1,3},{2,4},{3,5},{4,6},{5,7},{6,8},{7,9},{8,10},{9,11},{10,... | collective-permute-start | bytes 1179656 | tf_op jit(solution)/shard_map/ppermute | solution.py:356
  37.3 19.4 %collective-permute-start.11 = (bf16[2,64,1536]{2,1,0:T(8,128)(2,1)}, bf16[2,64,1536]{2,1,0:T(8,128)(2,1)S(1)}, u32[]{:S(2)}, u32[]{:S(2)}) collective-permute-start(bf16[2,64,1536]{2,1,0:T(8,128)(2,1)} %collective-permute-done.3.refs_8_), channel_id=1, source_target_pairs={{0,14},{1,15},{2,0},{3,1},{4,2},{5,3},{6,4},{7,5},{8,6},{9,7},{10,... | collective-permute-start | bytes 1179656 | tf_op jit(solution)/shard_map/ppermute | solution.py:356
  37.6 21.5 %collective-permute-start.4 = (bf16[2,64,1536]{2,1,0:T(8,128)(2,1)S(1)}, bf16[2,64,1536]{2,1,0:T(8,128)(2,1)S(1)}, u32[]{:S(2)}, u32[]{:S(2)}) collective-permute-start(bf16[2,64,1536]{2,1,0:T(8,128)(2,1)S(1)} %bitcast.13), channel_id=1, source_target_pairs={{0,1},{1,0},{2,3},{3,2},{4,5},{5,4},{6,7},{7,6},{8,9},{9,8},{10,11... | collective-permute-start | bytes 1179656 | tf_op jit(solution)/shard_map/ppermute | solution.py:359
  37.6 21.8 %collective-permute-start.5 = (bf16[2,64,1536]{2,1,0:T(8,128)(2,1)S(1)}, bf16[2,64,1536]{2,1,0:T(8,128)(2,1)S(1)}, u32[]{:S(2)}, u32[]{:S(2)}) collective-permute-start(bf16[2,64,1536]{2,1,0:T(8,128)(2,1)S(1)} %collective-permute-done.refs_2_), channel_id=1, source_target_pairs={{0,1},{1,0},{2,3},{3,2},{4,5},{5,4},{6,7},{7,6},{8,9},{9,8},{10,11... | collective-permute-start | bytes 1179656 | tf_op jit(solution)/shard_map/ppermute | solution.py:359
  38.1 21.3 %collective-permute-start.6 = (bf16[2,64,1536]{2,1,0:T(8,128)(2,1)S(1)}, bf16[2,64,1536]{2,1,0:T(8,128)(2,1)S(1)}, u32[]{:S(2)}, u32[]{:S(2)}) collective-permute-start(bf16[2,64,1536]{2,1,0:T(8,128)(2,1)S(1)} %collective-permute-done.1.refs_4_), channel_id=1, source_target_pairs={{0,1},{1,0},{2,3},{3,2},{4,5},{5,4},{6,7},{7,6},{8,9},{9,8},{10,11... | collective-permute-start | bytes 1179656 | tf_op jit(solution)/shard_map/ppermute | solution.py:359
  54.9 17.4 %copy-start.2 = (bf16[2,64,1536]{2,1,0:T(8,128)(2,1)}, bf16[2,64,1536]{2,1,0:T(8,128)(2,1)S(1)}, u32[]{:S(2)}) copy-start(bf16[2,64,1536]{2,1,0:T(8,128)(2,1)S(1)} %collective-permute-done.9.refs_10_) | copy-start | bytes 1179652
  54.9 5.0 %collective-permute-start.7 = (bf16[2,64,1536]{2,1,0:T(8,128)(2,1)}, bf16[2,64,1536]{2,1,0:T(8,128)(2,1)}, u32[]{:S(2)}, u32[]{:S(2)}) collective-permute-start(bf16[2,64,1536]{2,1,0:T(8,128)(2,1)} %collective-permute-done.2.refs_6_), channel_id=1, source_target_pairs={{0,1},{1,0},{2,3},{3,2},{4,5},{5,4},{6,7},{7,6},{8,9},{9,8},{10,11... | collective-permute-start | bytes 1179656 | tf_op jit(solution)/shard_map/ppermute | solution.py:359
  56.7 15.6 %copy-start.3 = (bf16[2,64,1536]{2,1,0:T(8,128)(2,1)}, bf16[2,64,1536]{2,1,0:T(8,128)(2,1)S(1)}, u32[]{:S(2)}) copy-start(bf16[2,64,1536]{2,1,0:T(8,128)(2,1)S(1)} %collective-permute-done.11.refs_12_) | copy-start | bytes 1179652
  56.7 11.3 %collective-permute-start.13 = (bf16[1,64,1536]{2,1,0:T(8,128)(2,1)S(1)}, bf16[1,64,1536]{2,1,0:T(8,128)(2,1)}, u32[]{:S(2)}, u32[]{:S(2)}) collective-permute-start(bf16[1,64,1536]{2,1,0:T(8,128)(2,1)S(1)} %slice.8), channel_id=1, source_target_pairs={{0,2},{1,3},{2,4},{3,5},{4,6},{5,7},{6,8},{7,9},{8,10},{9,11},{10,... | collective-permute-start | bytes 589832 | tf_op jit(solution)/shard_map/ppermute | solution.py:356
  59.1 13.2 %copy-start.6 = (bf16[2,64,1536]{2,1,0:T(8,128)(2,1)}, bf16[2,64,1536]{2,1,0:T(8,128)(2,1)S(1)}, u32[]{:S(2)}) copy-start(bf16[2,64,1536]{2,1,0:T(8,128)(2,1)S(1)} %collective-permute-done.4.refs_1_) | copy-start | bytes 1179652
  59.1 11.5 %collective-permute-start.15 = (bf16[1,64,1536]{2,1,0:T(8,128)(2,1)}, bf16[1,64,1536]{2,1,0:T(8,128)(2,1)}, u32[]{:S(2)}, u32[]{:S(2)}) collective-permute-start(bf16[1,64,1536]{2,1,0:T(8,128)(2,1)} %slice.9), channel_id=1, source_target_pairs={{0,14},{1,15},{2,0},{3,1},{4,2},{5,3},{6,4},{7,5},{8,6},{9,7},{10,... | collective-permute-start | bytes 589832 | tf_op jit(solution)/shard_map/ppermute | solution.py:356
  59.4 12.9 %copy-start.7 = (bf16[2,64,1536]{2,1,0:T(8,128)(2,1)}, bf16[2,64,1536]{2,1,0:T(8,128)(2,1)S(1)}, u32[]{:S(2)}) copy-start(bf16[2,64,1536]{2,1,0:T(8,128)(2,1)S(1)} %collective-permute-done.5.refs_3_) | copy-start | bytes 1179652
  59.4 11.8 %collective-permute-start.8 = (bf16[2,64,1536]{2,1,0:T(8,128)(2,1)}, bf16[2,64,1536]{2,1,0:T(8,128)(2,1)S(1)}, u32[]{:S(2)}, u32[]{:S(2)}) collective-permute-start(bf16[2,64,1536]{2,1,0:T(8,128)(2,1)} %collective-permute-done.3.refs_8_), channel_id=1, source_target_pairs={{0,1},{1,0},{2,3},{3,2},{4,5},{5,4},{6,7},{7,6},{8,9},{9,8},{10,11... | collective-permute-start | bytes 1179656 | tf_op jit(solution)/shard_map/ppermute | solution.py:359
  59.4 12.9 %copy-start.8 = (bf16[2,64,1536]{2,1,0:T(8,128)(2,1)}, bf16[2,64,1536]{2,1,0:T(8,128)(2,1)S(1)}, u32[]{:S(2)}) copy-start(bf16[2,64,1536]{2,1,0:T(8,128)(2,1)S(1)} %collective-permute-done.6.refs_5_) | copy-start | bytes 1179652
  59.4 12.9 %collective-permute-start.10 = (bf16[2,64,1536]{2,1,0:T(8,128)(2,1)S(1)}, bf16[2,64,1536]{2,1,0:T(8,128)(2,1)S(1)}, u32[]{:S(2)}, u32[]{:S(2)}) collective-permute-start(bf16[2,64,1536]{2,1,0:T(8,128)(2,1)S(1)} %collective-permute-done.9.refs_10_), channel_id=1, source_target_pairs={{0,1},{1,0},{2,3},{3,2},{4,5},{5,4},{6,7},{7,6},{8,9},{9,8},{10,11... | collective-permute-start | bytes 1179656 | tf_op jit(solution)/shard_map/ppermute | solution.py:359
  59.9 12.4 %collective-permute-start.12 = (bf16[2,64,1536]{2,1,0:T(8,128)(2,1)S(1)}, bf16[2,64,1536]{2,1,0:T(8,128)(2,1)S(1)}, u32[]{:S(2)}, u32[]{:S(2)}) collective-permute-start(bf16[2,64,1536]{2,1,0:T(8,128)(2,1)S(1)} %collective-permute-done.11.refs_12_), channel_id=1, source_target_pairs={{0,1},{1,0},{2,3},{3,2},{4,5},{5,4},{6,7},{7,6},{8,9},{9,8},{10,11... | collective-permute-start | bytes 1179656 | tf_op jit(solution)/shard_map/ppermute | solution.py:359
  68.0 3.2 %collective-permute-start.14 = (bf16[1,64,1536]{2,1,0:T(8,128)(2,1)}, bf16[1,64,1536]{2,1,0:T(8,128)(2,1)S(1)}, u32[]{:S(2)}, u32[]{:S(2)}) collective-permute-start(bf16[1,64,1536]{2,1,0:T(8,128)(2,1)} %collective-permute-done.13.refs_14_), channel_id=1, source_target_pairs={{0,1},{1,0},{2,3},{3,2},{4,5},{5,4},{6,7},{7,6},{8,9},{9,8},{10,11... | collective-permute-start | bytes 589832 | tf_op jit(solution)/shard_map/ppermute | solution.py:359
  70.6 1.7 collective-permute-start.16
  71.2 1.2 copy-start.9
  71.2 1.2 copy-start.12
  72.3 0.7 copy-start.13
  72.3 0.8 copy-start.10
  73.1 0.7 copy-start.11
  83.9 49.7 %all-to-all-start = ((s16[16,2,384,128]{3,2,1,0:T(8,128)(2,1)}), s16[16,2,384,128]{3,2,1,0:T(8,128)(2,1)}, u32[]{:S(2)}, u32[]{:S(2)}) async-start(s16[16,2,384,128]{3,2,1,0:T(8,128)(2,1)} %get-tuple-element.30), calls=%async_computation | async-start | bytes 6291456 | tf_op jit(solution)/shard_map/all_to_all | solution.py:383
  100.7 26.4 %copy-start = (f32[16,2,8,128]{3,2,1,0:T(8,128)S(1)}, f32[16,2,8,128]{3,2,1,0:T(8,128)}, u32[]{:S(2)}) copy-start(f32[16,2,8,128]{3,2,1,0:T(8,128)} %get-tuple-element.29.exponent_ref) | copy-start | bytes 393220
  112.1 2.0 %collective-permute-start.17 = (f32[2,1,128]{2,1,0:T(1,128)S(1)}, f32[2,1,128]{2,1,0:T(1,128)S(1)}, u32[]{:S(2)}, u32[]{:S(2)}) collective-permute-start(f32[2,1,128]{2,1,0:T(1,128)S(1)} %get-tuple-element.26), channel_id=1, source_target_pairs={{0,1},{1,0},{2,3},{3,2},{4,5},{5,4},{6,7},{7,6},{8,9},{9,8},{10,11... | collective-permute-start | bytes 3080 | tf_op jit(solution)/shard_map/ppermute | solution.py:359
  112.4 3.6 %collective-permute-start.18 = (f32[2,1,128]{2,1,0:T(1,128)S(1)}, f32[2,1,128]{2,1,0:T(1,128)S(1)}, u32[]{:S(2)}, u32[]{:S(2)}) collective-permute-start(f32[2,1,128]{2,1,0:T(1,128)S(1)} %get-tuple-element.26), channel_id=1, source_target_pairs={{0,2},{1,3},{2,0},{3,1},{4,6},{5,7},{6,4},{7,5},{8,10},{9,11},{10,... | collective-permute-start | bytes 3080 | tf_op jit(solution)/shard_map/ppermute | solution.py:359
  113.4 3.0 %collective-permute-start.19 = (f32[2,1,128]{2,1,0:T(1,128)S(1)}, f32[2,1,128]{2,1,0:T(1,128)S(1)}, u32[]{:S(2)}, u32[]{:S(2)}) collective-permute-start(f32[2,1,128]{2,1,0:T(1,128)S(1)} %get-tuple-element.26), channel_id=1, source_target_pairs={{0,3},{1,2},{2,1},{3,0},{4,7},{5,6},{6,5},{7,4},{8,11},{9,10},{10,... | collective-permute-start | bytes 3080 | tf_op jit(solution)/shard_map/ppermute | solution.py:359
  116.4 7.3 %collective-permute-start.20 = (f32[2,1,128]{2,1,0:T(1,128)S(1)}, f32[2,1,128]{2,1,0:T(1,128)S(1)}, u32[]{:S(2)}, u32[]{:S(2)}) collective-permute-start(f32[2,1,128]{2,1,0:T(1,128)S(1)} %add_add_fusion.1), channel_id=1, source_target_pairs={{0,4},{1,5},{2,6},{3,7},{4,0},{5,1},{6,2},{7,3},{8,12},{9,13},{10,... | collective-permute-start | bytes 3080 | tf_op jit(solution)/shard_map/ppermute | solution.py:359
  119.5 7.5 %collective-permute-start.21 = (f32[2,1,128]{2,1,0:T(1,128)S(1)}, f32[2,1,128]{2,1,0:T(1,128)S(1)}, u32[]{:S(2)}, u32[]{:S(2)}) collective-permute-start(f32[2,1,128]{2,1,0:T(1,128)S(1)} %add_add_fusion.1), channel_id=1, source_target_pairs={{0,8},{1,9},{2,10},{3,11},{4,12},{5,13},{6,14},{7,15},{8,0},{9,1},... | collective-permute-start | bytes 3080 | tf_op jit(solution)/shard_map/ppermute | solution.py:359
  121.4 5.7 %collective-permute-start.22 = (f32[2,1,128]{2,1,0:T(1,128)S(1)}, f32[2,1,128]{2,1,0:T(1,128)S(1)}, u32[]{:S(2)}, u32[]{:S(2)}) collective-permute-start(f32[2,1,128]{2,1,0:T(1,128)S(1)} %add_add_fusion.1), channel_id=1, source_target_pairs={{0,12},{1,13},{2,14},{3,15},{4,8},{5,9},{6,10},{7,11},{8,4},{9,5},... | collective-permute-start | bytes 3080 | tf_op jit(solution)/shard_map/ppermute | solution.py:359
Sparse Core Ops, SparseCore 0:
  21.8 78.8 all-gather.2

commit v3 on v2

--- a/solution.py
+++ b/solution.py
@@ -9,7 +9,7 @@
 
 LANES = 128
 EXTRA = 16
-TOGETHER = 2
+TOGETHER = 4
 LEAST = 1e-33
 PARAMS = pltpu.CompilerParams(vmem_limit_bytes=56 * 1024 * 1024)
 LESS = pltpu.CompilerParams(vmem_limit_bytes=28 * 1024 * 1024)
@@ -35,6 +35,9 @@
     taken = features // OWNED * sum(width for _, width in parts)
     return pl.pallas_call(
         functools.partial(part_kernel, parts),
+        grid=(examples,),
+        in_specs=[pl.BlockSpec((shard, features), lambda e: (e, 0))],
+        out_specs=pl.BlockSpec((shard, taken), lambda e: (e, 0)),
         out_shape=jax.ShapeDtypeStruct((examples * shard, taken), acts.dtype),
         compiler_params=PARAMS,
     )(acts.reshape(examples * shard, features)).reshape(examples, shard, taken)
@@ -364,20 +367,20 @@
     masked = jnp.where(positions < lengths[:, None, None], out_grads, jnp.zeros_like(out_grads))
     masked = jnp.swapaxes(masked, 1, 2)
 
+    step = jnp.array([2 * k for k in ARRIVALS for _ in range(2)], jnp.int32)
+    second_core = jnp.array([0, 1] * len(ARRIVALS), jnp.int32)
+    order = ((here & ~1) + step + ((here & 1) ^ second_core)) & (devices - 1)
+
     up1, down1 = along_z(own, 1), along_z(own, -1)
-    up1, down1, second = lax.optimization_barrier((up1, down1, second))
+    up2, down2 = along_z(up1, 1), along_z(down1, -1)
+    up2, down2, second, masked, order = lax.optimization_barrier((up2, down2, second, masked, order))
     second = lax.all_gather(second, "tensor")
-    up2, down2 = along_z(up1, 1), along_z(down1, -1)
-    up2, down2, masked = lax.optimization_barrier((up2, down2, masked))
     up3, down3 = along_z(up2, 1), along_z(down2, -1)
     up4, down4 = along_z(up3[:1], 1), along_z(down3[1:], -1)
     pieces = []
     for piece in (own, up1, down1, up2, down2, up3, down3):
         pieces += [piece, crossed(piece, 1)]
     pieces += [up4, crossed(up4, 1), down4, crossed(down4, 1)]
-    step = jnp.array([2 * k for k in ARRIVALS for _ in range(2)], jnp.int32)
-    second_core = jnp.array([0, 1] * len(ARRIVALS), jnp.int32)
-    order = ((here & ~1) + step + ((here & 1) ^ second_core)) & (devices - 1)
 
     raw, exponents, squares = raw_products(order, pieces, masked)
     raw = lax.all_to_all(raw, "dp", 0, 0)

time: 191 us -> 187 us (0.979)
  blocking collectives: 43.7 us -> 40.7 us
  waiting for transfers between devices: 63.5 us -> 60.5 us
  starting transfers between devices: 26.2 us -> 28.9 us
  Pallas kernels: 35.9 us -> 33.9 us
    all_gather x1, waiting for transfers between devices: 9.65 us -> 23.7 us  [per_device(): second = lax.all_gather(second, 'tensor')]
    ppermute x8, waiting for transfers between devices: 43.7 us -> 29.8 us  [along_z(): lax.ppermute(x, 'tensor', [(t, (t + 2 * k) % devices) for t in range(devi...]
    all_to_all x1, waiting for transfers between devices: 3.29 us -> 0.01 us  [per_device(): raw = lax.all_to_all(raw, 'dp', 0, 0)]
    all_to_all x1, blocking collectives: 43.7 us -> 40.7 us  [per_device(): clipped = lax.all_to_all(clipped, 'dp', 0, 0)]
    ppermute x8, starting transfers between devices: 9.29 us -> 11.4 us  [along_z(): lax.ppermute(x, 'tensor', [(t, (t + 2 * k) % devices) for t in range(devi...]
  transfers between devices with their start and end apart: 25 -> 25, of which waited for: 15 -> 13; matrix products, arithmetic and copies ran while one was open for 3% -> 3% of each run, Pallas kernels for 14% -> 14%
where the time goes in v3:
time: 187 us; the launch traced here: 186 us
  waiting for transfers between devices  60.5 us (32%)
  blocking collectives  40.7 us (22%)
  Pallas kernels  33.9 us (18%)
  starting transfers between devices  28.9 us (15%)
  between operations  14.3 us (8%)
  local copies, waits for them, and re-layouts  4.54 us (2%)
  other arithmetic  3.44 us (2%)
    all_to_all x1, blocking collectives, per_device(): clipped = lax.all_to_all(clipped, 'dp', 0, 0)  40.7 us
    ppermute x8, waiting for transfers between devices, along_z(): lax.ppermute(x, 'tensor', [(t, (t + 2 * k) % devices) for t in range(devi...  29.8 us
    all_gather x1, waiting for transfers between devices, per_device(): second = lax.all_gather(second, 'tensor')  23.7 us
    ppermute x8, starting transfers between devices, along_z(): lax.ppermute(x, 'tensor', [(t, (t + 2 * k) % devices) for t in range(devi...  11.4 us
    pallas_call x1, Pallas kernels, plain_products(): pl.pallas_call(plain_kernel, grid=(examples, features // width), in_specs...  11.4 us
    ppermute x15, starting transfers between devices, crossed(): return lax.ppermute(x, 'tensor', [(t, t ^ k) for t in range(devices)])  10.3 us
    pallas_call x1, Pallas kernels, raw_products(): pl.pallas_call(raw_kernel, grid=(examples,), in_specs=[pl.BlockSpec(memor...  9.99 us
    all_to_all x1, starting transfers between devices, per_device(): raw = lax.all_to_all(raw, 'dp', 0, 0)  7.13 us
  transfers between devices with their start and end apart: 25, of which 13 were waited for; matrix products, arithmetic and copies ran while one was open for 3% of the time, Pallas kernels for 14%

profile of v3, /device:TPU:32, one launch (start us, length us, event | category | flops | bytes accessed | tf_op | source)
XLA Modules:
  0.0 186.2 jit_solution(10527914929547039477)
XLA Ops:
  6.5 2.0 %shard_map.73 = bf16[128,1536]{1,0:T(8,128)(2,1)} custom-call(bf16[128,4096]{1,0:T(8,128)(2,1)} %bitcast.7), custom_call_target="tpu_custom_call" | custom-call | tf_op jit(solution)/shard_map/pallas_call | solution.py:36
  8.6 1.9 %collective-permute-start = (bf16[2,64,1536]{2,1,0:T(8,128)(2,1)}, bf16[2,64,1536]{2,1,0:T(8,128)(2,1)S(1)}, u32[]{:S(2)}, u32[]{:S(2)}) collective-permute-start(bf16[2,64,1536]{2,1,0:T(8,128)(2,1)} %bitcast.10), channel_id=1, source_target_pairs={{0,2},{1,3},{2,4},{3,5},{4,6},{5,7},{6,8},{7,9},{8,10},{9,11},{10,... | collective-permute-start | bytes 1179656 | tf_op jit(solution)/shard_map/ppermute | solution.py:359
  10.5 0.1 collective-permute-start.2
  10.6 0.7 iota_compare_fusion
  11.3 8.3 %collective-permute-done.refs_2_ = bf16[2,64,1536]{2,1,0:T(8,128)(2,1)S(1)} collective-permute-done((bf16[2,64,1536]{2,1,0:T(8,128)(2,1)}, bf16[2,64,1536]{2,1,0:T(8,128)(2,1)S(1)}, u32[]{:S(2)}, u32[]{:S(2)}) %collective-permute-start) | collective-permute-done | bytes 393248 | tf_op jit(solution)/shard_map/ppermute | solution.py:359
  19.6 1.9 %collective-permute-start.1 = (bf16[2,64,1536]{2,1,0:T(8,128)(2,1)S(1)}, bf16[2,64,1536]{2,1,0:T(8,128)(2,1)}, u32[]{:S(2)}, u32[]{:S(2)}) collective-permute-start(bf16[2,64,1536]{2,1,0:T(8,128)(2,1)S(1)} %collective-permute-done.refs_2_), channel_id=1, source_target_pairs={{0,2},{1,3},{2,4},{3,5},{4,6},{5,7},{6,8},{7,9},{8,10},{9,11},{10,... | collective-permute-start | bytes 1179656 | tf_op jit(solution)/shard_map/ppermute | solution.py:359
  21.6 2.4 %collective-permute-start.3 = (bf16[2,64,1536]{2,1,0:T(8,128)(2,1)S(1)}, bf16[2,64,1536]{2,1,0:T(8,128)(2,1)}, u32[]{:S(2)}, u32[]{:S(2)}) collective-permute-start(bf16[2,64,1536]{2,1,0:T(8,128)(2,1)S(1)} %collective-permute-done.2.refs_4_), channel_id=1, source_target_pairs={{0,14},{1,15},{2,0},{3,1},{4,2},{5,3},{6,4},{7,5},{8,6},{9,7},{10,... | collective-permute-start | bytes 1179656 | tf_op jit(solution)/shard_map/ppermute | solution.py:359
  24.0 1.2 add_and_fusion.order_ref
  25.2 2.0 %shard_map.74 = bf16[128,2560]{1,0:T(8,128)(2,1)} custom-call(bf16[128,4096]{1,0:T(8,128)(2,1)} %bitcast.8), custom_call_target="tpu_custom_call" | custom-call | tf_op jit(solution)/shard_map/pallas_call | solution.py:36
  27.2 3.0 %copy.9 = bf16[2,1024,512]{1,2,0:T(8,128)(2,1)S(1)} copy(bf16[2,1024,512]{2,1,0:T(8,128)(2,1)} %param.8) | data formatting | bytes 4194304 | tf_op args[1]
  30.2 0.0 copy-start.1
  30.2 1.5 select_bitcast_fusion.refs_18_.grads_ref
  31.7 0.8 collective-permute-done.1.refs_6_
  32.5 0.4 collective-permute-done.3.refs_8_
  33.0 0.0 all-gather.3.cloned.1.call-update
  33.0 3.0 %collective-permute-start.9 = (bf16[2,64,1536]{2,1,0:T(8,128)(2,1)}, bf16[2,64,1536]{2,1,0:T(8,128)(2,1)S(1)}, u32[]{:S(2)}, u32[]{:S(2)}) collective-permute-start(bf16[2,64,1536]{2,1,0:T(8,128)(2,1)} %collective-permute-done.1.refs_6_), channel_id=1, source_target_pairs={{0,2},{1,3},{2,4},{3,5},{4,6},{5,7},{6,8},{7,9},{8,10},{9,11},{10,... | collective-permute-start | bytes 1179656 | tf_op jit(solution)/shard_map/ppermute | solution.py:359
  36.0 0.0 collective-permute-start.11
  36.0 0.5 collective-permute-start.5
  36.5 0.1 collective-permute-start.6
  36.6 6.8 %collective-permute-done.9.refs_10_ = bf16[2,64,1536]{2,1,0:T(8,128)(2,1)S(1)} collective-permute-done((bf16[2,64,1536]{2,1,0:T(8,128)(2,1)}, bf16[2,64,1536]{2,1,0:T(8,128)(2,1)S(1)}, u32[]{:S(2)}, u32[]{:S(2)}) %collective-permute-start.9) | collective-permute-done | bytes 393248 | tf_op jit(solution)/shard_map/ppermute | solution.py:359
  43.5 2.5 %collective-permute-done.11.refs_12_ = bf16[2,64,1536]{2,1,0:T(8,128)(2,1)S(1)} collective-permute-done((bf16[2,64,1536]{2,1,0:T(8,128)(2,1)}, bf16[2,64,1536]{2,1,0:T(8,128)(2,1)S(1)}, u32[]{:S(2)}, u32[]{:S(2)}) %collective-permute-start.11) | collective-permute-done | bytes 393248 | tf_op jit(solution)/shard_map/ppermute | solution.py:359
  46.0 1.8 collective-permute-start.13
  47.8 0.3 collective-permute-start.15
  48.1 0.1 collective-permute-start.10
  48.1 0.5 collective-permute-start.12
  48.6 9.2 %collective-permute-done.13.refs_14_ = bf16[1,64,1536]{2,1,0:T(8,128)(2,1)S(1)} collective-permute-done((bf16[1,64,1536]{2,1,0:T(8,128)(2,1)S(1)}, bf16[1,64,1536]{2,1,0:T(8,128)(2,1)S(1)}, u32[]{:S(2)}, u32[]{:S(2)}) %collective-permute-start.13) | collective-permute-done | bytes 196640 | tf_op jit(solution)/shard_map/ppermute | solution.py:359
  57.8 1.7 collective-permute-done.15.refs_16_
  59.5 0.0 collective-permute-start.16
  59.6 1.4 collective-permute-done.16.refs_17_
  61.1 0.6 copy-done.16
  61.6 0.2 copy-done.11
  61.8 0.7 copy-done.12
  62.5 10.0 %shard_map.75 = (s16[16,2,384,128]{3,2,1,0:T(8,128)(2,1)}, f32[16,2,8,128]{3,2,1,0:T(8,128)}, f32[2,1,128]{2,1,0:T(1,128)}) custom-call(s32[16]{0:T(128)} %add_and_fusion.order_ref, bf16[2,64,1536]{2,1,0:T(8,128)(2,1)} %bitcast.12, bf16[2,64,1536]{2,1,0:T(8,128)(2,1)} %copy-done.6, bf16[2,64,1536]{2,1,0:T(8,128)(2,1)} %copy-done.4, ...), custom_call_target="tpu_custom_call" | custom-call | tf_op jit(solution)/shard_map/pallas_call | solution.py:133
  72.6 7.1 %all-to-all-start = ((s16[16,2,384,128]{3,2,1,0:T(8,128)(2,1)}), s16[16,2,384,128]{3,2,1,0:T(8,128)(2,1)}, u32[]{:S(2)}, u32[]{:S(2)}) async-start(s16[16,2,384,128]{3,2,1,0:T(8,128)(2,1)} %get-tuple-element.28), calls=%async_computation | async-start | bytes 6291456 | tf_op jit(solution)/shard_map/all_to_all | solution.py:386
  79.7 23.7 %all-gather.3.cloned.1.call-done = bf16[32,64,2560]{2,1,0:T(8,128)(2,1)} async-done(((bf16[2,64,2560]{2,1,0:T(8,128)(2,1)}), bf16[32,64,2560]{2,1,0:T(8,128)(2,1)}) %all-gather.3.cloned.1.call-update) | async-done | bytes 10485776 | tf_op jit(solution)/shard_map/all_gather | solution.py:377
  103.4 11.4 %shard_map.76 = (f32[2,512,2560]{2,1,0:T(8,128)S(1)}, f32[2,1,2560]{2,1,0:T(1,128)S(1)}, f32[2,1,128]{2,1,0:T(1,128)S(1)}) custom-call(bf16[16,2,64,2560]{3,2,1,0:T(8,128)(2,1)} %bitcast.6, bf16[2,512,1024]{2,1,0:T(8,128)(2,1)} %select_bitcast_fusion.refs_18_.grads_ref, f32[2,1,128]{2,1,0:T(1,128)} %get-tuple-element.23.squares_ref), custom_call_target="tpu_custom_call" | custom-call | flops 1 | bytes 1 | tf_op jit(solution)/shard_map/pallas_call | solution.py:203
  114.8 0.3 collective-permute-start.17
  115.1 2.3 %collective-permute-start.18 = (f32[2,1,128]{2,1,0:T(1,128)S(1)}, f32[2,1,128]{2,1,0:T(1,128)S(1)}, u32[]{:S(2)}, u32[]{:S(2)}) collective-permute-start(f32[2,1,128]{2,1,0:T(1,128)S(1)} %get-tuple-element.24), channel_id=1, source_target_pairs={{0,2},{1,3},{2,0},{3,1},{4,6},{5,7},{6,4},{7,5},{8,10},{9,11},{10,... | collective-permute-start | bytes 3080 | tf_op jit(solution)/shard_map/ppermute | solution.py:362
  117.4 1.5 collective-permute-done.18
  119.0 1.4 collective-permute-done.19
  120.4 2.1 %collective-permute-start.20 = (f32[2,1,128]{2,1,0:T(1,128)S(1)}, f32[2,1,128]{2,1,0:T(1,128)S(1)}, u32[]{:S(2)}, u32[]{:S(2)}) collective-permute-start(f32[2,1,128]{2,1,0:T(1,128)S(1)} %add_add_fusion.1), channel_id=1, source_target_pairs={{0,4},{1,5},{2,6},{3,7},{4,0},{5,1},{6,2},{7,3},{8,12},{9,13},{10,... | collective-permute-start | bytes 3080 | tf_op jit(solution)/shard_map/ppermute | solution.py:362
  122.5 2.0 %collective-permute-start.21 = (f32[2,1,128]{2,1,0:T(1,128)S(1)}, f32[2,1,128]{2,1,0:T(1,128)S(1)}, u32[]{:S(2)}, u32[]{:S(2)}) collective-permute-start(f32[2,1,128]{2,1,0:T(1,128)S(1)} %add_add_fusion.1), channel_id=1, source_target_pairs={{0,8},{1,9},{2,10},{3,11},{4,12},{5,13},{6,14},{7,15},{8,0},{9,1},... | collective-permute-start | bytes 3080 | tf_op jit(solution)/shard_map/ppermute | solution.py:362
  124.5 2.4 %collective-permute-start.22 = (f32[2,1,128]{2,1,0:T(1,128)S(1)}, f32[2,1,128]{2,1,0:T(1,128)S(1)}, u32[]{:S(2)}, u32[]{:S(2)}) collective-permute-start(f32[2,1,128]{2,1,0:T(1,128)S(1)} %add_add_fusion.1), channel_id=1, source_target_pairs={{0,12},{1,13},{2,14},{3,15},{4,8},{5,9},{6,10},{7,11},{8,4},{9,5},... | collective-permute-start | bytes 3080 | tf_op jit(solution)/shard_map/ppermute | solution.py:362
  127.6 2.4 %collective-permute-done.21 = f32[2,1,128]{2,1,0:T(1,128)S(1)} collective-permute-done((f32[2,1,128]{2,1,0:T(1,128)S(1)}, f32[2,1,128]{2,1,0:T(1,128)S(1)}, u32[]{:S(2)}, u32[]{:S(2)}) %collective-permute-start.21) | collective-permute-done | bytes 1056 | tf_op jit(solution)/shard_map/ppermute | solution.py:362
  130.0 0.2 collective-permute-done.22
  130.2 3.2 %shard_map.77 = s16[16,656,128]{2,1,0:T(8,128)(2,1)S(1)} custom-call(f32[1]{0:T(128)S(6)} %copy.10.clip_ref, f32[2,1,128]{2,1,0:T(1,128)S(1)} %add_add_fusion.shares_ref, f32[2,512,2560]{2,1,0:T(8,128)S(1)} %get-tuple-element.25.wide_ref.thin_ref, f32[2,512,2560]{2,1,0:T(8,128)S(1)} %get-tuple-element.25.wide_ref.thin_ref, ...), custom_call_target="tpu_custom_call" | custom-call | flops 1 | bytes 1 | tf_op jit(solution)/shard_map/pallas_call | solution.py:265
  133.5 40.7 %all_to_all.10.clipped_ref = s16[16,656,128]{2,1,0:T(8,128)(2,1)} all-to-all(s16[16,656,128]{2,1,0:T(8,128)(2,1)S(1)} %shard_map.77), channel_id=1, replica_groups=mesh['dp'=16,'tensor'=16] {'dp'}, dimensions={0} | all-to-all | bytes 5373952 | tf_op jit(solution)/shard_map/all_to_all | solution.py:392
  174.2 5.2 %shard_map.78 = f32[256,512]{1,0:T(8,128)} custom-call(s16[16,2,384,128]{3,2,1,0:T(8,128)(2,1)} %all-to-all-done.raw_ref, s16[16,656,128]{2,1,0:T(8,128)(2,1)} %all_to_all.10.clipped_ref, f32[256,512]{1,0:T(8,128)} %noise_ref.1), custom_call_target="tpu_custom_call" | custom-call | tf_op jit(solution)/shard_map/pallas_call | solution.py:337
  (52 shorter events, 0.1 us)
Async XLA Ops:
  6.5 96.8 %all-gather.3.cloned.1.call-start = ((), (), s32[]{:S(2)}) async-start(), calls=%async_computation.2 | async-start | bytes 11141120 | tf_op jit(solution)/shard_map/all_gather | solution.py:377
  8.6 11.1 %collective-permute-start = (bf16[2,64,1536]{2,1,0:T(8,128)(2,1)}, bf16[2,64,1536]{2,1,0:T(8,128)(2,1)S(1)}, u32[]{:S(2)}, u32[]{:S(2)}) collective-permute-start(bf16[2,64,1536]{2,1,0:T(8,128)(2,1)} %bitcast.10), channel_id=1, source_target_pairs={{0,2},{1,3},{2,4},{3,5},{4,6},{5,7},{6,8},{7,9},{8,10},{9,11},{10,... | collective-permute-start | bytes 1179656 | tf_op jit(solution)/shard_map/ppermute | solution.py:359
  10.5 11.1 %collective-permute-start.2 = (bf16[2,64,1536]{2,1,0:T(8,128)(2,1)}, bf16[2,64,1536]{2,1,0:T(8,128)(2,1)S(1)}, u32[]{:S(2)}, u32[]{:S(2)}) collective-permute-start(bf16[2,64,1536]{2,1,0:T(8,128)(2,1)} %bitcast.11), channel_id=1, source_target_pairs={{0,14},{1,15},{2,0},{3,1},{4,2},{5,3},{6,4},{7,5},{8,6},{9,7},{10,... | collective-permute-start | bytes 1179656 | tf_op jit(solution)/shard_map/ppermute | solution.py:359
  19.6 16.4 %copy-start.4 = (bf16[2,64,1536]{2,1,0:T(8,128)(2,1)}, bf16[2,64,1536]{2,1,0:T(8,128)(2,1)S(1)}, u32[]{:S(2)}) copy-start(bf16[2,64,1536]{2,1,0:T(8,128)(2,1)S(1)} %collective-permute-done.refs_2_) | copy-start | bytes 1179652
  19.6 12.9 %collective-permute-start.1 = (bf16[2,64,1536]{2,1,0:T(8,128)(2,1)S(1)}, bf16[2,64,1536]{2,1,0:T(8,128)(2,1)}, u32[]{:S(2)}, u32[]{:S(2)}) collective-permute-start(bf16[2,64,1536]{2,1,0:T(8,128)(2,1)S(1)} %collective-permute-done.refs_2_), channel_id=1, source_target_pairs={{0,2},{1,3},{2,4},{3,5},{4,6},{5,7},{6,8},{7,9},{8,10},{9,11},{10,... | collective-permute-start | bytes 1179656 | tf_op jit(solution)/shard_map/ppermute | solution.py:359
  21.6 14.9 %copy-start.5 = (bf16[2,64,1536]{2,1,0:T(8,128)(2,1)}, bf16[2,64,1536]{2,1,0:T(8,128)(2,1)S(1)}, u32[]{:S(2)}) copy-start(bf16[2,64,1536]{2,1,0:T(8,128)(2,1)S(1)} %collective-permute-done.2.refs_4_) | copy-start | bytes 1179652
  21.6 11.4 %collective-permute-start.3 = (bf16[2,64,1536]{2,1,0:T(8,128)(2,1)S(1)}, bf16[2,64,1536]{2,1,0:T(8,128)(2,1)}, u32[]{:S(2)}, u32[]{:S(2)}) collective-permute-start(bf16[2,64,1536]{2,1,0:T(8,128)(2,1)S(1)} %collective-permute-done.2.refs_4_), channel_id=1, source_target_pairs={{0,14},{1,15},{2,0},{3,1},{4,2},{5,3},{6,4},{7,5},{8,6},{9,7},{10,... | collective-permute-start | bytes 1179656 | tf_op jit(solution)/shard_map/ppermute | solution.py:359
  30.2 5.8 %copy-start.1 = (bf16[128,1536]{1,0:T(8,128)(2,1)S(1)}, bf16[128,1536]{1,0:T(8,128)(2,1)}, u32[]{:S(2)}) copy-start(bf16[128,1536]{1,0:T(8,128)(2,1)} %shard_map.73) | copy-start | bytes 1179652
  33.0 10.5 %collective-permute-start.9 = (bf16[2,64,1536]{2,1,0:T(8,128)(2,1)}, bf16[2,64,1536]{2,1,0:T(8,128)(2,1)S(1)}, u32[]{:S(2)}, u32[]{:S(2)}) collective-permute-start(bf16[2,64,1536]{2,1,0:T(8,128)(2,1)} %collective-permute-done.1.refs_6_), channel_id=1, source_target_pairs={{0,2},{1,3},{2,4},{3,5},{4,6},{5,7},{6,8},{7,9},{8,10},{9,11},{10,... | collective-permute-start | bytes 1179656 | tf_op jit(solution)/shard_map/ppermute | solution.py:359
  36.0 9.9 %collective-permute-start.11 = (bf16[2,64,1536]{2,1,0:T(8,128)(2,1)}, bf16[2,64,1536]{2,1,0:T(8,128)(2,1)S(1)}, u32[]{:S(2)}, u32[]{:S(2)}) collective-permute-start(bf16[2,64,1536]{2,1,0:T(8,128)(2,1)} %collective-permute-done.3.refs_8_), channel_id=1, source_target_pairs={{0,14},{1,15},{2,0},{3,1},{4,2},{5,3},{6,4},{7,5},{8,6},{9,7},{10,... | collective-permute-start | bytes 1179656 | tf_op jit(solution)/shard_map/ppermute | solution.py:359
  36.0 9.9 %collective-permute-start.4 = (bf16[2,64,1536]{2,1,0:T(8,128)(2,1)S(1)}, bf16[2,64,1536]{2,1,0:T(8,128)(2,1)S(1)}, u32[]{:S(2)}, u32[]{:S(2)}) collective-permute-start(bf16[2,64,1536]{2,1,0:T(8,128)(2,1)S(1)} %bitcast.13), channel_id=1, source_target_pairs={{0,1},{1,0},{2,3},{3,2},{4,5},{5,4},{6,7},{7,6},{8,9},{9,8},{10,11... | collective-permute-start | bytes 1179656 | tf_op jit(solution)/shard_map/ppermute | solution.py:362
  36.0 11.8 %collective-permute-start.5 = (bf16[2,64,1536]{2,1,0:T(8,128)(2,1)S(1)}, bf16[2,64,1536]{2,1,0:T(8,128)(2,1)S(1)}, u32[]{:S(2)}, u32[]{:S(2)}) collective-permute-start(bf16[2,64,1536]{2,1,0:T(8,128)(2,1)S(1)} %collective-permute-done.refs_2_), channel_id=1, source_target_pairs={{0,1},{1,0},{2,3},{3,2},{4,5},{5,4},{6,7},{7,6},{8,9},{9,8},{10,11... | collective-permute-start | bytes 1179656 | tf_op jit(solution)/shard_map/ppermute | solution.py:362
  36.5 11.6 %collective-permute-start.6 = (bf16[2,64,1536]{2,1,0:T(8,128)(2,1)S(1)}, bf16[2,64,1536]{2,1,0:T(8,128)(2,1)S(1)}, u32[]{:S(2)}, u32[]{:S(2)}) collective-permute-start(bf16[2,64,1536]{2,1,0:T(8,128)(2,1)S(1)} %collective-permute-done.2.refs_4_), channel_id=1, source_target_pairs={{0,1},{1,0},{2,3},{3,2},{4,5},{5,4},{6,7},{7,6},{8,9},{9,8},{10,11... | collective-permute-start | bytes 1179656 | tf_op jit(solution)/shard_map/ppermute | solution.py:362
  43.4 17.5 %copy-start.2 = (bf16[2,64,1536]{2,1,0:T(8,128)(2,1)}, bf16[2,64,1536]{2,1,0:T(8,128)(2,1)S(1)}, u32[]{:S(2)}) copy-start(bf16[2,64,1536]{2,1,0:T(8,128)(2,1)S(1)} %collective-permute-done.9.refs_10_) | copy-start | bytes 1179652
  43.4 4.7 %collective-permute-start.7 = (bf16[2,64,1536]{2,1,0:T(8,128)(2,1)}, bf16[2,64,1536]{2,1,0:T(8,128)(2,1)S(1)}, u32[]{:S(2)}, u32[]{:S(2)}) collective-permute-start(bf16[2,64,1536]{2,1,0:T(8,128)(2,1)} %collective-permute-done.1.refs_6_), channel_id=1, source_target_pairs={{0,1},{1,0},{2,3},{3,2},{4,5},{5,4},{6,7},{7,6},{8,9},{9,8},{10,11... | collective-permute-start | bytes 1179656 | tf_op jit(solution)/shard_map/ppermute | solution.py:362
  45.9 15.1 %copy-start.3 = (bf16[2,64,1536]{2,1,0:T(8,128)(2,1)}, bf16[2,64,1536]{2,1,0:T(8,128)(2,1)S(1)}, u32[]{:S(2)}) copy-start(bf16[2,64,1536]{2,1,0:T(8,128)(2,1)S(1)} %collective-permute-done.11.refs_12_) | copy-start | bytes 1179652
  45.9 13.6 %collective-permute-start.8 = (bf16[2,64,1536]{2,1,0:T(8,128)(2,1)}, bf16[2,64,1536]{2,1,0:T(8,128)(2,1)S(1)}, u32[]{:S(2)}, u32[]{:S(2)}) collective-permute-start(bf16[2,64,1536]{2,1,0:T(8,128)(2,1)} %collective-permute-done.3.refs_8_), channel_id=1, source_target_pairs={{0,1},{1,0},{2,3},{3,2},{4,5},{5,4},{6,7},{7,6},{8,9},{9,8},{10,11... | collective-permute-start | bytes 1179656 | tf_op jit(solution)/shard_map/ppermute | solution.py:362
  46.0 15.0 %copy-start.6 = (bf16[2,64,1536]{2,1,0:T(8,128)(2,1)}, bf16[2,64,1536]{2,1,0:T(8,128)(2,1)S(1)}, u32[]{:S(2)}) copy-start(bf16[2,64,1536]{2,1,0:T(8,128)(2,1)S(1)} %collective-permute-done.4.refs_1_) | copy-start | bytes 1179652
  46.0 11.8 %collective-permute-start.13 = (bf16[1,64,1536]{2,1,0:T(8,128)(2,1)S(1)}, bf16[1,64,1536]{2,1,0:T(8,128)(2,1)S(1)}, u32[]{:S(2)}, u32[]{:S(2)}) collective-permute-start(bf16[1,64,1536]{2,1,0:T(8,128)(2,1)S(1)} %slice.8), channel_id=1, source_target_pairs={{0,2},{1,3},{2,4},{3,5},{4,6},{5,7},{6,8},{7,9},{8,10},{9,11},{10,... | collective-permute-start | bytes 589832 | tf_op jit(solution)/shard_map/ppermute | solution.py:359
  47.8 13.2 %copy-start.7 = (bf16[2,64,1536]{2,1,0:T(8,128)(2,1)}, bf16[2,64,1536]{2,1,0:T(8,128)(2,1)S(1)}, u32[]{:S(2)}) copy-start(bf16[2,64,1536]{2,1,0:T(8,128)(2,1)S(1)} %collective-permute-done.5.refs_3_) | copy-start | bytes 1179652
  47.8 11.7 %collective-permute-start.15 = (bf16[1,64,1536]{2,1,0:T(8,128)(2,1)S(1)}, bf16[1,64,1536]{2,1,0:T(8,128)(2,1)S(1)}, u32[]{:S(2)}, u32[]{:S(2)}) collective-permute-start(bf16[1,64,1536]{2,1,0:T(8,128)(2,1)S(1)} %slice.9), channel_id=1, source_target_pairs={{0,14},{1,15},{2,0},{3,1},{4,2},{5,3},{6,4},{7,5},{8,6},{9,7},{10,... | collective-permute-start | bytes 589832 | tf_op jit(solution)/shard_map/ppermute | solution.py:359
  48.1 12.9 %copy-start.8 = (bf16[2,64,1536]{2,1,0:T(8,128)(2,1)}, bf16[2,64,1536]{2,1,0:T(8,128)(2,1)S(1)}, u32[]{:S(2)}) copy-start(bf16[2,64,1536]{2,1,0:T(8,128)(2,1)S(1)} %collective-permute-done.6.refs_5_) | copy-start | bytes 1179652
  48.1 12.9 %collective-permute-start.10 = (bf16[2,64,1536]{2,1,0:T(8,128)(2,1)S(1)}, bf16[2,64,1536]{2,1,0:T(8,128)(2,1)S(1)}, u32[]{:S(2)}, u32[]{:S(2)}) collective-permute-start(bf16[2,64,1536]{2,1,0:T(8,128)(2,1)S(1)} %collective-permute-done.9.refs_10_), channel_id=1, source_target_pairs={{0,1},{1,0},{2,3},{3,2},{4,5},{5,4},{6,7},{7,6},{8,9},{9,8},{10,11... | collective-permute-start | bytes 1179656 | tf_op jit(solution)/shard_map/ppermute | solution.py:362
  48.1 12.9 %copy-start.9 = (bf16[2,64,1536]{2,1,0:T(8,128)(2,1)}, bf16[2,64,1536]{2,1,0:T(8,128)(2,1)S(1)}, u32[]{:S(2)}) copy-start(bf16[2,64,1536]{2,1,0:T(8,128)(2,1)S(1)} %collective-permute-done.7.refs_7_) | copy-start | bytes 1179652
  48.1 12.8 %collective-permute-start.12 = (bf16[2,64,1536]{2,1,0:T(8,128)(2,1)S(1)}, bf16[2,64,1536]{2,1,0:T(8,128)(2,1)S(1)}, u32[]{:S(2)}, u32[]{:S(2)}) collective-permute-start(bf16[2,64,1536]{2,1,0:T(8,128)(2,1)S(1)} %collective-permute-done.11.refs_12_), channel_id=1, source_target_pairs={{0,1},{1,0},{2,3},{3,2},{4,5},{5,4},{6,7},{7,6},{8,9},{9,8},{10,11... | collective-permute-start | bytes 1179656 | tf_op jit(solution)/shard_map/ppermute | solution.py:362
  57.8 3.2 %copy-start.13 = (bf16[1,64,1536]{2,1,0:T(8,128)(2,1)}, bf16[1,64,1536]{2,1,0:T(8,128)(2,1)S(1)}, u32[]{:S(2)}) copy-start(bf16[1,64,1536]{2,1,0:T(8,128)(2,1)S(1)} %collective-permute-done.13.refs_14_) | copy-start | bytes 589828
  57.8 1.7 collective-permute-start.14
  59.5 1.5 copy-start.14
  59.5 1.4 collective-permute-start.16
  59.5 1.5 copy-start.10
  59.6 1.5 copy-start.15
  61.0 0.7 copy-start.16
  61.0 0.8 copy-start.11
  61.8 0.7 copy-start.12
  72.6 60.9 %all-to-all-start = ((s16[16,2,384,128]{3,2,1,0:T(8,128)(2,1)}), s16[16,2,384,128]{3,2,1,0:T(8,128)(2,1)}, u32[]{:S(2)}, u32[]{:S(2)}) async-start(s16[16,2,384,128]{3,2,1,0:T(8,128)(2,1)} %get-tuple-element.28), calls=%async_computation | async-start | bytes 6291456 | tf_op jit(solution)/shard_map/all_to_all | solution.py:386
  103.4 26.8 %copy-start = (f32[16,2,8,128]{3,2,1,0:T(8,128)S(1)}, f32[16,2,8,128]{3,2,1,0:T(8,128)}, u32[]{:S(2)}) copy-start(f32[16,2,8,128]{3,2,1,0:T(8,128)} %get-tuple-element.27.exponent_ref) | copy-start | bytes 393220
  114.8 2.7 %collective-permute-start.17 = (f32[2,1,128]{2,1,0:T(1,128)S(1)}, f32[2,1,128]{2,1,0:T(1,128)S(1)}, u32[]{:S(2)}, u32[]{:S(2)}) collective-permute-start(f32[2,1,128]{2,1,0:T(1,128)S(1)} %get-tuple-element.24), channel_id=1, source_target_pairs={{0,1},{1,0},{2,3},{3,2},{4,5},{5,4},{6,7},{7,6},{8,9},{9,8},{10,11... | collective-permute-start | bytes 3080 | tf_op jit(solution)/shard_map/ppermute | solution.py:362
  115.1 3.9 %collective-permute-start.18 = (f32[2,1,128]{2,1,0:T(1,128)S(1)}, f32[2,1,128]{2,1,0:T(1,128)S(1)}, u32[]{:S(2)}, u32[]{:S(2)}) collective-permute-start(f32[2,1,128]{2,1,0:T(1,128)S(1)} %get-tuple-element.24), channel_id=1, source_target_pairs={{0,2},{1,3},{2,0},{3,1},{4,6},{5,7},{6,4},{7,5},{8,10},{9,11},{10,... | collective-permute-start | bytes 3080 | tf_op jit(solution)/shard_map/ppermute | solution.py:362
  117.4 3.0 %collective-permute-start.19 = (f32[2,1,128]{2,1,0:T(1,128)S(1)}, f32[2,1,128]{2,1,0:T(1,128)S(1)}, u32[]{:S(2)}, u32[]{:S(2)}) collective-permute-start(f32[2,1,128]{2,1,0:T(1,128)S(1)} %get-tuple-element.24), channel_id=1, source_target_pairs={{0,3},{1,2},{2,1},{3,0},{4,7},{5,6},{6,5},{7,4},{8,11},{9,10},{10,... | collective-permute-start | bytes 3080 | tf_op jit(solution)/shard_map/ppermute | solution.py:362
  120.4 7.2 %collective-permute-start.20 = (f32[2,1,128]{2,1,0:T(1,128)S(1)}, f32[2,1,128]{2,1,0:T(1,128)S(1)}, u32[]{:S(2)}, u32[]{:S(2)}) collective-permute-start(f32[2,1,128]{2,1,0:T(1,128)S(1)} %add_add_fusion.1), channel_id=1, source_target_pairs={{0,4},{1,5},{2,6},{3,7},{4,0},{5,1},{6,2},{7,3},{8,12},{9,13},{10,... | collective-permute-start | bytes 3080 | tf_op jit(solution)/shard_map/ppermute | solution.py:362
  122.5 7.5 %collective-permute-start.21 = (f32[2,1,128]{2,1,0:T(1,128)S(1)}, f32[2,1,128]{2,1,0:T(1,128)S(1)}, u32[]{:S(2)}, u32[]{:S(2)}) collective-permute-start(f32[2,1,128]{2,1,0:T(1,128)S(1)} %add_add_fusion.1), channel_id=1, source_target_pairs={{0,8},{1,9},{2,10},{3,11},{4,12},{5,13},{6,14},{7,15},{8,0},{9,1},... | collective-permute-start | bytes 3080 | tf_op jit(solution)/shard_map/ppermute | solution.py:362
  124.5 5.7 %collective-permute-start.22 = (f32[2,1,128]{2,1,0:T(1,128)S(1)}, f32[2,1,128]{2,1,0:T(1,128)S(1)}, u32[]{:S(2)}, u32[]{:S(2)}) collective-permute-start(f32[2,1,128]{2,1,0:T(1,128)S(1)} %add_add_fusion.1), channel_id=1, source_target_pairs={{0,12},{1,13},{2,14},{3,15},{4,8},{5,9},{6,10},{7,11},{8,4},{9,5},... | collective-permute-start | bytes 3080 | tf_op jit(solution)/shard_map/ppermute | solution.py:362
Sparse Core Ops, SparseCore 0:
  33.1 70.2 all-gather.2

commit v4 on v3

--- a/solution.py
+++ b/solution.py
@@ -11,6 +11,8 @@
 EXTRA = 16
 TOGETHER = 4
 LEAST = 1e-33
+CHUNK = 256
+ROUND = 12582912.0
 PARAMS = pltpu.CompilerParams(vmem_limit_bytes=56 * 1024 * 1024)
 LESS = pltpu.CompilerParams(vmem_limit_bytes=28 * 1024 * 1024)
 RAW = ((0, 64), (64, 32))
@@ -49,7 +51,7 @@
 
 def coded(values, top):
     exponent = jnp.ceil(jnp.log2(jnp.maximum(top, LEAST)) - 14.99)
-    return jnp.round(values * jnp.exp2(-exponent)), exponent
+    return (values * jnp.exp2(-exponent) + ROUND) - ROUND, exponent
 
 
 def narrow(units):
@@ -108,21 +110,26 @@
         for copy in copies(1):
             copy.wait()
 
-    product = jnp.dot(grads[example], acts[example], preferred_element_type=jnp.float32)
-    squares_ref[0] = lane_sums(product)
+    columns = grads.shape[1]
+    squares = jnp.zeros((1, LANES), jnp.float32)
     at = row = 0
     for h, (_, width) in enumerate(RAW):
         together = LANES // width
-        rows = product.shape[0] // together
+        rows = columns // together
         for tile in range(coded_ref.shape[0] // together):
-            tile_values = product[:, at : at + LANES]
-            units, exponent = coded(tile_values, tops(tile_values))
+            if at % CHUNK == 0:
+                some = acts[example, :, at : at + CHUNK]
+                product = jnp.dot(grads[example], some, preferred_element_type=jnp.float32)
+                squares = squares + lane_sums(product)
+            values = product[:, at % CHUNK : at % CHUNK + LANES]
+            units, exponent = coded(values, tops(values))
             exponents = packed_row(exponent, together)
             for k, block in enumerate(packed(units, together)):
                 coded_ref[tile * together + k, 0, row : row + rows] = narrow(block)
                 exponent_ref[tile * together + k, 0, h : h + 1] = exponents[k]
             at += LANES
         row += rows
+    squares_ref[0] = squares
 
 
 def raw_products(order, pieces, grads):
@@ -181,17 +188,21 @@
             acts_copy(step).wait()
             if step % tiles == 0:
                 grads_copy(step // tiles).wait()
-            rows = acts[step % 2].reshape(devices * shard, width)
-            product_ref[0] = jnp.dot(grads[step // tiles], rows, preferred_element_type=jnp.float32)
-
-    product = product_ref[0]
-    top_ref[0] = tops(product)
 
     @pl.when(tile == 0)
     def _():
         share_ref[...] = squares_ref[...]
 
-    share_ref[0] += lane_sums(product)
+    slot = (example * tiles + tile) % 2
+    share = share_ref[0]
+    for at in range(0, width, CHUNK):
+        here = slice(at, at + CHUNK)
+        some = acts[slot, :, :, here].reshape(devices * shard, CHUNK)
+        product = jnp.dot(grads[example], some, preferred_element_type=jnp.float32)
+        product_ref[0, :, here] = product
+        top_ref[0, :, here] = tops(product)
+        share = share + lane_sums(product)
+    share_ref[0] = share
 
 
 def plain_products(acts, grads, squares):

time: 187 us -> 186 us (level)
  no operation moved by 1% of the time
where the time goes in v4:
time: 186 us; the launch traced here: 185 us
  waiting for transfers between devices  60.3 us (32%)
  blocking collectives  40.7 us (22%)
  Pallas kernels  33.1 us (18%)
  starting transfers between devices  28.9 us (16%)
  between operations  14.3 us (8%)
  local copies, waits for them, and re-layouts  4.54 us (2%)
  other arithmetic  3.44 us (2%)
    all_to_all x1, blocking collectives, per_device(): clipped = lax.all_to_all(clipped, 'dp', 0, 0)  40.7 us
    ppermute x8, waiting for transfers between devices, along_z(): lax.ppermute(x, 'tensor', [(t, (t + 2 * k) % devices) for t in range(devi...  29.8 us
    all_gather x1, waiting for transfers between devices, per_device(): second = lax.all_gather(second, 'tensor')  23.5 us
    ppermute x8, starting transfers between devices, along_z(): lax.ppermute(x, 'tensor', [(t, (t + 2 * k) % devices) for t in range(devi...  11.4 us
    ppermute x15, starting transfers between devices, crossed(): return lax.ppermute(x, 'tensor', [(t, t ^ k) for t in range(devices)])  10.3 us
    pallas_call x1, Pallas kernels, raw_products(): pl.pallas_call(raw_kernel, grid=(examples,), in_specs=[pl.BlockSpec(memor...  10.2 us
    pallas_call x1, Pallas kernels, plain_products(): pl.pallas_call(plain_kernel, grid=(examples, features // width), in_specs...  9.82 us
    all_to_all x1, starting transfers between devices, per_device(): raw = lax.all_to_all(raw, 'dp', 0, 0)  7.12 us
  transfers between devices with their start and end apart: 25, of which 13 were waited for; matrix products, arithmetic and copies ran while one was open for 3% of the time, Pallas kernels for 14%

profile of v4, /device:TPU:32, one launch (start us, length us, event | category | flops | bytes accessed | tf_op | source)
XLA Modules:
  0.0 185.2 jit_solution(8227108431052123141)
XLA Ops:
  6.5 2.0 %shard_map.73 = bf16[128,1536]{1,0:T(8,128)(2,1)} custom-call(bf16[128,4096]{1,0:T(8,128)(2,1)} %bitcast.7), custom_call_target="tpu_custom_call" | custom-call | tf_op jit(solution)/shard_map/pallas_call | solution.py:38
  8.6 1.9 %collective-permute-start = (bf16[2,64,1536]{2,1,0:T(8,128)(2,1)}, bf16[2,64,1536]{2,1,0:T(8,128)(2,1)S(1)}, u32[]{:S(2)}, u32[]{:S(2)}) collective-permute-start(bf16[2,64,1536]{2,1,0:T(8,128)(2,1)} %bitcast.10), channel_id=1, source_target_pairs={{0,2},{1,3},{2,4},{3,5},{4,6},{5,7},{6,8},{7,9},{8,10},{9,11},{10,... | collective-permute-start | bytes 1179656 | tf_op jit(solution)/shard_map/ppermute | solution.py:370
  10.5 0.1 collective-permute-start.2
  10.6 0.7 iota_compare_fusion
  11.3 8.3 %collective-permute-done.refs_2_ = bf16[2,64,1536]{2,1,0:T(8,128)(2,1)S(1)} collective-permute-done((bf16[2,64,1536]{2,1,0:T(8,128)(2,1)}, bf16[2,64,1536]{2,1,0:T(8,128)(2,1)S(1)}, u32[]{:S(2)}, u32[]{:S(2)}) %collective-permute-start) | collective-permute-done | bytes 393248 | tf_op jit(solution)/shard_map/ppermute | solution.py:370
  19.6 1.9 %collective-permute-start.1 = (bf16[2,64,1536]{2,1,0:T(8,128)(2,1)S(1)}, bf16[2,64,1536]{2,1,0:T(8,128)(2,1)}, u32[]{:S(2)}, u32[]{:S(2)}) collective-permute-start(bf16[2,64,1536]{2,1,0:T(8,128)(2,1)S(1)} %collective-permute-done.refs_2_), channel_id=1, source_target_pairs={{0,2},{1,3},{2,4},{3,5},{4,6},{5,7},{6,8},{7,9},{8,10},{9,11},{10,... | collective-permute-start | bytes 1179656 | tf_op jit(solution)/shard_map/ppermute | solution.py:370
  21.6 0.0 collective-permute-done.2.refs_4_
  21.6 2.4 %collective-permute-start.3 = (bf16[2,64,1536]{2,1,0:T(8,128)(2,1)S(1)}, bf16[2,64,1536]{2,1,0:T(8,128)(2,1)}, u32[]{:S(2)}, u32[]{:S(2)}) collective-permute-start(bf16[2,64,1536]{2,1,0:T(8,128)(2,1)S(1)} %collective-permute-done.2.refs_4_), channel_id=1, source_target_pairs={{0,14},{1,15},{2,0},{3,1},{4,2},{5,3},{6,4},{7,5},{8,6},{9,7},{10,... | collective-permute-start | bytes 1179656 | tf_op jit(solution)/shard_map/ppermute | solution.py:370
  24.0 1.2 add_and_fusion.order_ref
  25.2 2.0 %shard_map.74 = bf16[128,2560]{1,0:T(8,128)(2,1)} custom-call(bf16[128,4096]{1,0:T(8,128)(2,1)} %bitcast.8), custom_call_target="tpu_custom_call" | custom-call | tf_op jit(solution)/shard_map/pallas_call | solution.py:38
  27.2 3.0 %copy.9 = bf16[2,1024,512]{1,2,0:T(8,128)(2,1)S(1)} copy(bf16[2,1024,512]{2,1,0:T(8,128)(2,1)} %param.8) | data formatting | bytes 4194304 | tf_op args[1]
  30.2 0.0 copy-start.1
  30.2 1.5 select_bitcast_fusion.refs_18_.grads_ref
  31.7 0.8 collective-permute-done.1.refs_6_
  32.5 0.4 collective-permute-done.3.refs_8_
  33.0 0.0 all-gather.3.cloned.1.call-update
  33.0 3.0 %collective-permute-start.9 = (bf16[2,64,1536]{2,1,0:T(8,128)(2,1)}, bf16[2,64,1536]{2,1,0:T(8,128)(2,1)S(1)}, u32[]{:S(2)}, u32[]{:S(2)}) collective-permute-start(bf16[2,64,1536]{2,1,0:T(8,128)(2,1)} %collective-permute-done.1.refs_6_), channel_id=1, source_target_pairs={{0,2},{1,3},{2,4},{3,5},{4,6},{5,7},{6,8},{7,9},{8,10},{9,11},{10,... | collective-permute-start | bytes 1179656 | tf_op jit(solution)/shard_map/ppermute | solution.py:370
  36.0 0.5 collective-permute-start.5
  36.5 0.1 collective-permute-start.6
  36.6 6.8 %collective-permute-done.9.refs_10_ = bf16[2,64,1536]{2,1,0:T(8,128)(2,1)S(1)} collective-permute-done((bf16[2,64,1536]{2,1,0:T(8,128)(2,1)}, bf16[2,64,1536]{2,1,0:T(8,128)(2,1)S(1)}, u32[]{:S(2)}, u32[]{:S(2)}) %collective-permute-start.9) | collective-permute-done | bytes 393248 | tf_op jit(solution)/shard_map/ppermute | solution.py:370
  43.5 2.5 %collective-permute-done.11.refs_12_ = bf16[2,64,1536]{2,1,0:T(8,128)(2,1)S(1)} collective-permute-done((bf16[2,64,1536]{2,1,0:T(8,128)(2,1)}, bf16[2,64,1536]{2,1,0:T(8,128)(2,1)S(1)}, u32[]{:S(2)}, u32[]{:S(2)}) %collective-permute-start.11) | collective-permute-done | bytes 393248 | tf_op jit(solution)/shard_map/ppermute | solution.py:370
  46.0 1.8 collective-permute-start.13
  47.8 0.3 collective-permute-start.15
  48.1 0.1 collective-permute-start.10
  48.1 0.5 collective-permute-start.12
  48.6 9.2 %collective-permute-done.13.refs_14_ = bf16[1,64,1536]{2,1,0:T(8,128)(2,1)S(1)} collective-permute-done((bf16[1,64,1536]{2,1,0:T(8,128)(2,1)S(1)}, bf16[1,64,1536]{2,1,0:T(8,128)(2,1)S(1)}, u32[]{:S(2)}, u32[]{:S(2)}) %collective-permute-start.13) | collective-permute-done | bytes 196640 | tf_op jit(solution)/shard_map/ppermute | solution.py:370
  57.8 1.7 collective-permute-done.15.refs_16_
  59.5 0.0 collective-permute-start.16
  59.6 1.4 collective-permute-done.16.refs_17_
  61.1 0.6 copy-done.16
  61.6 0.2 copy-done.11
  61.8 0.7 copy-done.12
  62.5 10.2 %shard_map.75 = (s16[16,2,384,128]{3,2,1,0:T(8,128)(2,1)}, f32[16,2,8,128]{3,2,1,0:T(8,128)}, f32[2,1,128]{2,1,0:T(1,128)}) custom-call(s32[16]{0:T(128)} %add_and_fusion.order_ref, bf16[2,64,1536]{2,1,0:T(8,128)(2,1)} %bitcast.12, bf16[2,64,1536]{2,1,0:T(8,128)(2,1)} %copy-done.6, bf16[2,64,1536]{2,1,0:T(8,128)(2,1)} %copy-done.4, ...), custom_call_target="tpu_custom_call" | custom-call | tf_op jit(solution)/shard_map/pallas_call | solution.py:140
  72.7 7.1 %all-to-all-start = ((s16[16,2,384,128]{3,2,1,0:T(8,128)(2,1)}), s16[16,2,384,128]{3,2,1,0:T(8,128)(2,1)}, u32[]{:S(2)}, u32[]{:S(2)}) async-start(s16[16,2,384,128]{3,2,1,0:T(8,128)(2,1)} %get-tuple-element.28), calls=%async_computation | async-start | bytes 6291456 | tf_op jit(solution)/shard_map/all_to_all | solution.py:397
  79.9 23.5 %all-gather.3.cloned.1.call-done = bf16[32,64,2560]{2,1,0:T(8,128)(2,1)} async-done(((bf16[2,64,2560]{2,1,0:T(8,128)(2,1)}), bf16[32,64,2560]{2,1,0:T(8,128)(2,1)}) %all-gather.3.cloned.1.call-update) | async-done | bytes 10485776 | tf_op jit(solution)/shard_map/all_gather | solution.py:388
  103.4 9.8 %shard_map.76 = (f32[2,512,2560]{2,1,0:T(8,128)S(1)}, f32[2,1,2560]{2,1,0:T(1,128)S(1)}, f32[2,1,128]{2,1,0:T(1,128)S(1)}) custom-call(bf16[16,2,64,2560]{3,2,1,0:T(8,128)(2,1)} %bitcast.6, bf16[2,512,1024]{2,1,0:T(8,128)(2,1)} %select_bitcast_fusion.refs_18_.grads_ref, f32[2,1,128]{2,1,0:T(1,128)} %get-tuple-element.23.squares_ref), custom_call_target="tpu_custom_call" | custom-call | flops 1 | bytes 1 | tf_op jit(solution)/shard_map/pallas_call | solution.py:214
  113.2 0.3 collective-permute-start.17
  113.5 2.3 %collective-permute-start.18 = (f32[2,1,128]{2,1,0:T(1,128)S(1)}, f32[2,1,128]{2,1,0:T(1,128)S(1)}, u32[]{:S(2)}, u32[]{:S(2)}) collective-permute-start(f32[2,1,128]{2,1,0:T(1,128)S(1)} %get-tuple-element.24), channel_id=1, source_target_pairs={{0,2},{1,3},{2,0},{3,1},{4,6},{5,7},{6,4},{7,5},{8,10},{9,11},{10,... | collective-permute-start | bytes 3080 | tf_op jit(solution)/shard_map/ppermute | solution.py:373
  115.9 1.5 collective-permute-done.18
  117.4 1.4 collective-permute-done.19
  118.9 2.1 %collective-permute-start.20 = (f32[2,1,128]{2,1,0:T(1,128)S(1)}, f32[2,1,128]{2,1,0:T(1,128)S(1)}, u32[]{:S(2)}, u32[]{:S(2)}) collective-permute-start(f32[2,1,128]{2,1,0:T(1,128)S(1)} %add_add_fusion.1), channel_id=1, source_target_pairs={{0,4},{1,5},{2,6},{3,7},{4,0},{5,1},{6,2},{7,3},{8,12},{9,13},{10,... | collective-permute-start | bytes 3080 | tf_op jit(solution)/shard_map/ppermute | solution.py:373
  121.0 2.0 %collective-permute-start.21 = (f32[2,1,128]{2,1,0:T(1,128)S(1)}, f32[2,1,128]{2,1,0:T(1,128)S(1)}, u32[]{:S(2)}, u32[]{:S(2)}) collective-permute-start(f32[2,1,128]{2,1,0:T(1,128)S(1)} %add_add_fusion.1), channel_id=1, source_target_pairs={{0,8},{1,9},{2,10},{3,11},{4,12},{5,13},{6,14},{7,15},{8,0},{9,1},... | collective-permute-start | bytes 3080 | tf_op jit(solution)/shard_map/ppermute | solution.py:373
  123.0 2.4 %collective-permute-start.22 = (f32[2,1,128]{2,1,0:T(1,128)S(1)}, f32[2,1,128]{2,1,0:T(1,128)S(1)}, u32[]{:S(2)}, u32[]{:S(2)}) collective-permute-start(f32[2,1,128]{2,1,0:T(1,128)S(1)} %add_add_fusion.1), channel_id=1, source_target_pairs={{0,12},{1,13},{2,14},{3,15},{4,8},{5,9},{6,10},{7,11},{8,4},{9,5},... | collective-permute-start | bytes 3080 | tf_op jit(solution)/shard_map/ppermute | solution.py:373
  126.1 2.4 %collective-permute-done.21 = f32[2,1,128]{2,1,0:T(1,128)S(1)} collective-permute-done((f32[2,1,128]{2,1,0:T(1,128)S(1)}, f32[2,1,128]{2,1,0:T(1,128)S(1)}, u32[]{:S(2)}, u32[]{:S(2)}) %collective-permute-start.21) | collective-permute-done | bytes 1056 | tf_op jit(solution)/shard_map/ppermute | solution.py:373
  128.4 0.2 collective-permute-done.22
  128.6 3.8 %shard_map.77 = s16[16,656,128]{2,1,0:T(8,128)(2,1)S(1)} custom-call(f32[1]{0:T(128)S(6)} %copy.10.clip_ref, f32[2,1,128]{2,1,0:T(1,128)S(1)} %add_add_fusion.shares_ref, f32[2,512,2560]{2,1,0:T(8,128)S(1)} %get-tuple-element.25.wide_ref.thin_ref, f32[2,512,2560]{2,1,0:T(8,128)S(1)} %get-tuple-element.25.wide_ref.thin_ref, ...), custom_call_target="tpu_custom_call" | custom-call | flops 1 | bytes 1 | tf_op jit(solution)/shard_map/pallas_call | solution.py:276
  132.5 40.7 %all_to_all.10.clipped_ref = s16[16,656,128]{2,1,0:T(8,128)(2,1)} all-to-all(s16[16,656,128]{2,1,0:T(8,128)(2,1)S(1)} %shard_map.77), channel_id=1, replica_groups=mesh['dp'=16,'tensor'=16] {'dp'}, dimensions={0} | all-to-all | bytes 5373952 | tf_op jit(solution)/shard_map/all_to_all | solution.py:403
  173.2 5.2 %shard_map.78 = f32[256,512]{1,0:T(8,128)} custom-call(s16[16,2,384,128]{3,2,1,0:T(8,128)(2,1)} %all-to-all-done.raw_ref, s16[16,656,128]{2,1,0:T(8,128)(2,1)} %all_to_all.10.clipped_ref, f32[256,512]{1,0:T(8,128)} %noise_ref.1), custom_call_target="tpu_custom_call" | custom-call | tf_op jit(solution)/shard_map/pallas_call | solution.py:348
  (52 shorter events, 0.1 us)
Async XLA Ops:
  6.5 96.8 %all-gather.3.cloned.1.call-start = ((), (), s32[]{:S(2)}) async-start(), calls=%async_computation.2 | async-start | bytes 11141120 | tf_op jit(solution)/shard_map/all_gather | solution.py:388
  8.6 11.1 %collective-permute-start = (bf16[2,64,1536]{2,1,0:T(8,128)(2,1)}, bf16[2,64,1536]{2,1,0:T(8,128)(2,1)S(1)}, u32[]{:S(2)}, u32[]{:S(2)}) collective-permute-start(bf16[2,64,1536]{2,1,0:T(8,128)(2,1)} %bitcast.10), channel_id=1, source_target_pairs={{0,2},{1,3},{2,4},{3,5},{4,6},{5,7},{6,8},{7,9},{8,10},{9,11},{10,... | collective-permute-start | bytes 1179656 | tf_op jit(solution)/shard_map/ppermute | solution.py:370
  10.5 11.1 %collective-permute-start.2 = (bf16[2,64,1536]{2,1,0:T(8,128)(2,1)}, bf16[2,64,1536]{2,1,0:T(8,128)(2,1)S(1)}, u32[]{:S(2)}, u32[]{:S(2)}) collective-permute-start(bf16[2,64,1536]{2,1,0:T(8,128)(2,1)} %bitcast.11), channel_id=1, source_target_pairs={{0,14},{1,15},{2,0},{3,1},{4,2},{5,3},{6,4},{7,5},{8,6},{9,7},{10,... | collective-permute-start | bytes 1179656 | tf_op jit(solution)/shard_map/ppermute | solution.py:370
  19.6 16.4 %copy-start.4 = (bf16[2,64,1536]{2,1,0:T(8,128)(2,1)}, bf16[2,64,1536]{2,1,0:T(8,128)(2,1)S(1)}, u32[]{:S(2)}) copy-start(bf16[2,64,1536]{2,1,0:T(8,128)(2,1)S(1)} %collective-permute-done.refs_2_) | copy-start | bytes 1179652
  19.6 12.9 %collective-permute-start.1 = (bf16[2,64,1536]{2,1,0:T(8,128)(2,1)S(1)}, bf16[2,64,1536]{2,1,0:T(8,128)(2,1)}, u32[]{:S(2)}, u32[]{:S(2)}) collective-permute-start(bf16[2,64,1536]{2,1,0:T(8,128)(2,1)S(1)} %collective-permute-done.refs_2_), channel_id=1, source_target_pairs={{0,2},{1,3},{2,4},{3,5},{4,6},{5,7},{6,8},{7,9},{8,10},{9,11},{10,... | collective-permute-start | bytes 1179656 | tf_op jit(solution)/shard_map/ppermute | solution.py:370
  21.6 14.9 %copy-start.5 = (bf16[2,64,1536]{2,1,0:T(8,128)(2,1)}, bf16[2,64,1536]{2,1,0:T(8,128)(2,1)S(1)}, u32[]{:S(2)}) copy-start(bf16[2,64,1536]{2,1,0:T(8,128)(2,1)S(1)} %collective-permute-done.2.refs_4_) | copy-start | bytes 1179652
  21.6 11.4 %collective-permute-start.3 = (bf16[2,64,1536]{2,1,0:T(8,128)(2,1)S(1)}, bf16[2,64,1536]{2,1,0:T(8,128)(2,1)}, u32[]{:S(2)}, u32[]{:S(2)}) collective-permute-start(bf16[2,64,1536]{2,1,0:T(8,128)(2,1)S(1)} %collective-permute-done.2.refs_4_), channel_id=1, source_target_pairs={{0,14},{1,15},{2,0},{3,1},{4,2},{5,3},{6,4},{7,5},{8,6},{9,7},{10,... | collective-permute-start | bytes 1179656 | tf_op jit(solution)/shard_map/ppermute | solution.py:370
  30.2 5.8 %copy-start.1 = (bf16[128,1536]{1,0:T(8,128)(2,1)S(1)}, bf16[128,1536]{1,0:T(8,128)(2,1)}, u32[]{:S(2)}) copy-start(bf16[128,1536]{1,0:T(8,128)(2,1)} %shard_map.73) | copy-start | bytes 1179652
  33.0 10.5 %collective-permute-start.9 = (bf16[2,64,1536]{2,1,0:T(8,128)(2,1)}, bf16[2,64,1536]{2,1,0:T(8,128)(2,1)S(1)}, u32[]{:S(2)}, u32[]{:S(2)}) collective-permute-start(bf16[2,64,1536]{2,1,0:T(8,128)(2,1)} %collective-permute-done.1.refs_6_), channel_id=1, source_target_pairs={{0,2},{1,3},{2,4},{3,5},{4,6},{5,7},{6,8},{7,9},{8,10},{9,11},{10,... | collective-permute-start | bytes 1179656 | tf_op jit(solution)/shard_map/ppermute | solution.py:370
  36.0 9.9 %collective-permute-start.11 = (bf16[2,64,1536]{2,1,0:T(8,128)(2,1)}, bf16[2,64,1536]{2,1,0:T(8,128)(2,1)S(1)}, u32[]{:S(2)}, u32[]{:S(2)}) collective-permute-start(bf16[2,64,1536]{2,1,0:T(8,128)(2,1)} %collective-permute-done.3.refs_8_), channel_id=1, source_target_pairs={{0,14},{1,15},{2,0},{3,1},{4,2},{5,3},{6,4},{7,5},{8,6},{9,7},{10,... | collective-permute-start | bytes 1179656 | tf_op jit(solution)/shard_map/ppermute | solution.py:370
  36.0 9.9 %collective-permute-start.4 = (bf16[2,64,1536]{2,1,0:T(8,128)(2,1)S(1)}, bf16[2,64,1536]{2,1,0:T(8,128)(2,1)S(1)}, u32[]{:S(2)}, u32[]{:S(2)}) collective-permute-start(bf16[2,64,1536]{2,1,0:T(8,128)(2,1)S(1)} %bitcast.13), channel_id=1, source_target_pairs={{0,1},{1,0},{2,3},{3,2},{4,5},{5,4},{6,7},{7,6},{8,9},{9,8},{10,11... | collective-permute-start | bytes 1179656 | tf_op jit(solution)/shard_map/ppermute | solution.py:373
  36.0 11.8 %collective-permute-start.5 = (bf16[2,64,1536]{2,1,0:T(8,128)(2,1)S(1)}, bf16[2,64,1536]{2,1,0:T(8,128)(2,1)S(1)}, u32[]{:S(2)}, u32[]{:S(2)}) collective-permute-start(bf16[2,64,1536]{2,1,0:T(8,128)(2,1)S(1)} %collective-permute-done.refs_2_), channel_id=1, source_target_pairs={{0,1},{1,0},{2,3},{3,2},{4,5},{5,4},{6,7},{7,6},{8,9},{9,8},{10,11... | collective-permute-start | bytes 1179656 | tf_op jit(solution)/shard_map/ppermute | solution.py:373
  36.5 11.6 %collective-permute-start.6 = (bf16[2,64,1536]{2,1,0:T(8,128)(2,1)S(1)}, bf16[2,64,1536]{2,1,0:T(8,128)(2,1)S(1)}, u32[]{:S(2)}, u32[]{:S(2)}) collective-permute-start(bf16[2,64,1536]{2,1,0:T(8,128)(2,1)S(1)} %collective-permute-done.2.refs_4_), channel_id=1, source_target_pairs={{0,1},{1,0},{2,3},{3,2},{4,5},{5,4},{6,7},{7,6},{8,9},{9,8},{10,11... | collective-permute-start | bytes 1179656 | tf_op jit(solution)/shard_map/ppermute | solution.py:373
  43.4 17.5 %copy-start.2 = (bf16[2,64,1536]{2,1,0:T(8,128)(2,1)}, bf16[2,64,1536]{2,1,0:T(8,128)(2,1)S(1)}, u32[]{:S(2)}) copy-start(bf16[2,64,1536]{2,1,0:T(8,128)(2,1)S(1)} %collective-permute-done.9.refs_10_) | copy-start | bytes 1179652
  43.4 4.7 %collective-permute-start.7 = (bf16[2,64,1536]{2,1,0:T(8,128)(2,1)}, bf16[2,64,1536]{2,1,0:T(8,128)(2,1)S(1)}, u32[]{:S(2)}, u32[]{:S(2)}) collective-permute-start(bf16[2,64,1536]{2,1,0:T(8,128)(2,1)} %collective-permute-done.1.refs_6_), channel_id=1, source_target_pairs={{0,1},{1,0},{2,3},{3,2},{4,5},{5,4},{6,7},{7,6},{8,9},{9,8},{10,11... | collective-permute-start | bytes 1179656 | tf_op jit(solution)/shard_map/ppermute | solution.py:373
  45.9 15.1 %copy-start.3 = (bf16[2,64,1536]{2,1,0:T(8,128)(2,1)}, bf16[2,64,1536]{2,1,0:T(8,128)(2,1)S(1)}, u32[]{:S(2)}) copy-start(bf16[2,64,1536]{2,1,0:T(8,128)(2,1)S(1)} %collective-permute-done.11.refs_12_) | copy-start | bytes 1179652
  45.9 13.6 %collective-permute-start.8 = (bf16[2,64,1536]{2,1,0:T(8,128)(2,1)}, bf16[2,64,1536]{2,1,0:T(8,128)(2,1)S(1)}, u32[]{:S(2)}, u32[]{:S(2)}) collective-permute-start(bf16[2,64,1536]{2,1,0:T(8,128)(2,1)} %collective-permute-done.3.refs_8_), channel_id=1, source_target_pairs={{0,1},{1,0},{2,3},{3,2},{4,5},{5,4},{6,7},{7,6},{8,9},{9,8},{10,11... | collective-permute-start | bytes 1179656 | tf_op jit(solution)/shard_map/ppermute | solution.py:373
  46.0 15.0 %copy-start.6 = (bf16[2,64,1536]{2,1,0:T(8,128)(2,1)}, bf16[2,64,1536]{2,1,0:T(8,128)(2,1)S(1)}, u32[]{:S(2)}) copy-start(bf16[2,64,1536]{2,1,0:T(8,128)(2,1)S(1)} %collective-permute-done.4.refs_1_) | copy-start | bytes 1179652
  46.0 11.8 %collective-permute-start.13 = (bf16[1,64,1536]{2,1,0:T(8,128)(2,1)S(1)}, bf16[1,64,1536]{2,1,0:T(8,128)(2,1)S(1)}, u32[]{:S(2)}, u32[]{:S(2)}) collective-permute-start(bf16[1,64,1536]{2,1,0:T(8,128)(2,1)S(1)} %slice.8), channel_id=1, source_target_pairs={{0,2},{1,3},{2,4},{3,5},{4,6},{5,7},{6,8},{7,9},{8,10},{9,11},{10,... | collective-permute-start | bytes 589832 | tf_op jit(solution)/shard_map/ppermute | solution.py:370
  47.8 13.2 %copy-start.7 = (bf16[2,64,1536]{2,1,0:T(8,128)(2,1)}, bf16[2,64,1536]{2,1,0:T(8,128)(2,1)S(1)}, u32[]{:S(2)}) copy-start(bf16[2,64,1536]{2,1,0:T(8,128)(2,1)S(1)} %collective-permute-done.5.refs_3_) | copy-start | bytes 1179652
  47.8 11.7 %collective-permute-start.15 = (bf16[1,64,1536]{2,1,0:T(8,128)(2,1)S(1)}, bf16[1,64,1536]{2,1,0:T(8,128)(2,1)S(1)}, u32[]{:S(2)}, u32[]{:S(2)}) collective-permute-start(bf16[1,64,1536]{2,1,0:T(8,128)(2,1)S(1)} %slice.9), channel_id=1, source_target_pairs={{0,14},{1,15},{2,0},{3,1},{4,2},{5,3},{6,4},{7,5},{8,6},{9,7},{10,... | collective-permute-start | bytes 589832 | tf_op jit(solution)/shard_map/ppermute | solution.py:370
  48.1 12.9 %copy-start.8 = (bf16[2,64,1536]{2,1,0:T(8,128)(2,1)}, bf16[2,64,1536]{2,1,0:T(8,128)(2,1)S(1)}, u32[]{:S(2)}) copy-start(bf16[2,64,1536]{2,1,0:T(8,128)(2,1)S(1)} %collective-permute-done.6.refs_5_) | copy-start | bytes 1179652
  48.1 12.9 %collective-permute-start.10 = (bf16[2,64,1536]{2,1,0:T(8,128)(2,1)S(1)}, bf16[2,64,1536]{2,1,0:T(8,128)(2,1)S(1)}, u32[]{:S(2)}, u32[]{:S(2)}) collective-permute-start(bf16[2,64,1536]{2,1,0:T(8,128)(2,1)S(1)} %collective-permute-done.9.refs_10_), channel_id=1, source_target_pairs={{0,1},{1,0},{2,3},{3,2},{4,5},{5,4},{6,7},{7,6},{8,9},{9,8},{10,11... | collective-permute-start | bytes 1179656 | tf_op jit(solution)/shard_map/ppermute | solution.py:373
  48.1 12.9 %copy-start.9 = (bf16[2,64,1536]{2,1,0:T(8,128)(2,1)}, bf16[2,64,1536]{2,1,0:T(8,128)(2,1)S(1)}, u32[]{:S(2)}) copy-start(bf16[2,64,1536]{2,1,0:T(8,128)(2,1)S(1)} %collective-permute-done.7.refs_7_) | copy-start | bytes 1179652
  48.1 12.8 %collective-permute-start.12 = (bf16[2,64,1536]{2,1,0:T(8,128)(2,1)S(1)}, bf16[2,64,1536]{2,1,0:T(8,128)(2,1)S(1)}, u32[]{:S(2)}, u32[]{:S(2)}) collective-permute-start(bf16[2,64,1536]{2,1,0:T(8,128)(2,1)S(1)} %collective-permute-done.11.refs_12_), channel_id=1, source_target_pairs={{0,1},{1,0},{2,3},{3,2},{4,5},{5,4},{6,7},{7,6},{8,9},{9,8},{10,11... | collective-permute-start | bytes 1179656 | tf_op jit(solution)/shard_map/ppermute | solution.py:373
  57.8 3.2 %copy-start.13 = (bf16[1,64,1536]{2,1,0:T(8,128)(2,1)}, bf16[1,64,1536]{2,1,0:T(8,128)(2,1)S(1)}, u32[]{:S(2)}) copy-start(bf16[1,64,1536]{2,1,0:T(8,128)(2,1)S(1)} %collective-permute-done.13.refs_14_) | copy-start | bytes 589828
  57.8 1.7 collective-permute-start.14
  59.5 1.5 copy-start.14
  59.5 1.4 collective-permute-start.16
  59.5 1.5 copy-start.10
  59.6 1.5 copy-start.15
  61.0 0.7 copy-start.16
  61.0 0.8 copy-start.11
  61.8 0.7 copy-start.12
  72.7 59.7 %all-to-all-start = ((s16[16,2,384,128]{3,2,1,0:T(8,128)(2,1)}), s16[16,2,384,128]{3,2,1,0:T(8,128)(2,1)}, u32[]{:S(2)}, u32[]{:S(2)}) async-start(s16[16,2,384,128]{3,2,1,0:T(8,128)(2,1)} %get-tuple-element.28), calls=%async_computation | async-start | bytes 6291456 | tf_op jit(solution)/shard_map/all_to_all | solution.py:397
  103.4 25.3 %copy-start = (f32[16,2,8,128]{3,2,1,0:T(8,128)S(1)}, f32[16,2,8,128]{3,2,1,0:T(8,128)}, u32[]{:S(2)}) copy-start(f32[16,2,8,128]{3,2,1,0:T(8,128)} %get-tuple-element.27.exponent_ref) | copy-start | bytes 393220
  113.2 2.7 %collective-permute-start.17 = (f32[2,1,128]{2,1,0:T(1,128)S(1)}, f32[2,1,128]{2,1,0:T(1,128)S(1)}, u32[]{:S(2)}, u32[]{:S(2)}) collective-permute-start(f32[2,1,128]{2,1,0:T(1,128)S(1)} %get-tuple-element.24), channel_id=1, source_target_pairs={{0,1},{1,0},{2,3},{3,2},{4,5},{5,4},{6,7},{7,6},{8,9},{9,8},{10,11... | collective-permute-start | bytes 3080 | tf_op jit(solution)/shard_map/ppermute | solution.py:373
  113.5 3.9 %collective-permute-start.18 = (f32[2,1,128]{2,1,0:T(1,128)S(1)}, f32[2,1,128]{2,1,0:T(1,128)S(1)}, u32[]{:S(2)}, u32[]{:S(2)}) collective-permute-start(f32[2,1,128]{2,1,0:T(1,128)S(1)} %get-tuple-element.24), channel_id=1, source_target_pairs={{0,2},{1,3},{2,0},{3,1},{4,6},{5,7},{6,4},{7,5},{8,10},{9,11},{10,... | collective-permute-start | bytes 3080 | tf_op jit(solution)/shard_map/ppermute | solution.py:373
  115.9 3.0 %collective-permute-start.19 = (f32[2,1,128]{2,1,0:T(1,128)S(1)}, f32[2,1,128]{2,1,0:T(1,128)S(1)}, u32[]{:S(2)}, u32[]{:S(2)}) collective-permute-start(f32[2,1,128]{2,1,0:T(1,128)S(1)} %get-tuple-element.24), channel_id=1, source_target_pairs={{0,3},{1,2},{2,1},{3,0},{4,7},{5,6},{6,5},{7,4},{8,11},{9,10},{10,... | collective-permute-start | bytes 3080 | tf_op jit(solution)/shard_map/ppermute | solution.py:373
  118.9 7.2 %collective-permute-start.20 = (f32[2,1,128]{2,1,0:T(1,128)S(1)}, f32[2,1,128]{2,1,0:T(1,128)S(1)}, u32[]{:S(2)}, u32[]{:S(2)}) collective-permute-start(f32[2,1,128]{2,1,0:T(1,128)S(1)} %add_add_fusion.1), channel_id=1, source_target_pairs={{0,4},{1,5},{2,6},{3,7},{4,0},{5,1},{6,2},{7,3},{8,12},{9,13},{10,... | collective-permute-start | bytes 3080 | tf_op jit(solution)/shard_map/ppermute | solution.py:373
  121.0 7.5 %collective-permute-start.21 = (f32[2,1,128]{2,1,0:T(1,128)S(1)}, f32[2,1,128]{2,1,0:T(1,128)S(1)}, u32[]{:S(2)}, u32[]{:S(2)}) collective-permute-start(f32[2,1,128]{2,1,0:T(1,128)S(1)} %add_add_fusion.1), channel_id=1, source_target_pairs={{0,8},{1,9},{2,10},{3,11},{4,12},{5,13},{6,14},{7,15},{8,0},{9,1},... | collective-permute-start | bytes 3080 | tf_op jit(solution)/shard_map/ppermute | solution.py:373
  123.0 5.7 %collective-permute-start.22 = (f32[2,1,128]{2,1,0:T(1,128)S(1)}, f32[2,1,128]{2,1,0:T(1,128)S(1)}, u32[]{:S(2)}, u32[]{:S(2)}) collective-permute-start(f32[2,1,128]{2,1,0:T(1,128)S(1)} %add_add_fusion.1), channel_id=1, source_target_pairs={{0,12},{1,13},{2,14},{3,15},{4,8},{5,9},{6,10},{7,11},{8,4},{9,5},... | collective-permute-start | bytes 3080 | tf_op jit(solution)/shard_map/ppermute | solution.py:373
Sparse Core Ops, SparseCore 0:
  33.1 70.2 all-gather.2

commit v5 on v4

--- a/solution.py
+++ b/solution.py
@@ -12,7 +12,6 @@
 TOGETHER = 4
 LEAST = 1e-33
 CHUNK = 256
-ROUND = 12582912.0
 PARAMS = pltpu.CompilerParams(vmem_limit_bytes=56 * 1024 * 1024)
 LESS = pltpu.CompilerParams(vmem_limit_bytes=28 * 1024 * 1024)
 RAW = ((0, 64), (64, 32))
@@ -51,7 +50,7 @@
 
 def coded(values, top):
     exponent = jnp.ceil(jnp.log2(jnp.maximum(top, LEAST)) - 14.99)
-    return (values * jnp.exp2(-exponent) + ROUND) - ROUND, exponent
+    return jnp.round(values * jnp.exp2(-exponent)), exponent
 
 
 def narrow(units):
@@ -241,14 +240,11 @@
     owners = coded_ref.shape[0]
     clip = clip_ref[0]
     blank = jnp.zeros((1, LANES), jnp.float32)
-    wide, thin, wide_top, thin_top, extra = 0.0, 0.0, 0.0, 0.0, [[] for _ in range(owners)]
+    factors, extra = [], [[] for _ in range(owners)]
     for e in range(examples):
         square = jnp.sum(shares_ref[e], axis=1, keepdims=True)
         factor = clip / jnp.maximum(jnp.sqrt(square), clip)
-        wide = wide + factor * wide_ref[e]
-        thin = thin + factor * thin_ref[e]
-        wide_top = wide_top + factor * wide_top_ref[e]
-        thin_top = thin_top + factor * thin_top_ref[e]
+        factors.append(factor)
         power = jnp.floor(jnp.log2(jnp.maximum(factor, LEAST))) + 1.0
         scaled = factor * jnp.exp2(-power) * 16384.0
         high = jnp.floor(scaled)
@@ -256,14 +252,22 @@
         for k in range(owners):
             extra[k] += [blank + high, blank + low]
             extra[k] += [exponent_ref[k, e, h : h + 1] + power for h in range(len(RAW))]
-    thin_units, exponent = coded(thin, thin_top)
+
+    def added(ref, *at):
+        return sum(factors[e] * ref[(e,) + at] for e in range(examples))
+
+    everything = slice(None)
+    thin_units, exponent = coded(added(thin_ref, everything, everything), added(thin_top_ref, everything, everything))
     thin_units, thin_exponents = packed(thin_units, owners), packed_row(exponent, owners)
     for k in range(owners):
         here = slice(k * LANES, (k + 1) * LANES)
-        units, exponent = coded(wide[:, here], wide_top[:, here])
+        top = added(wide_top_ref, everything, here)
+        for at in range(0, columns, LANES):
+            rows = slice(at, at + LANES)
+            units, exponent = coded(added(wide_ref, rows, here), top)
+            coded_ref[k, rows] = narrow(units)
         rows = extra[k] + [exponent, thin_exponents[k]]
         rows = jnp.concatenate(rows + [blank] * (EXTRA - len(rows)), axis=0)
-        coded_ref[k, :columns] = narrow(units)
         coded_ref[k, columns : coded_ref.shape[1] - EXTRA] = narrow(thin_units[k])
         coded_ref[k, coded_ref.shape[1] - EXTRA :] = narrow(rows)
 
@@ -305,27 +309,28 @@
     kinds = len(RAW)
     bottom = clipped_sum.shape[0]
     extra = [clipped_ref[g, bottom:].astype(jnp.float32) for g in range(TOGETHER)]
+    row = lambda g, k: extra[g][k : k + 1]
     at = 0
     for h, (_, width) in enumerate(RAW):
-        rows = columns * width // LANES
-        total = raw_sum[at : at + rows]
+        weights = []
         for g in range(TOGETHER):
-            row = lambda k: extra[g][k : k + 1]
             for e in range(examples):
                 base = e * (2 + kinds)
-                weight = (row(base) + row(base + 1) * (1.0 / 16384.0)) * (1.0 / 16384.0) * jnp.exp2(row(base + 2 + h))
-                total = total + weight * raw_ref[g, e, at : at + rows].astype(jnp.float32)
-        raw_sum[at : at + rows] = total
-        at += rows
+                weight = (row(g, base) + row(g, base + 1) * (1.0 / 16384.0)) * (1.0 / 16384.0)
+                weights.append((g, e, weight * jnp.exp2(row(g, base + 2 + h))))
+        end = at + columns * width // LANES
+        for block in range(at, end, LANES):
+            rows = slice(block, block + LANES)
+            raw_sum[rows] += sum(w * raw_ref[g, e, rows].astype(jnp.float32) for g, e, w in weights)
+        at = end
     at = 0
     for h, (_, width) in enumerate(CLIPPED):
-        rows = columns * width // LANES
-        total = clipped_sum[at : at + rows]
-        for g in range(TOGETHER):
-            k = examples * (2 + kinds) + h
-            total = total + jnp.exp2(extra[g][k : k + 1]) * clipped_ref[g, at : at + rows].astype(jnp.float32)
-        clipped_sum[at : at + rows] = total
-        at += rows
+        steps = [jnp.exp2(row(g, examples * (2 + kinds) + h)) for g in range(TOGETHER)]
+        end = at + columns * width // LANES
+        for block in range(at, end, LANES):
+            rows = slice(block, block + LANES)
+            clipped_sum[rows] += sum(w * clipped_ref[g, rows].astype(jnp.float32) for g, w in enumerate(steps))
+        at = end
 
     @pl.when(group == pl.num_programs(0) - 1)
     def _():
@@ -373,7 +378,6 @@
         return lax.ppermute(x, "tensor", [(t, t ^ k) for t in range(devices)])
 
     own = part_features(activations, RAW)
-    second = part_features(activations, CLIPPED)
     positions = lax.broadcasted_iota(jnp.int32, (1, out_grads.shape[1], 1), 1)
     masked = jnp.where(positions < lengths[:, None, None], out_grads, jnp.zeros_like(out_grads))
     masked = jnp.swapaxes(masked, 1, 2)
@@ -383,9 +387,10 @@
     order = ((here & ~1) + step + ((here & 1) ^ second_core)) & (devices - 1)
 
     up1, down1 = along_z(own, 1), along_z(own, -1)
+    up1, down1, activations = lax.optimization_barrier((up1, down1, activations))
     up2, down2 = along_z(up1, 1), along_z(down1, -1)
-    up2, down2, second, masked, order = lax.optimization_barrier((up2, down2, second, masked, order))
-    second = lax.all_gather(second, "tensor")
+    second = lax.all_gather(part_features(activations, CLIPPED), "tensor")
+    up2, down2, masked, order = lax.optimization_barrier((up2, down2, masked, order))
     up3, down3 = along_z(up2, 1), along_z(down2, -1)
     up4, down4 = along_z(up3[:1], 1), along_z(down3[1:], -1)
     pieces = []

time: 186 us -> 192 us (1.032)
  waiting for transfers between devices: 60.3 us -> 67.7 us
  blocking collectives: 40.7 us -> 43.9 us
  starting transfers between devices: 28.9 us -> 26.5 us
    ppermute x8, waiting for transfers between devices: 29.8 us -> 46 us  [along_z(): lax.ppermute(x, 'tensor', [(t, (t + 2 * k) % devices) for t in range(devi...]
    all_gather x1, waiting for transfers between devices: 23.5 us -> 9.73 us  [per_device(): second = lax.all_gather(part_features(activations, CLIPPED), 'tensor')]
    all_to_all x1, waiting for transfers between devices: 0.01 us -> 4.95 us  [per_device(): raw = lax.all_to_all(raw, 'dp', 0, 0)]
    all_to_all x1, blocking collectives: 40.7 us -> 43.9 us  [per_device(): clipped = lax.all_to_all(clipped, 'dp', 0, 0)]
    ppermute x8, starting transfers between devices: 11.4 us -> 9.3 us  [along_z(): lax.ppermute(x, 'tensor', [(t, (t + 2 * k) % devices) for t in range(devi...]
    unnamed x35 -> x43, local copies, waits for them, and re-layouts: 4.51 us -> 4.52 us
  transfers between devices with their start and end apart: 25 -> 25, of which waited for: 13 -> 15; matrix products, arithmetic and copies ran while one was open for 3% -> 3% of each run, Pallas kernels for 14% -> 12%
where the time goes in v5:
time: 192 us
  waiting for transfers between devices  67.7 us (35%)
  blocking collectives  43.9 us (23%)
  Pallas kernels  32.4 us (17%)
  starting transfers between devices  26.5 us (14%)
  between operations  14.3 us (7%)
  local copies, waits for them, and re-layouts  4.55 us (2%)
  other arithmetic  2.15 us (1%)
    ppermute x8, waiting for transfers between devices, along_z(): lax.ppermute(x, 'tensor', [(t, (t + 2 * k) % devices) for t in range(devi...  46 us
    all_to_all x1, blocking collectives, per_device(): clipped = lax.all_to_all(clipped, 'dp', 0, 0)  43.9 us
    pallas_call x1, Pallas kernels, raw_products(): pl.pallas_call(raw_kernel, grid=(examples,), in_specs=[pl.BlockSpec(memor...  10.2 us
    ppermute x15, starting transfers between devices, crossed(): return lax.ppermute(x, 'tensor', [(t, t ^ k) for t in range(devices)])  9.96 us
    pallas_call x1, Pallas kernels, plain_products(): pl.pallas_call(plain_kernel, grid=(examples, features // width), in_specs...  9.78 us
    all_gather x1, waiting for transfers between devices, per_device(): second = lax.all_gather(part_features(activations, CLIPPED), 'tensor')  9.73 us
    ppermute x8, starting transfers between devices, along_z(): lax.ppermute(x, 'tensor', [(t, (t + 2 * k) % devices) for t in range(devi...  9.3 us
    all_to_all x1, starting transfers between devices, per_device(): raw = lax.all_to_all(raw, 'dp', 0, 0)  7.26 us
  transfers between devices with their start and end apart: 25, of which 15 were waited for; matrix products, arithmetic and copies ran while one was open for 3% of the time, Pallas kernels for 12%

profile of v5, /device:TPU:32, one launch (start us, length us, event | category | flops | bytes accessed | tf_op | source)
XLA Modules:
  0.0 191.5 jit_solution(2492763355509876699)
XLA Ops:
  6.5 2.1 %shard_map.73 = bf16[128,1536]{1,0:T(8,128)(2,1)} custom-call(bf16[128,4096]{1,0:T(8,128)(2,1)} %bitcast.6), custom_call_target="tpu_custom_call" | custom-call | tf_op jit(solution)/shard_map/pallas_call | solution.py:37
  8.6 1.9 %collective-permute-start = (bf16[2,64,1536]{2,1,0:T(8,128)(2,1)}, bf16[2,64,1536]{2,1,0:T(8,128)(2,1)S(1)}, u32[]{:S(2)}, u32[]{:S(2)}) collective-permute-start(bf16[2,64,1536]{2,1,0:T(8,128)(2,1)} %bitcast.9), channel_id=1, source_target_pairs={{0,2},{1,3},{2,4},{3,5},{4,6},{5,7},{6,8},{7,9},{8,10},{9,11},{10,... | collective-permute-start | bytes 1179656 | tf_op jit(solution)/shard_map/ppermute | solution.py:375
  10.5 0.1 collective-permute-start.1
  10.7 9.0 %collective-permute-done.refs_2_ = bf16[2,64,1536]{2,1,0:T(8,128)(2,1)S(1)} collective-permute-done((bf16[2,64,1536]{2,1,0:T(8,128)(2,1)}, bf16[2,64,1536]{2,1,0:T(8,128)(2,1)S(1)}, u32[]{:S(2)}, u32[]{:S(2)}) %collective-permute-start) | collective-permute-done | bytes 393248 | tf_op jit(solution)/shard_map/ppermute | solution.py:375
  19.7 1.8 collective-permute-done.1.refs_4_
  21.5 2.2 %shard_map.74 = bf16[128,2560]{1,0:T(8,128)(2,1)} custom-call(bf16[128,4096]{1,0:T(8,128)(2,1)} %bitcast.7), custom_call_target="tpu_custom_call" | custom-call | tf_op jit(solution)/shard_map/pallas_call | solution.py:37
  23.7 0.0 all-gather.2.cloned.1.call-update
  23.8 0.1 iota_compare_fusion
  23.8 3.1 %collective-permute-start.2 = (bf16[2,64,1536]{2,1,0:T(8,128)(2,1)S(1)}, bf16[2,64,1536]{2,1,0:T(8,128)(2,1)S(1)}, u32[]{:S(2)}, u32[]{:S(2)}) collective-permute-start(bf16[2,64,1536]{2,1,0:T(8,128)(2,1)S(1)} %collective-permute-done.refs_2_), channel_id=1, source_target_pairs={{0,2},{1,3},{2,4},{3,5},{4,6},{5,7},{6,8},{7,9},{8,10},{9,11},{10,... | collective-permute-start | bytes 1179656 | tf_op jit(solution)/shard_map/ppermute | solution.py:375
  27.0 0.6 add_and_fusion.order_ref
  27.6 3.0 %copy.9 = bf16[2,1024,512]{1,2,0:T(8,128)(2,1)S(1)} copy(bf16[2,1024,512]{2,1,0:T(8,128)(2,1)} %param.8) | data formatting | bytes 4194304 | tf_op args[1]
  30.6 1.5 select_bitcast_fusion.refs_18_.grads_ref
  32.1 2.9 %collective-permute-done.2.refs_6_ = bf16[2,64,1536]{2,1,0:T(8,128)(2,1)S(1)} collective-permute-done((bf16[2,64,1536]{2,1,0:T(8,128)(2,1)S(1)}, bf16[2,64,1536]{2,1,0:T(8,128)(2,1)S(1)}, u32[]{:S(2)}, u32[]{:S(2)}) %collective-permute-start.2) | collective-permute-done | bytes 393248 | tf_op jit(solution)/shard_map/ppermute | solution.py:375
  34.9 2.7 %collective-permute-done.3.refs_8_ = bf16[2,64,1536]{2,1,0:T(8,128)(2,1)} collective-permute-done((bf16[2,64,1536]{2,1,0:T(8,128)(2,1)S(1)}, bf16[2,64,1536]{2,1,0:T(8,128)(2,1)}, u32[]{:S(2)}, u32[]{:S(2)}) %collective-permute-start.3) | collective-permute-done | bytes 393248 | tf_op jit(solution)/shard_map/ppermute | solution.py:375
  37.6 1.7 collective-permute-start.9
  39.4 0.3 collective-permute-start.11
  39.7 0.5 collective-permute-start.5
  40.2 0.1 collective-permute-start.6
  40.3 16.5 %collective-permute-done.9.refs_10_ = bf16[2,64,1536]{2,1,0:T(8,128)(2,1)S(1)} collective-permute-done((bf16[2,64,1536]{2,1,0:T(8,128)(2,1)S(1)}, bf16[2,64,1536]{2,1,0:T(8,128)(2,1)S(1)}, u32[]{:S(2)}, u32[]{:S(2)}) %collective-permute-start.9) | collective-permute-done | bytes 393248 | tf_op jit(solution)/shard_map/ppermute | solution.py:375
  56.9 1.9 collective-permute-done.11.refs_12_
  58.8 2.0 %collective-permute-start.13 = (bf16[1,64,1536]{2,1,0:T(8,128)(2,1)S(1)}, bf16[1,64,1536]{2,1,0:T(8,128)(2,1)S(1)}, u32[]{:S(2)}, u32[]{:S(2)}) collective-permute-start(bf16[1,64,1536]{2,1,0:T(8,128)(2,1)S(1)} %slice.8), channel_id=1, source_target_pairs={{0,2},{1,3},{2,4},{3,5},{4,6},{5,7},{6,8},{7,9},{8,10},{9,11},{10,... | collective-permute-start | bytes 589832 | tf_op jit(solution)/shard_map/ppermute | solution.py:375
  60.8 0.1 collective-permute-start.15
  60.9 0.2 collective-permute-start.10
  61.1 0.3 collective-permute-start.12
  61.4 9.2 %collective-permute-done.13.refs_14_ = bf16[1,64,1536]{2,1,0:T(8,128)(2,1)S(1)} collective-permute-done((bf16[1,64,1536]{2,1,0:T(8,128)(2,1)S(1)}, bf16[1,64,1536]{2,1,0:T(8,128)(2,1)S(1)}, u32[]{:S(2)}, u32[]{:S(2)}) %collective-permute-start.13) | collective-permute-done | bytes 196640 | tf_op jit(solution)/shard_map/ppermute | solution.py:375
  70.7 1.8 collective-permute-done.15.refs_16_
  72.5 1.4 collective-permute-done.16.refs_17_
  74.1 0.6 copy-done.17
  74.6 0.1 copy-done.12
  74.8 0.8 copy-done.13
  75.5 10.2 %shard_map.75 = (s16[16,2,384,128]{3,2,1,0:T(8,128)(2,1)}, f32[16,2,8,128]{3,2,1,0:T(8,128)}, f32[2,1,128]{2,1,0:T(1,128)}) custom-call(s32[16]{0:T(128)} %add_and_fusion.order_ref, bf16[2,64,1536]{2,1,0:T(8,128)(2,1)} %bitcast.11, bf16[2,64,1536]{2,1,0:T(8,128)(2,1)} %copy-done.7, bf16[2,64,1536]{2,1,0:T(8,128)(2,1)} %copy-done.4, ...), custom_call_target="tpu_custom_call" | custom-call | tf_op jit(solution)/shard_map/pallas_call | solution.py:139
  85.7 7.3 %all-to-all-start = ((s16[16,2,384,128]{3,2,1,0:T(8,128)(2,1)}), s16[16,2,384,128]{3,2,1,0:T(8,128)(2,1)}, u32[]{:S(2)}, u32[]{:S(2)}) async-start(s16[16,2,384,128]{3,2,1,0:T(8,128)(2,1)} %get-tuple-element.32), calls=%async_computation | async-start | bytes 6291456 | tf_op jit(solution)/shard_map/all_to_all | solution.py:402
  93.0 9.7 %all-gather.2.cloned.1.call-done.acts_ref = bf16[16,2,64,2560]{3,2,1,0:T(8,128)(2,1)} async-done(((bf16[1,2,64,2560]{3,2,1,0:T(8,128)(2,1)}), bf16[16,2,64,2560]{3,2,1,0:T(8,128)(2,1)}) %all-gather.2.cloned.1.call-update) | async-done | bytes 10485776 | tf_op jit(solution)/shard_map/all_gather | solution.py:392
  102.7 9.8 %shard_map.76 = (f32[2,512,2560]{2,1,0:T(8,128)S(1)}, f32[2,1,2560]{2,1,0:T(1,128)S(1)}, f32[2,1,128]{2,1,0:T(1,128)S(1)}) custom-call(bf16[16,2,64,2560]{3,2,1,0:T(8,128)(2,1)} %all-gather.2.cloned.1.call-done.acts_ref, bf16[2,512,1024]{2,1,0:T(8,128)(2,1)} %select_bitcast_fusion.refs_18_.grads_ref, f32[2,1,128]{2,1,0:T(1,128)} %get-tuple-element.27.squares_ref), custom_call_target="tpu_custom_call" | custom-call | flops 1 | bytes 1 | tf_op jit(solution)/shard_map/pallas_call | solution.py:213
  112.5 0.3 collective-permute-start.17
  112.8 0.9 collective-permute-start.18
  113.8 0.7 collective-permute-start.19
  114.5 1.9 %collective-permute-done.18 = f32[2,1,128]{2,1,0:T(1,128)S(1)} collective-permute-done((f32[2,1,128]{2,1,0:T(1,128)S(1)}, f32[2,1,128]{2,1,0:T(1,128)S(1)}, u32[]{:S(2)}, u32[]{:S(2)}) %collective-permute-start.18) | collective-permute-done | bytes 1056 | tf_op jit(solution)/shard_map/ppermute | solution.py:378
  116.4 0.3 collective-permute-done.19
  116.8 3.2 %collective-permute-start.20 = (f32[2,1,128]{2,1,0:T(1,128)S(1)}, f32[2,1,128]{2,1,0:T(1,128)S(1)}, u32[]{:S(2)}, u32[]{:S(2)}) collective-permute-start(f32[2,1,128]{2,1,0:T(1,128)S(1)} %add_add_fusion.1), channel_id=1, source_target_pairs={{0,4},{1,5},{2,6},{3,7},{4,0},{5,1},{6,2},{7,3},{8,12},{9,13},{10,... | collective-permute-start | bytes 3080 | tf_op jit(solution)/shard_map/ppermute | solution.py:378
  120.0 1.9 %collective-permute-start.21 = (f32[2,1,128]{2,1,0:T(1,128)S(1)}, f32[2,1,128]{2,1,0:T(1,128)S(1)}, u32[]{:S(2)}, u32[]{:S(2)}) collective-permute-start(f32[2,1,128]{2,1,0:T(1,128)S(1)} %add_add_fusion.1), channel_id=1, source_target_pairs={{0,8},{1,9},{2,10},{3,11},{4,12},{5,13},{6,14},{7,15},{8,0},{9,1},... | collective-permute-start | bytes 3080 | tf_op jit(solution)/shard_map/ppermute | solution.py:378
  121.9 1.7 collective-permute-start.22
  124.3 3.1 %collective-permute-done.21 = f32[2,1,128]{2,1,0:T(1,128)S(1)} collective-permute-done((f32[2,1,128]{2,1,0:T(1,128)S(1)}, f32[2,1,128]{2,1,0:T(1,128)S(1)}, u32[]{:S(2)}, u32[]{:S(2)}) %collective-permute-start.21) | collective-permute-done | bytes 1056 | tf_op jit(solution)/shard_map/ppermute | solution.py:378
  127.5 0.1 collective-permute-done.22
  127.6 3.0 %shard_map.77 = s16[16,656,128]{2,1,0:T(8,128)(2,1)S(1)} custom-call(f32[1]{0:T(128)S(6)} %copy.10.clip_ref, f32[2,1,128]{2,1,0:T(1,128)S(1)} %add_add_fusion.shares_ref, f32[2,512,2560]{2,1,0:T(8,128)S(1)} %get-tuple-element.29.wide_ref.thin_ref, f32[2,512,2560]{2,1,0:T(8,128)S(1)} %get-tuple-element.29.wide_ref.thin_ref, ...), custom_call_target="tpu_custom_call" | custom-call | flops 1 | bytes 1 | tf_op jit(solution)/shard_map/pallas_call | solution.py:280
  130.6 4.9 %all-to-all-done.raw_ref = s16[16,2,384,128]{3,2,1,0:T(8,128)(2,1)} async-done(((s16[16,2,384,128]{3,2,1,0:T(8,128)(2,1)}), s16[16,2,384,128]{3,2,1,0:T(8,128)(2,1)}, u32[]{:S(2)}, u32[]{:S(2)}) %all-to-all-start) | async-done | bytes 3145760 | tf_op jit(solution)/shard_map/all_to_all | solution.py:402
  135.6 43.9 %all_to_all.10.clipped_ref = s16[16,656,128]{2,1,0:T(8,128)(2,1)} all-to-all(s16[16,656,128]{2,1,0:T(8,128)(2,1)S(1)} %shard_map.77), channel_id=1, replica_groups=mesh['dp'=16,'tensor'=16] {'dp'}, dimensions={0} | all-to-all | bytes 5373952 | tf_op jit(solution)/shard_map/all_to_all | solution.py:408
  179.5 5.2 %shard_map.78 = f32[256,512]{1,0:T(8,128)} custom-call(s16[16,2,384,128]{3,2,1,0:T(8,128)(2,1)} %all-to-all-done.raw_ref, s16[16,656,128]{2,1,0:T(8,128)(2,1)} %all_to_all.10.clipped_ref, f32[256,512]{1,0:T(8,128)} %noise_ref.1), custom_call_target="tpu_custom_call" | custom-call | tf_op jit(solution)/shard_map/pallas_call | solution.py:353
  (60 shorter events, 0.2 us)
Async XLA Ops:
  6.5 20.4 %copy-start.19 = (s32[16]{0:T(128)S(1)}, s32[16]{0:T(128)}, u32[]{:S(2)}) copy-start(s32[16]{0:T(128)} %constant.16.clone) | copy-start | bytes 196
  6.5 20.4 %copy-start.20 = (s32[16]{0:T(128)S(1)}, s32[16]{0:T(128)}, u32[]{:S(2)}) copy-start(s32[16]{0:T(128)} %constant.17.clone) | copy-start | bytes 196
  6.5 17.2 %copy-start.18 = (s32[2]{0:T(128)S(1)}, s32[2]{0:T(128)}, u32[]{:S(2)}) copy-start(s32[2]{0:T(128)} %param.9) | copy-start | bytes 28
  6.5 96.2 %all-gather.2.cloned.1.call-start = ((), (), s32[]{:S(2)}) async-start(), calls=%async_computation.2 | async-start | bytes 11141120 | tf_op jit(solution)/shard_map/all_gather | solution.py:392
  8.6 11.1 %collective-permute-start = (bf16[2,64,1536]{2,1,0:T(8,128)(2,1)}, bf16[2,64,1536]{2,1,0:T(8,128)(2,1)S(1)}, u32[]{:S(2)}, u32[]{:S(2)}) collective-permute-start(bf16[2,64,1536]{2,1,0:T(8,128)(2,1)} %bitcast.9), channel_id=1, source_target_pairs={{0,2},{1,3},{2,4},{3,5},{4,6},{5,7},{6,8},{7,9},{8,10},{9,11},{10,... | collective-permute-start | bytes 1179656 | tf_op jit(solution)/shard_map/ppermute | solution.py:375
  10.5 11.0 %collective-permute-start.1 = (bf16[2,64,1536]{2,1,0:T(8,128)(2,1)}, bf16[2,64,1536]{2,1,0:T(8,128)(2,1)S(1)}, u32[]{:S(2)}, u32[]{:S(2)}) collective-permute-start(bf16[2,64,1536]{2,1,0:T(8,128)(2,1)} %bitcast.10), channel_id=1, source_target_pairs={{0,14},{1,15},{2,0},{3,1},{4,2},{5,3},{6,4},{7,5},{8,6},{9,7},{10,... | collective-permute-start | bytes 1179656 | tf_op jit(solution)/shard_map/ppermute | solution.py:375
  19.7 20.0 %copy-start.4 = (bf16[2,64,1536]{2,1,0:T(8,128)(2,1)}, bf16[2,64,1536]{2,1,0:T(8,128)(2,1)S(1)}, u32[]{:S(2)}) copy-start(bf16[2,64,1536]{2,1,0:T(8,128)(2,1)S(1)} %collective-permute-done.refs_2_) | copy-start | bytes 1179652
  21.5 18.7 %copy-start.5 = (bf16[2,64,1536]{2,1,0:T(8,128)(2,1)}, bf16[2,64,1536]{2,1,0:T(8,128)(2,1)S(1)}, u32[]{:S(2)}) copy-start(bf16[2,64,1536]{2,1,0:T(8,128)(2,1)S(1)} %collective-permute-done.1.refs_4_) | copy-start | bytes 1179652
  23.8 11.1 %collective-permute-start.2 = (bf16[2,64,1536]{2,1,0:T(8,128)(2,1)S(1)}, bf16[2,64,1536]{2,1,0:T(8,128)(2,1)S(1)}, u32[]{:S(2)}, u32[]{:S(2)}) collective-permute-start(bf16[2,64,1536]{2,1,0:T(8,128)(2,1)S(1)} %collective-permute-done.refs_2_), channel_id=1, source_target_pairs={{0,2},{1,3},{2,4},{3,5},{4,6},{5,7},{6,8},{7,9},{8,10},{9,11},{10,... | collective-permute-start | bytes 1179656 | tf_op jit(solution)/shard_map/ppermute | solution.py:375
  27.0 10.7 %collective-permute-start.3 = (bf16[2,64,1536]{2,1,0:T(8,128)(2,1)S(1)}, bf16[2,64,1536]{2,1,0:T(8,128)(2,1)}, u32[]{:S(2)}, u32[]{:S(2)}) collective-permute-start(bf16[2,64,1536]{2,1,0:T(8,128)(2,1)S(1)} %collective-permute-done.1.refs_4_), channel_id=1, source_target_pairs={{0,14},{1,15},{2,0},{3,1},{4,2},{5,3},{6,4},{7,5},{8,6},{9,7},{10,... | collective-permute-start | bytes 1179656 | tf_op jit(solution)/shard_map/ppermute | solution.py:375
  30.6 9.1 %copy-start.1 = (bf16[128,1536]{1,0:T(8,128)(2,1)S(1)}, bf16[128,1536]{1,0:T(8,128)(2,1)}, u32[]{:S(2)}) copy-start(bf16[128,1536]{1,0:T(8,128)(2,1)} %shard_map.73) | copy-start | bytes 1179652
  34.9 39.0 %copy-start.6 = (bf16[2,64,1536]{2,1,0:T(8,128)(2,1)}, bf16[2,64,1536]{2,1,0:T(8,128)(2,1)S(1)}, u32[]{:S(2)}) copy-start(bf16[2,64,1536]{2,1,0:T(8,128)(2,1)S(1)} %collective-permute-done.2.refs_6_) | copy-start | bytes 1179652
  37.6 19.2 %collective-permute-start.9 = (bf16[2,64,1536]{2,1,0:T(8,128)(2,1)S(1)}, bf16[2,64,1536]{2,1,0:T(8,128)(2,1)S(1)}, u32[]{:S(2)}, u32[]{:S(2)}) collective-permute-start(bf16[2,64,1536]{2,1,0:T(8,128)(2,1)S(1)} %collective-permute-done.2.refs_6_), channel_id=1, source_target_pairs={{0,2},{1,3},{2,4},{3,5},{4,6},{5,7},{6,8},{7,9},{8,10},{9,11},{10,... | collective-permute-start | bytes 1179656 | tf_op jit(solution)/shard_map/ppermute | solution.py:375
  39.4 19.4 %collective-permute-start.11 = (bf16[2,64,1536]{2,1,0:T(8,128)(2,1)}, bf16[2,64,1536]{2,1,0:T(8,128)(2,1)S(1)}, u32[]{:S(2)}, u32[]{:S(2)}) collective-permute-start(bf16[2,64,1536]{2,1,0:T(8,128)(2,1)} %collective-permute-done.3.refs_8_), channel_id=1, source_target_pairs={{0,14},{1,15},{2,0},{3,1},{4,2},{5,3},{6,4},{7,5},{8,6},{9,7},{10,... | collective-permute-start | bytes 1179656 | tf_op jit(solution)/shard_map/ppermute | solution.py:375
  39.7 19.1 %collective-permute-start.4 = (bf16[2,64,1536]{2,1,0:T(8,128)(2,1)S(1)}, bf16[2,64,1536]{2,1,0:T(8,128)(2,1)S(1)}, u32[]{:S(2)}, u32[]{:S(2)}) collective-permute-start(bf16[2,64,1536]{2,1,0:T(8,128)(2,1)S(1)} %bitcast.12), channel_id=1, source_target_pairs={{0,1},{1,0},{2,3},{3,2},{4,5},{5,4},{6,7},{7,6},{8,9},{9,8},{10,11... | collective-permute-start | bytes 1179656 | tf_op jit(solution)/shard_map/ppermute | solution.py:378
  39.7 21.1 %collective-permute-start.5 = (bf16[2,64,1536]{2,1,0:T(8,128)(2,1)S(1)}, bf16[2,64,1536]{2,1,0:T(8,128)(2,1)S(1)}, u32[]{:S(2)}, u32[]{:S(2)}) collective-permute-start(bf16[2,64,1536]{2,1,0:T(8,128)(2,1)S(1)} %collective-permute-done.refs_2_), channel_id=1, source_target_pairs={{0,1},{1,0},{2,3},{3,2},{4,5},{5,4},{6,7},{7,6},{8,9},{9,8},{10,11... | collective-permute-start | bytes 1179656 | tf_op jit(solution)/shard_map/ppermute | solution.py:378
  40.2 20.7 %collective-permute-start.6 = (bf16[2,64,1536]{2,1,0:T(8,128)(2,1)S(1)}, bf16[2,64,1536]{2,1,0:T(8,128)(2,1)S(1)}, u32[]{:S(2)}, u32[]{:S(2)}) collective-permute-start(bf16[2,64,1536]{2,1,0:T(8,128)(2,1)S(1)} %collective-permute-done.1.refs_4_), channel_id=1, source_target_pairs={{0,1},{1,0},{2,3},{3,2},{4,5},{5,4},{6,7},{7,6},{8,9},{9,8},{10,11... | collective-permute-start | bytes 1179656 | tf_op jit(solution)/shard_map/ppermute | solution.py:378
  56.8 17.1 %copy-start.2 = (bf16[2,64,1536]{2,1,0:T(8,128)(2,1)}, bf16[2,64,1536]{2,1,0:T(8,128)(2,1)S(1)}, u32[]{:S(2)}) copy-start(bf16[2,64,1536]{2,1,0:T(8,128)(2,1)S(1)} %collective-permute-done.9.refs_10_) | copy-start | bytes 1179652
  56.8 4.3 %collective-permute-start.7 = (bf16[2,64,1536]{2,1,0:T(8,128)(2,1)S(1)}, bf16[2,64,1536]{2,1,0:T(8,128)(2,1)S(1)}, u32[]{:S(2)}, u32[]{:S(2)}) collective-permute-start(bf16[2,64,1536]{2,1,0:T(8,128)(2,1)S(1)} %collective-permute-done.2.refs_6_), channel_id=1, source_target_pairs={{0,1},{1,0},{2,3},{3,2},{4,5},{5,4},{6,7},{7,6},{8,9},{9,8},{10,11... | collective-permute-start | bytes 1179656 | tf_op jit(solution)/shard_map/ppermute | solution.py:378
  58.8 15.2 %copy-start.3 = (bf16[2,64,1536]{2,1,0:T(8,128)(2,1)}, bf16[2,64,1536]{2,1,0:T(8,128)(2,1)S(1)}, u32[]{:S(2)}) copy-start(bf16[2,64,1536]{2,1,0:T(8,128)(2,1)S(1)} %collective-permute-done.11.refs_12_) | copy-start | bytes 1179652
  58.8 13.7 %collective-permute-start.8 = (bf16[2,64,1536]{2,1,0:T(8,128)(2,1)}, bf16[2,64,1536]{2,1,0:T(8,128)(2,1)S(1)}, u32[]{:S(2)}, u32[]{:S(2)}) collective-permute-start(bf16[2,64,1536]{2,1,0:T(8,128)(2,1)} %collective-permute-done.3.refs_8_), channel_id=1, source_target_pairs={{0,1},{1,0},{2,3},{3,2},{4,5},{5,4},{6,7},{7,6},{8,9},{9,8},{10,11... | collective-permute-start | bytes 1179656 | tf_op jit(solution)/shard_map/ppermute | solution.py:378
  58.8 15.2 %copy-start.7 = (bf16[2,64,1536]{2,1,0:T(8,128)(2,1)}, bf16[2,64,1536]{2,1,0:T(8,128)(2,1)S(1)}, u32[]{:S(2)}) copy-start(bf16[2,64,1536]{2,1,0:T(8,128)(2,1)S(1)} %collective-permute-done.4.refs_1_) | copy-start | bytes 1179652
  58.8 11.9 %collective-permute-start.13 = (bf16[1,64,1536]{2,1,0:T(8,128)(2,1)S(1)}, bf16[1,64,1536]{2,1,0:T(8,128)(2,1)S(1)}, u32[]{:S(2)}, u32[]{:S(2)}) collective-permute-start(bf16[1,64,1536]{2,1,0:T(8,128)(2,1)S(1)} %slice.8), channel_id=1, source_target_pairs={{0,2},{1,3},{2,4},{3,5},{4,6},{5,7},{6,8},{7,9},{8,10},{9,11},{10,... | collective-permute-start | bytes 589832 | tf_op jit(solution)/shard_map/ppermute | solution.py:375
  60.8 13.2 %copy-start.8 = (bf16[2,64,1536]{2,1,0:T(8,128)(2,1)}, bf16[2,64,1536]{2,1,0:T(8,128)(2,1)S(1)}, u32[]{:S(2)}) copy-start(bf16[2,64,1536]{2,1,0:T(8,128)(2,1)S(1)} %collective-permute-done.5.refs_3_) | copy-start | bytes 1179652
  60.8 11.7 %collective-permute-start.15 = (bf16[1,64,1536]{2,1,0:T(8,128)(2,1)S(1)}, bf16[1,64,1536]{2,1,0:T(8,128)(2,1)S(1)}, u32[]{:S(2)}, u32[]{:S(2)}) collective-permute-start(bf16[1,64,1536]{2,1,0:T(8,128)(2,1)S(1)} %slice.9), channel_id=1, source_target_pairs={{0,14},{1,15},{2,0},{3,1},{4,2},{5,3},{6,4},{7,5},{8,6},{9,7},{10,... | collective-permute-start | bytes 589832 | tf_op jit(solution)/shard_map/ppermute | solution.py:375
  60.9 13.1 %copy-start.9 = (bf16[2,64,1536]{2,1,0:T(8,128)(2,1)}, bf16[2,64,1536]{2,1,0:T(8,128)(2,1)S(1)}, u32[]{:S(2)}) copy-start(bf16[2,64,1536]{2,1,0:T(8,128)(2,1)S(1)} %collective-permute-done.6.refs_5_) | copy-start | bytes 1179652
  60.9 13.0 %collective-permute-start.10 = (bf16[2,64,1536]{2,1,0:T(8,128)(2,1)S(1)}, bf16[2,64,1536]{2,1,0:T(8,128)(2,1)S(1)}, u32[]{:S(2)}, u32[]{:S(2)}) collective-permute-start(bf16[2,64,1536]{2,1,0:T(8,128)(2,1)S(1)} %collective-permute-done.9.refs_10_), channel_id=1, source_target_pairs={{0,1},{1,0},{2,3},{3,2},{4,5},{5,4},{6,7},{7,6},{8,9},{9,8},{10,11... | collective-permute-start | bytes 1179656 | tf_op jit(solution)/shard_map/ppermute | solution.py:378
  61.1 12.9 %copy-start.10 = (bf16[2,64,1536]{2,1,0:T(8,128)(2,1)}, bf16[2,64,1536]{2,1,0:T(8,128)(2,1)S(1)}, u32[]{:S(2)}) copy-start(bf16[2,64,1536]{2,1,0:T(8,128)(2,1)S(1)} %collective-permute-done.7.refs_7_) | copy-start | bytes 1179652
  61.1 12.8 %collective-permute-start.12 = (bf16[2,64,1536]{2,1,0:T(8,128)(2,1)S(1)}, bf16[2,64,1536]{2,1,0:T(8,128)(2,1)S(1)}, u32[]{:S(2)}, u32[]{:S(2)}) collective-permute-start(bf16[2,64,1536]{2,1,0:T(8,128)(2,1)S(1)} %collective-permute-done.11.refs_12_), channel_id=1, source_target_pairs={{0,1},{1,0},{2,3},{3,2},{4,5},{5,4},{6,7},{7,6},{8,9},{9,8},{10,11... | collective-permute-start | bytes 1179656 | tf_op jit(solution)/shard_map/ppermute | solution.py:378
  70.7 3.3 %copy-start.14 = (bf16[1,64,1536]{2,1,0:T(8,128)(2,1)}, bf16[1,64,1536]{2,1,0:T(8,128)(2,1)S(1)}, u32[]{:S(2)}) copy-start(bf16[1,64,1536]{2,1,0:T(8,128)(2,1)S(1)} %collective-permute-done.13.refs_14_) | copy-start | bytes 589828
  70.7 1.8 collective-permute-start.14
  72.5 1.5 copy-start.15
  72.5 1.4 collective-permute-start.16
  72.5 1.5 copy-start.11
  72.5 1.5 copy-start.16
  73.9 0.7 copy-start.17
  73.9 0.8 copy-start.12
  74.8 0.8 copy-start.13
  85.7 49.9 %all-to-all-start = ((s16[16,2,384,128]{3,2,1,0:T(8,128)(2,1)}), s16[16,2,384,128]{3,2,1,0:T(8,128)(2,1)}, u32[]{:S(2)}, u32[]{:S(2)}) async-start(s16[16,2,384,128]{3,2,1,0:T(8,128)(2,1)} %get-tuple-element.32), calls=%async_computation | async-start | bytes 6291456 | tf_op jit(solution)/shard_map/all_to_all | solution.py:402
  102.7 24.9 %copy-start = (f32[16,2,8,128]{3,2,1,0:T(8,128)S(1)}, f32[16,2,8,128]{3,2,1,0:T(8,128)}, u32[]{:S(2)}) copy-start(f32[16,2,8,128]{3,2,1,0:T(8,128)} %get-tuple-element.31.exponent_ref) | copy-start | bytes 393220
  112.5 2.0 %collective-permute-start.17 = (f32[2,1,128]{2,1,0:T(1,128)S(1)}, f32[2,1,128]{2,1,0:T(1,128)S(1)}, u32[]{:S(2)}, u32[]{:S(2)}) collective-permute-start(f32[2,1,128]{2,1,0:T(1,128)S(1)} %get-tuple-element.28), channel_id=1, source_target_pairs={{0,1},{1,0},{2,3},{3,2},{4,5},{5,4},{6,7},{7,6},{8,9},{9,8},{10,11... | collective-permute-start | bytes 3080 | tf_op jit(solution)/shard_map/ppermute | solution.py:378
  112.8 3.6 %collective-permute-start.18 = (f32[2,1,128]{2,1,0:T(1,128)S(1)}, f32[2,1,128]{2,1,0:T(1,128)S(1)}, u32[]{:S(2)}, u32[]{:S(2)}) collective-permute-start(f32[2,1,128]{2,1,0:T(1,128)S(1)} %get-tuple-element.28), channel_id=1, source_target_pairs={{0,2},{1,3},{2,0},{3,1},{4,6},{5,7},{6,4},{7,5},{8,10},{9,11},{10,... | collective-permute-start | bytes 3080 | tf_op jit(solution)/shard_map/ppermute | solution.py:378
  113.8 3.0 %collective-permute-start.19 = (f32[2,1,128]{2,1,0:T(1,128)S(1)}, f32[2,1,128]{2,1,0:T(1,128)S(1)}, u32[]{:S(2)}, u32[]{:S(2)}) collective-permute-start(f32[2,1,128]{2,1,0:T(1,128)S(1)} %get-tuple-element.28), channel_id=1, source_target_pairs={{0,3},{1,2},{2,1},{3,0},{4,7},{5,6},{6,5},{7,4},{8,11},{9,10},{10,... | collective-permute-start | bytes 3080 | tf_op jit(solution)/shard_map/ppermute | solution.py:378
  116.8 7.6 %collective-permute-start.20 = (f32[2,1,128]{2,1,0:T(1,128)S(1)}, f32[2,1,128]{2,1,0:T(1,128)S(1)}, u32[]{:S(2)}, u32[]{:S(2)}) collective-permute-start(f32[2,1,128]{2,1,0:T(1,128)S(1)} %add_add_fusion.1), channel_id=1, source_target_pairs={{0,4},{1,5},{2,6},{3,7},{4,0},{5,1},{6,2},{7,3},{8,12},{9,13},{10,... | collective-permute-start | bytes 3080 | tf_op jit(solution)/shard_map/ppermute | solution.py:378
  120.0 7.5 %collective-permute-start.21 = (f32[2,1,128]{2,1,0:T(1,128)S(1)}, f32[2,1,128]{2,1,0:T(1,128)S(1)}, u32[]{:S(2)}, u32[]{:S(2)}) collective-permute-start(f32[2,1,128]{2,1,0:T(1,128)S(1)} %add_add_fusion.1), channel_id=1, source_target_pairs={{0,8},{1,9},{2,10},{3,11},{4,12},{5,13},{6,14},{7,15},{8,0},{9,1},... | collective-permute-start | bytes 3080 | tf_op jit(solution)/shard_map/ppermute | solution.py:378
  121.9 5.7 %collective-permute-start.22 = (f32[2,1,128]{2,1,0:T(1,128)S(1)}, f32[2,1,128]{2,1,0:T(1,128)S(1)}, u32[]{:S(2)}, u32[]{:S(2)}) collective-permute-start(f32[2,1,128]{2,1,0:T(1,128)S(1)} %add_add_fusion.1), channel_id=1, source_target_pairs={{0,12},{1,13},{2,14},{3,15},{4,8},{5,9},{6,10},{7,11},{8,4},{9,5},... | collective-permute-start | bytes 3080 | tf_op jit(solution)/shard_map/ppermute | solution.py:378
Sparse Core Ops, SparseCore 0:
  23.9 78.8 all-gather.1

commit v6 on v5

--- a/solution.py
+++ b/solution.py
@@ -9,7 +9,7 @@
 
 LANES = 128
 EXTRA = 16
-TOGETHER = 4
+TOGETHER = 8
 LEAST = 1e-33
 CHUNK = 256
 PARAMS = pltpu.CompilerParams(vmem_limit_bytes=56 * 1024 * 1024)
@@ -378,6 +378,7 @@
         return lax.ppermute(x, "tensor", [(t, t ^ k) for t in range(devices)])
 
     own = part_features(activations, RAW)
+    second = part_features(activations, CLIPPED)
     positions = lax.broadcasted_iota(jnp.int32, (1, out_grads.shape[1], 1), 1)
     masked = jnp.where(positions < lengths[:, None, None], out_grads, jnp.zeros_like(out_grads))
     masked = jnp.swapaxes(masked, 1, 2)
@@ -387,10 +388,9 @@
     order = ((here & ~1) + step + ((here & 1) ^ second_core)) & (devices - 1)
 
     up1, down1 = along_z(own, 1), along_z(own, -1)
-    up1, down1, activations = lax.optimization_barrier((up1, down1, activations))
     up2, down2 = along_z(up1, 1), along_z(down1, -1)
-    second = lax.all_gather(part_features(activations, CLIPPED), "tensor")
-    up2, down2, masked, order = lax.optimization_barrier((up2, down2, masked, order))
+    up2, down2, second, masked, order = lax.optimization_barrier((up2, down2, second, masked, order))
+    second = lax.all_gather(second, "tensor")
     up3, down3 = along_z(up2, 1), along_z(down2, -1)
     up4, down4 = along_z(up3[:1], 1), along_z(down3[1:], -1)
     pieces = []

time: 192 us -> 184 us (0.958)
  waiting for transfers between devices: 67.7 us -> 60.3 us
  blocking collectives: 43.9 us -> 40.7 us
  starting transfers between devices: 26.5 us -> 28.9 us
    ppermute x8, waiting for transfers between devices: 46 us -> 29.8 us  [along_z(): lax.ppermute(x, 'tensor', [(t, (t + 2 * k) % devices) for t in range(devi...]
    all_gather x1, waiting for transfers between devices: 9.73 us -> 23.6 us  [per_device(): second = lax.all_gather(second, 'tensor')]
    all_to_all x1, waiting for transfers between devices: 4.95 us -> 0.01 us  [per_device(): raw = lax.all_to_all(raw, 'dp', 0, 0)]
    all_to_all x1, blocking collectives: 43.9 us -> 40.7 us  [per_device(): clipped = lax.all_to_all(clipped, 'dp', 0, 0)]
    ppermute x8, starting transfers between devices: 9.3 us -> 11.4 us  [along_z(): lax.ppermute(x, 'tensor', [(t, (t + 2 * k) % devices) for t in range(devi...]
    unnamed x43 -> x35, local copies, waits for them, and re-layouts: 4.52 us -> 4.51 us
  transfers between devices with their start and end apart: 25 -> 25, of which waited for: 15 -> 13; matrix products, arithmetic and copies ran while one was open for 3% -> 4% of each run, Pallas kernels for 12% -> 14%
where the time goes in v6:
time: 184 us
  waiting for transfers between devices  60.3 us (33%)
  blocking collectives  40.7 us (22%)
  Pallas kernels  31.6 us (17%)
  starting transfers between devices  28.9 us (16%)
  between operations  14.3 us (8%)
  local copies, waits for them, and re-layouts  4.54 us (2%)
  other arithmetic  3.44 us (2%)
    all_to_all x1, blocking collectives, per_device(): clipped = lax.all_to_all(clipped, 'dp', 0, 0)  40.7 us
    ppermute x8, waiting for transfers between devices, along_z(): lax.ppermute(x, 'tensor', [(t, (t + 2 * k) % devices) for t in range(devi...  29.8 us
    all_gather x1, waiting for transfers between devices, per_device(): second = lax.all_gather(second, 'tensor')  23.6 us
    ppermute x8, starting transfers between devices, along_z(): lax.ppermute(x, 'tensor', [(t, (t + 2 * k) % devices) for t in range(devi...  11.4 us
    ppermute x15, starting transfers between devices, crossed(): return lax.ppermute(x, 'tensor', [(t, t ^ k) for t in range(devices)])  10.3 us
    pallas_call x1, Pallas kernels, raw_products(): pl.pallas_call(raw_kernel, grid=(examples,), in_specs=[pl.BlockSpec(memor...  10.1 us
    pallas_call x1, Pallas kernels, plain_products(): pl.pallas_call(plain_kernel, grid=(examples, features // width), in_specs...  9.82 us
    all_to_all x1, starting transfers between devices, per_device(): raw = lax.all_to_all(raw, 'dp', 0, 0)  7.13 us
  transfers between devices with their start and end apart: 25, of which 13 were waited for; matrix products, arithmetic and copies ran while one was open for 4% of the time, Pallas kernels for 14%

profile of v6, /device:TPU:32, one launch (start us, length us, event | category | flops | bytes accessed | tf_op | source)
XLA Modules:
  0.0 183.9 jit_solution(677660271595369303)
XLA Ops:
  6.5 2.0 %shard_map.73 = bf16[128,1536]{1,0:T(8,128)(2,1)} custom-call(bf16[128,4096]{1,0:T(8,128)(2,1)} %bitcast.7), custom_call_target="tpu_custom_call" | custom-call | tf_op jit(solution)/shard_map/pallas_call | solution.py:37
  8.6 1.9 %collective-permute-start = (bf16[2,64,1536]{2,1,0:T(8,128)(2,1)}, bf16[2,64,1536]{2,1,0:T(8,128)(2,1)S(1)}, u32[]{:S(2)}, u32[]{:S(2)}) collective-permute-start(bf16[2,64,1536]{2,1,0:T(8,128)(2,1)} %bitcast.10), channel_id=1, source_target_pairs={{0,2},{1,3},{2,4},{3,5},{4,6},{5,7},{6,8},{7,9},{8,10},{9,11},{10,... | collective-permute-start | bytes 1179656 | tf_op jit(solution)/shard_map/ppermute | solution.py:375
  10.5 0.1 collective-permute-start.2
  10.6 0.7 iota_compare_fusion
  11.3 8.3 %collective-permute-done.refs_2_ = bf16[2,64,1536]{2,1,0:T(8,128)(2,1)S(1)} collective-permute-done((bf16[2,64,1536]{2,1,0:T(8,128)(2,1)}, bf16[2,64,1536]{2,1,0:T(8,128)(2,1)S(1)}, u32[]{:S(2)}, u32[]{:S(2)}) %collective-permute-start) | collective-permute-done | bytes 393248 | tf_op jit(solution)/shard_map/ppermute | solution.py:375
  19.6 1.9 %collective-permute-start.1 = (bf16[2,64,1536]{2,1,0:T(8,128)(2,1)S(1)}, bf16[2,64,1536]{2,1,0:T(8,128)(2,1)}, u32[]{:S(2)}, u32[]{:S(2)}) collective-permute-start(bf16[2,64,1536]{2,1,0:T(8,128)(2,1)S(1)} %collective-permute-done.refs_2_), channel_id=1, source_target_pairs={{0,2},{1,3},{2,4},{3,5},{4,6},{5,7},{6,8},{7,9},{8,10},{9,11},{10,... | collective-permute-start | bytes 1179656 | tf_op jit(solution)/shard_map/ppermute | solution.py:375
  21.6 0.0 collective-permute-done.2.refs_4_
  21.6 2.4 %collective-permute-start.3 = (bf16[2,64,1536]{2,1,0:T(8,128)(2,1)S(1)}, bf16[2,64,1536]{2,1,0:T(8,128)(2,1)}, u32[]{:S(2)}, u32[]{:S(2)}) collective-permute-start(bf16[2,64,1536]{2,1,0:T(8,128)(2,1)S(1)} %collective-permute-done.2.refs_4_), channel_id=1, source_target_pairs={{0,14},{1,15},{2,0},{3,1},{4,2},{5,3},{6,4},{7,5},{8,6},{9,7},{10,... | collective-permute-start | bytes 1179656 | tf_op jit(solution)/shard_map/ppermute | solution.py:375
  24.0 1.2 add_and_fusion.order_ref
  25.2 2.0 %shard_map.74 = bf16[128,2560]{1,0:T(8,128)(2,1)} custom-call(bf16[128,4096]{1,0:T(8,128)(2,1)} %bitcast.8), custom_call_target="tpu_custom_call" | custom-call | tf_op jit(solution)/shard_map/pallas_call | solution.py:37
  27.2 3.0 %copy.9 = bf16[2,1024,512]{1,2,0:T(8,128)(2,1)S(1)} copy(bf16[2,1024,512]{2,1,0:T(8,128)(2,1)} %param.8) | data formatting | bytes 4194304 | tf_op args[1]
  30.2 0.0 copy-start.1
  30.2 1.5 select_bitcast_fusion.refs_18_.grads_ref
  31.7 0.8 collective-permute-done.1.refs_6_
  32.5 0.4 collective-permute-done.3.refs_8_
  33.0 0.0 all-gather.3.cloned.1.call-update
  33.0 3.0 %collective-permute-start.9 = (bf16[2,64,1536]{2,1,0:T(8,128)(2,1)}, bf16[2,64,1536]{2,1,0:T(8,128)(2,1)S(1)}, u32[]{:S(2)}, u32[]{:S(2)}) collective-permute-start(bf16[2,64,1536]{2,1,0:T(8,128)(2,1)} %collective-permute-done.1.refs_6_), channel_id=1, source_target_pairs={{0,2},{1,3},{2,4},{3,5},{4,6},{5,7},{6,8},{7,9},{8,10},{9,11},{10,... | collective-permute-start | bytes 1179656 | tf_op jit(solution)/shard_map/ppermute | solution.py:375
  36.0 0.5 collective-permute-start.5
  36.5 0.1 collective-permute-start.6
  36.6 6.8 %collective-permute-done.9.refs_10_ = bf16[2,64,1536]{2,1,0:T(8,128)(2,1)S(1)} collective-permute-done((bf16[2,64,1536]{2,1,0:T(8,128)(2,1)}, bf16[2,64,1536]{2,1,0:T(8,128)(2,1)S(1)}, u32[]{:S(2)}, u32[]{:S(2)}) %collective-permute-start.9) | collective-permute-done | bytes 393248 | tf_op jit(solution)/shard_map/ppermute | solution.py:375
  43.5 2.5 %collective-permute-done.11.refs_12_ = bf16[2,64,1536]{2,1,0:T(8,128)(2,1)S(1)} collective-permute-done((bf16[2,64,1536]{2,1,0:T(8,128)(2,1)}, bf16[2,64,1536]{2,1,0:T(8,128)(2,1)S(1)}, u32[]{:S(2)}, u32[]{:S(2)}) %collective-permute-start.11) | collective-permute-done | bytes 393248 | tf_op jit(solution)/shard_map/ppermute | solution.py:375
  46.0 1.8 collective-permute-start.13
  47.8 0.3 collective-permute-start.15
  48.1 0.1 collective-permute-start.10
  48.1 0.5 collective-permute-start.12
  48.6 9.2 %collective-permute-done.13.refs_14_ = bf16[1,64,1536]{2,1,0:T(8,128)(2,1)S(1)} collective-permute-done((bf16[1,64,1536]{2,1,0:T(8,128)(2,1)S(1)}, bf16[1,64,1536]{2,1,0:T(8,128)(2,1)S(1)}, u32[]{:S(2)}, u32[]{:S(2)}) %collective-permute-start.13) | collective-permute-done | bytes 196640 | tf_op jit(solution)/shard_map/ppermute | solution.py:375
  57.8 1.7 collective-permute-done.15.refs_16_
  59.5 0.0 collective-permute-start.16
  59.6 1.4 collective-permute-done.16.refs_17_
  61.1 0.6 copy-done.16
  61.6 0.2 copy-done.11
  61.8 0.7 copy-done.12
  62.5 10.1 %shard_map.75 = (s16[16,2,384,128]{3,2,1,0:T(8,128)(2,1)}, f32[16,2,8,128]{3,2,1,0:T(8,128)}, f32[2,1,128]{2,1,0:T(1,128)}) custom-call(s32[16]{0:T(128)} %add_and_fusion.order_ref, bf16[2,64,1536]{2,1,0:T(8,128)(2,1)} %bitcast.12, bf16[2,64,1536]{2,1,0:T(8,128)(2,1)} %copy-done.6, bf16[2,64,1536]{2,1,0:T(8,128)(2,1)} %copy-done.4, ...), custom_call_target="tpu_custom_call" | custom-call | tf_op jit(solution)/shard_map/pallas_call | solution.py:139
  72.7 7.1 %all-to-all-start = ((s16[16,2,384,128]{3,2,1,0:T(8,128)(2,1)}), s16[16,2,384,128]{3,2,1,0:T(8,128)(2,1)}, u32[]{:S(2)}, u32[]{:S(2)}) async-start(s16[16,2,384,128]{3,2,1,0:T(8,128)(2,1)} %get-tuple-element.28), calls=%async_computation | async-start | bytes 6291456 | tf_op jit(solution)/shard_map/all_to_all | solution.py:402
  79.8 23.6 %all-gather.3.cloned.1.call-done = bf16[32,64,2560]{2,1,0:T(8,128)(2,1)} async-done(((bf16[2,64,2560]{2,1,0:T(8,128)(2,1)}), bf16[32,64,2560]{2,1,0:T(8,128)(2,1)}) %all-gather.3.cloned.1.call-update) | async-done | bytes 10485776 | tf_op jit(solution)/shard_map/all_gather | solution.py:393
  103.4 9.8 %shard_map.76 = (f32[2,512,2560]{2,1,0:T(8,128)S(1)}, f32[2,1,2560]{2,1,0:T(1,128)S(1)}, f32[2,1,128]{2,1,0:T(1,128)S(1)}) custom-call(bf16[16,2,64,2560]{3,2,1,0:T(8,128)(2,1)} %bitcast.6, bf16[2,512,1024]{2,1,0:T(8,128)(2,1)} %select_bitcast_fusion.refs_18_.grads_ref, f32[2,1,128]{2,1,0:T(1,128)} %get-tuple-element.23.squares_ref), custom_call_target="tpu_custom_call" | custom-call | flops 1 | bytes 1 | tf_op jit(solution)/shard_map/pallas_call | solution.py:213
  113.2 0.3 collective-permute-start.17
  113.5 2.3 %collective-permute-start.18 = (f32[2,1,128]{2,1,0:T(1,128)S(1)}, f32[2,1,128]{2,1,0:T(1,128)S(1)}, u32[]{:S(2)}, u32[]{:S(2)}) collective-permute-start(f32[2,1,128]{2,1,0:T(1,128)S(1)} %get-tuple-element.24), channel_id=1, source_target_pairs={{0,2},{1,3},{2,0},{3,1},{4,6},{5,7},{6,4},{7,5},{8,10},{9,11},{10,... | collective-permute-start | bytes 3080 | tf_op jit(solution)/shard_map/ppermute | solution.py:378
  115.9 1.5 collective-permute-done.18
  117.4 1.4 collective-permute-done.19
  118.9 2.1 %collective-permute-start.20 = (f32[2,1,128]{2,1,0:T(1,128)S(1)}, f32[2,1,128]{2,1,0:T(1,128)S(1)}, u32[]{:S(2)}, u32[]{:S(2)}) collective-permute-start(f32[2,1,128]{2,1,0:T(1,128)S(1)} %add_add_fusion.1), channel_id=1, source_target_pairs={{0,4},{1,5},{2,6},{3,7},{4,0},{5,1},{6,2},{7,3},{8,12},{9,13},{10,... | collective-permute-start | bytes 3080 | tf_op jit(solution)/shard_map/ppermute | solution.py:378
  121.0 2.0 %collective-permute-start.21 = (f32[2,1,128]{2,1,0:T(1,128)S(1)}, f32[2,1,128]{2,1,0:T(1,128)S(1)}, u32[]{:S(2)}, u32[]{:S(2)}) collective-permute-start(f32[2,1,128]{2,1,0:T(1,128)S(1)} %add_add_fusion.1), channel_id=1, source_target_pairs={{0,8},{1,9},{2,10},{3,11},{4,12},{5,13},{6,14},{7,15},{8,0},{9,1},... | collective-permute-start | bytes 3080 | tf_op jit(solution)/shard_map/ppermute | solution.py:378
  123.0 2.4 %collective-permute-start.22 = (f32[2,1,128]{2,1,0:T(1,128)S(1)}, f32[2,1,128]{2,1,0:T(1,128)S(1)}, u32[]{:S(2)}, u32[]{:S(2)}) collective-permute-start(f32[2,1,128]{2,1,0:T(1,128)S(1)} %add_add_fusion.1), channel_id=1, source_target_pairs={{0,12},{1,13},{2,14},{3,15},{4,8},{5,9},{6,10},{7,11},{8,4},{9,5},... | collective-permute-start | bytes 3080 | tf_op jit(solution)/shard_map/ppermute | solution.py:378
  126.1 2.4 %collective-permute-done.21 = f32[2,1,128]{2,1,0:T(1,128)S(1)} collective-permute-done((f32[2,1,128]{2,1,0:T(1,128)S(1)}, f32[2,1,128]{2,1,0:T(1,128)S(1)}, u32[]{:S(2)}, u32[]{:S(2)}) %collective-permute-start.21) | collective-permute-done | bytes 1056 | tf_op jit(solution)/shard_map/ppermute | solution.py:378
  128.4 0.2 collective-permute-done.22
  128.6 3.0 %shard_map.77 = s16[16,656,128]{2,1,0:T(8,128)(2,1)S(1)} custom-call(f32[1]{0:T(128)S(6)} %copy.10.clip_ref, f32[2,1,128]{2,1,0:T(1,128)S(1)} %add_add_fusion.shares_ref, f32[2,512,2560]{2,1,0:T(8,128)S(1)} %get-tuple-element.25.wide_ref.thin_ref, f32[2,512,2560]{2,1,0:T(8,128)S(1)} %get-tuple-element.25.wide_ref.thin_ref, ...), custom_call_target="tpu_custom_call" | custom-call | flops 1 | bytes 1 | tf_op jit(solution)/shard_map/pallas_call | solution.py:280
  131.7 40.7 %all_to_all.10.clipped_ref = s16[16,656,128]{2,1,0:T(8,128)(2,1)} all-to-all(s16[16,656,128]{2,1,0:T(8,128)(2,1)S(1)} %shard_map.77), channel_id=1, replica_groups=mesh['dp'=16,'tensor'=16] {'dp'}, dimensions={0} | all-to-all | bytes 5373952 | tf_op jit(solution)/shard_map/all_to_all | solution.py:408
  172.4 4.6 %shard_map.78 = f32[256,512]{1,0:T(8,128)} custom-call(s16[16,2,384,128]{3,2,1,0:T(8,128)(2,1)} %all-to-all-done.raw_ref, s16[16,656,128]{2,1,0:T(8,128)(2,1)} %all_to_all.10.clipped_ref, f32[256,512]{1,0:T(8,128)} %noise_ref.1), custom_call_target="tpu_custom_call" | custom-call | tf_op jit(solution)/shard_map/pallas_call | solution.py:353
  (52 shorter events, 0.1 us)
Async XLA Ops:
  6.5 96.8 %all-gather.3.cloned.1.call-start = ((), (), s32[]{:S(2)}) async-start(), calls=%async_computation.2 | async-start | bytes 11141120 | tf_op jit(solution)/shard_map/all_gather | solution.py:393
  8.6 11.1 %collective-permute-start = (bf16[2,64,1536]{2,1,0:T(8,128)(2,1)}, bf16[2,64,1536]{2,1,0:T(8,128)(2,1)S(1)}, u32[]{:S(2)}, u32[]{:S(2)}) collective-permute-start(bf16[2,64,1536]{2,1,0:T(8,128)(2,1)} %bitcast.10), channel_id=1, source_target_pairs={{0,2},{1,3},{2,4},{3,5},{4,6},{5,7},{6,8},{7,9},{8,10},{9,11},{10,... | collective-permute-start | bytes 1179656 | tf_op jit(solution)/shard_map/ppermute | solution.py:375
  10.5 11.1 %collective-permute-start.2 = (bf16[2,64,1536]{2,1,0:T(8,128)(2,1)}, bf16[2,64,1536]{2,1,0:T(8,128)(2,1)S(1)}, u32[]{:S(2)}, u32[]{:S(2)}) collective-permute-start(bf16[2,64,1536]{2,1,0:T(8,128)(2,1)} %bitcast.11), channel_id=1, source_target_pairs={{0,14},{1,15},{2,0},{3,1},{4,2},{5,3},{6,4},{7,5},{8,6},{9,7},{10,... | collective-permute-start | bytes 1179656 | tf_op jit(solution)/shard_map/ppermute | solution.py:375
  19.6 16.4 %copy-start.4 = (bf16[2,64,1536]{2,1,0:T(8,128)(2,1)}, bf16[2,64,1536]{2,1,0:T(8,128)(2,1)S(1)}, u32[]{:S(2)}) copy-start(bf16[2,64,1536]{2,1,0:T(8,128)(2,1)S(1)} %collective-permute-done.refs_2_) | copy-start | bytes 1179652
  19.6 12.9 %collective-permute-start.1 = (bf16[2,64,1536]{2,1,0:T(8,128)(2,1)S(1)}, bf16[2,64,1536]{2,1,0:T(8,128)(2,1)}, u32[]{:S(2)}, u32[]{:S(2)}) collective-permute-start(bf16[2,64,1536]{2,1,0:T(8,128)(2,1)S(1)} %collective-permute-done.refs_2_), channel_id=1, source_target_pairs={{0,2},{1,3},{2,4},{3,5},{4,6},{5,7},{6,8},{7,9},{8,10},{9,11},{10,... | collective-permute-start | bytes 1179656 | tf_op jit(solution)/shard_map/ppermute | solution.py:375
  21.6 14.9 %copy-start.5 = (bf16[2,64,1536]{2,1,0:T(8,128)(2,1)}, bf16[2,64,1536]{2,1,0:T(8,128)(2,1)S(1)}, u32[]{:S(2)}) copy-start(bf16[2,64,1536]{2,1,0:T(8,128)(2,1)S(1)} %collective-permute-done.2.refs_4_) | copy-start | bytes 1179652
  21.6 11.4 %collective-permute-start.3 = (bf16[2,64,1536]{2,1,0:T(8,128)(2,1)S(1)}, bf16[2,64,1536]{2,1,0:T(8,128)(2,1)}, u32[]{:S(2)}, u32[]{:S(2)}) collective-permute-start(bf16[2,64,1536]{2,1,0:T(8,128)(2,1)S(1)} %collective-permute-done.2.refs_4_), channel_id=1, source_target_pairs={{0,14},{1,15},{2,0},{3,1},{4,2},{5,3},{6,4},{7,5},{8,6},{9,7},{10,... | collective-permute-start | bytes 1179656 | tf_op jit(solution)/shard_map/ppermute | solution.py:375
  30.2 5.8 %copy-start.1 = (bf16[128,1536]{1,0:T(8,128)(2,1)S(1)}, bf16[128,1536]{1,0:T(8,128)(2,1)}, u32[]{:S(2)}) copy-start(bf16[128,1536]{1,0:T(8,128)(2,1)} %shard_map.73) | copy-start | bytes 1179652
  33.0 10.5 %collective-permute-start.9 = (bf16[2,64,1536]{2,1,0:T(8,128)(2,1)}, bf16[2,64,1536]{2,1,0:T(8,128)(2,1)S(1)}, u32[]{:S(2)}, u32[]{:S(2)}) collective-permute-start(bf16[2,64,1536]{2,1,0:T(8,128)(2,1)} %collective-permute-done.1.refs_6_), channel_id=1, source_target_pairs={{0,2},{1,3},{2,4},{3,5},{4,6},{5,7},{6,8},{7,9},{8,10},{9,11},{10,... | collective-permute-start | bytes 1179656 | tf_op jit(solution)/shard_map/ppermute | solution.py:375
  36.0 9.9 %collective-permute-start.11 = (bf16[2,64,1536]{2,1,0:T(8,128)(2,1)}, bf16[2,64,1536]{2,1,0:T(8,128)(2,1)S(1)}, u32[]{:S(2)}, u32[]{:S(2)}) collective-permute-start(bf16[2,64,1536]{2,1,0:T(8,128)(2,1)} %collective-permute-done.3.refs_8_), channel_id=1, source_target_pairs={{0,14},{1,15},{2,0},{3,1},{4,2},{5,3},{6,4},{7,5},{8,6},{9,7},{10,... | collective-permute-start | bytes 1179656 | tf_op jit(solution)/shard_map/ppermute | solution.py:375
  36.0 9.9 %collective-permute-start.4 = (bf16[2,64,1536]{2,1,0:T(8,128)(2,1)S(1)}, bf16[2,64,1536]{2,1,0:T(8,128)(2,1)S(1)}, u32[]{:S(2)}, u32[]{:S(2)}) collective-permute-start(bf16[2,64,1536]{2,1,0:T(8,128)(2,1)S(1)} %bitcast.13), channel_id=1, source_target_pairs={{0,1},{1,0},{2,3},{3,2},{4,5},{5,4},{6,7},{7,6},{8,9},{9,8},{10,11... | collective-permute-start | bytes 1179656 | tf_op jit(solution)/shard_map/ppermute | solution.py:378
  36.0 11.8 %collective-permute-start.5 = (bf16[2,64,1536]{2,1,0:T(8,128)(2,1)S(1)}, bf16[2,64,1536]{2,1,0:T(8,128)(2,1)S(1)}, u32[]{:S(2)}, u32[]{:S(2)}) collective-permute-start(bf16[2,64,1536]{2,1,0:T(8,128)(2,1)S(1)} %collective-permute-done.refs_2_), channel_id=1, source_target_pairs={{0,1},{1,0},{2,3},{3,2},{4,5},{5,4},{6,7},{7,6},{8,9},{9,8},{10,11... | collective-permute-start | bytes 1179656 | tf_op jit(solution)/shard_map/ppermute | solution.py:378
  36.5 11.6 %collective-permute-start.6 = (bf16[2,64,1536]{2,1,0:T(8,128)(2,1)S(1)}, bf16[2,64,1536]{2,1,0:T(8,128)(2,1)S(1)}, u32[]{:S(2)}, u32[]{:S(2)}) collective-permute-start(bf16[2,64,1536]{2,1,0:T(8,128)(2,1)S(1)} %collective-permute-done.2.refs_4_), channel_id=1, source_target_pairs={{0,1},{1,0},{2,3},{3,2},{4,5},{5,4},{6,7},{7,6},{8,9},{9,8},{10,11... | collective-permute-start | bytes 1179656 | tf_op jit(solution)/shard_map/ppermute | solution.py:378
  43.4 17.5 %copy-start.2 = (bf16[2,64,1536]{2,1,0:T(8,128)(2,1)}, bf16[2,64,1536]{2,1,0:T(8,128)(2,1)S(1)}, u32[]{:S(2)}) copy-start(bf16[2,64,1536]{2,1,0:T(8,128)(2,1)S(1)} %collective-permute-done.9.refs_10_) | copy-start | bytes 1179652
  43.4 4.7 %collective-permute-start.7 = (bf16[2,64,1536]{2,1,0:T(8,128)(2,1)}, bf16[2,64,1536]{2,1,0:T(8,128)(2,1)S(1)}, u32[]{:S(2)}, u32[]{:S(2)}) collective-permute-start(bf16[2,64,1536]{2,1,0:T(8,128)(2,1)} %collective-permute-done.1.refs_6_), channel_id=1, source_target_pairs={{0,1},{1,0},{2,3},{3,2},{4,5},{5,4},{6,7},{7,6},{8,9},{9,8},{10,11... | collective-permute-start | bytes 1179656 | tf_op jit(solution)/shard_map/ppermute | solution.py:378
  45.9 15.1 %copy-start.3 = (bf16[2,64,1536]{2,1,0:T(8,128)(2,1)}, bf16[2,64,1536]{2,1,0:T(8,128)(2,1)S(1)}, u32[]{:S(2)}) copy-start(bf16[2,64,1536]{2,1,0:T(8,128)(2,1)S(1)} %collective-permute-done.11.refs_12_) | copy-start | bytes 1179652
  45.9 13.6 %collective-permute-start.8 = (bf16[2,64,1536]{2,1,0:T(8,128)(2,1)}, bf16[2,64,1536]{2,1,0:T(8,128)(2,1)S(1)}, u32[]{:S(2)}, u32[]{:S(2)}) collective-permute-start(bf16[2,64,1536]{2,1,0:T(8,128)(2,1)} %collective-permute-done.3.refs_8_), channel_id=1, source_target_pairs={{0,1},{1,0},{2,3},{3,2},{4,5},{5,4},{6,7},{7,6},{8,9},{9,8},{10,11... | collective-permute-start | bytes 1179656 | tf_op jit(solution)/shard_map/ppermute | solution.py:378
  46.0 15.0 %copy-start.6 = (bf16[2,64,1536]{2,1,0:T(8,128)(2,1)}, bf16[2,64,1536]{2,1,0:T(8,128)(2,1)S(1)}, u32[]{:S(2)}) copy-start(bf16[2,64,1536]{2,1,0:T(8,128)(2,1)S(1)} %collective-permute-done.4.refs_1_) | copy-start | bytes 1179652
  46.0 11.8 %collective-permute-start.13 = (bf16[1,64,1536]{2,1,0:T(8,128)(2,1)S(1)}, bf16[1,64,1536]{2,1,0:T(8,128)(2,1)S(1)}, u32[]{:S(2)}, u32[]{:S(2)}) collective-permute-start(bf16[1,64,1536]{2,1,0:T(8,128)(2,1)S(1)} %slice.8), channel_id=1, source_target_pairs={{0,2},{1,3},{2,4},{3,5},{4,6},{5,7},{6,8},{7,9},{8,10},{9,11},{10,... | collective-permute-start | bytes 589832 | tf_op jit(solution)/shard_map/ppermute | solution.py:375
  47.8 13.2 %copy-start.7 = (bf16[2,64,1536]{2,1,0:T(8,128)(2,1)}, bf16[2,64,1536]{2,1,0:T(8,128)(2,1)S(1)}, u32[]{:S(2)}) copy-start(bf16[2,64,1536]{2,1,0:T(8,128)(2,1)S(1)} %collective-permute-done.5.refs_3_) | copy-start | bytes 1179652
  47.8 11.7 %collective-permute-start.15 = (bf16[1,64,1536]{2,1,0:T(8,128)(2,1)S(1)}, bf16[1,64,1536]{2,1,0:T(8,128)(2,1)S(1)}, u32[]{:S(2)}, u32[]{:S(2)}) collective-permute-start(bf16[1,64,1536]{2,1,0:T(8,128)(2,1)S(1)} %slice.9), channel_id=1, source_target_pairs={{0,14},{1,15},{2,0},{3,1},{4,2},{5,3},{6,4},{7,5},{8,6},{9,7},{10,... | collective-permute-start | bytes 589832 | tf_op jit(solution)/shard_map/ppermute | solution.py:375
  48.1 12.9 %copy-start.8 = (bf16[2,64,1536]{2,1,0:T(8,128)(2,1)}, bf16[2,64,1536]{2,1,0:T(8,128)(2,1)S(1)}, u32[]{:S(2)}) copy-start(bf16[2,64,1536]{2,1,0:T(8,128)(2,1)S(1)} %collective-permute-done.6.refs_5_) | copy-start | bytes 1179652
  48.1 12.9 %collective-permute-start.10 = (bf16[2,64,1536]{2,1,0:T(8,128)(2,1)S(1)}, bf16[2,64,1536]{2,1,0:T(8,128)(2,1)S(1)}, u32[]{:S(2)}, u32[]{:S(2)}) collective-permute-start(bf16[2,64,1536]{2,1,0:T(8,128)(2,1)S(1)} %collective-permute-done.9.refs_10_), channel_id=1, source_target_pairs={{0,1},{1,0},{2,3},{3,2},{4,5},{5,4},{6,7},{7,6},{8,9},{9,8},{10,11... | collective-permute-start | bytes 1179656 | tf_op jit(solution)/shard_map/ppermute | solution.py:378
  48.1 12.9 %copy-start.9 = (bf16[2,64,1536]{2,1,0:T(8,128)(2,1)}, bf16[2,64,1536]{2,1,0:T(8,128)(2,1)S(1)}, u32[]{:S(2)}) copy-start(bf16[2,64,1536]{2,1,0:T(8,128)(2,1)S(1)} %collective-permute-done.7.refs_7_) | copy-start | bytes 1179652
  48.1 12.8 %collective-permute-start.12 = (bf16[2,64,1536]{2,1,0:T(8,128)(2,1)S(1)}, bf16[2,64,1536]{2,1,0:T(8,128)(2,1)S(1)}, u32[]{:S(2)}, u32[]{:S(2)}) collective-permute-start(bf16[2,64,1536]{2,1,0:T(8,128)(2,1)S(1)} %collective-permute-done.11.refs_12_), channel_id=1, source_target_pairs={{0,1},{1,0},{2,3},{3,2},{4,5},{5,4},{6,7},{7,6},{8,9},{9,8},{10,11... | collective-permute-start | bytes 1179656 | tf_op jit(solution)/shard_map/ppermute | solution.py:378
  57.8 3.2 %copy-start.13 = (bf16[1,64,1536]{2,1,0:T(8,128)(2,1)}, bf16[1,64,1536]{2,1,0:T(8,128)(2,1)S(1)}, u32[]{:S(2)}) copy-start(bf16[1,64,1536]{2,1,0:T(8,128)(2,1)S(1)} %collective-permute-done.13.refs_14_) | copy-start | bytes 589828
  57.8 1.7 collective-permute-start.14
  59.5 1.5 copy-start.14
  59.5 1.4 collective-permute-start.16
  59.5 1.5 copy-start.10
  59.6 1.5 copy-start.15
  61.0 0.7 copy-start.16
  61.0 0.8 copy-start.11
  61.8 0.7 copy-start.12
  72.7 59.0 %all-to-all-start = ((s16[16,2,384,128]{3,2,1,0:T(8,128)(2,1)}), s16[16,2,384,128]{3,2,1,0:T(8,128)(2,1)}, u32[]{:S(2)}, u32[]{:S(2)}) async-start(s16[16,2,384,128]{3,2,1,0:T(8,128)(2,1)} %get-tuple-element.28), calls=%async_computation | async-start | bytes 6291456 | tf_op jit(solution)/shard_map/all_to_all | solution.py:402
  103.4 25.3 %copy-start = (f32[16,2,8,128]{3,2,1,0:T(8,128)S(1)}, f32[16,2,8,128]{3,2,1,0:T(8,128)}, u32[]{:S(2)}) copy-start(f32[16,2,8,128]{3,2,1,0:T(8,128)} %get-tuple-element.27.exponent_ref) | copy-start | bytes 393220
  113.2 2.7 %collective-permute-start.17 = (f32[2,1,128]{2,1,0:T(1,128)S(1)}, f32[2,1,128]{2,1,0:T(1,128)S(1)}, u32[]{:S(2)}, u32[]{:S(2)}) collective-permute-start(f32[2,1,128]{2,1,0:T(1,128)S(1)} %get-tuple-element.24), channel_id=1, source_target_pairs={{0,1},{1,0},{2,3},{3,2},{4,5},{5,4},{6,7},{7,6},{8,9},{9,8},{10,11... | collective-permute-start | bytes 3080 | tf_op jit(solution)/shard_map/ppermute | solution.py:378
  113.5 3.9 %collective-permute-start.18 = (f32[2,1,128]{2,1,0:T(1,128)S(1)}, f32[2,1,128]{2,1,0:T(1,128)S(1)}, u32[]{:S(2)}, u32[]{:S(2)}) collective-permute-start(f32[2,1,128]{2,1,0:T(1,128)S(1)} %get-tuple-element.24), channel_id=1, source_target_pairs={{0,2},{1,3},{2,0},{3,1},{4,6},{5,7},{6,4},{7,5},{8,10},{9,11},{10,... | collective-permute-start | bytes 3080 | tf_op jit(solution)/shard_map/ppermute | solution.py:378
  115.9 3.0 %collective-permute-start.19 = (f32[2,1,128]{2,1,0:T(1,128)S(1)}, f32[2,1,128]{2,1,0:T(1,128)S(1)}, u32[]{:S(2)}, u32[]{:S(2)}) collective-permute-start(f32[2,1,128]{2,1,0:T(1,128)S(1)} %get-tuple-element.24), channel_id=1, source_target_pairs={{0,3},{1,2},{2,1},{3,0},{4,7},{5,6},{6,5},{7,4},{8,11},{9,10},{10,... | collective-permute-start | bytes 3080 | tf_op jit(solution)/shard_map/ppermute | solution.py:378
  118.9 7.2 %collective-permute-start.20 = (f32[2,1,128]{2,1,0:T(1,128)S(1)}, f32[2,1,128]{2,1,0:T(1,128)S(1)}, u32[]{:S(2)}, u32[]{:S(2)}) collective-permute-start(f32[2,1,128]{2,1,0:T(1,128)S(1)} %add_add_fusion.1), channel_id=1, source_target_pairs={{0,4},{1,5},{2,6},{3,7},{4,0},{5,1},{6,2},{7,3},{8,12},{9,13},{10,... | collective-permute-start | bytes 3080 | tf_op jit(solution)/shard_map/ppermute | solution.py:378
  121.0 7.5 %collective-permute-start.21 = (f32[2,1,128]{2,1,0:T(1,128)S(1)}, f32[2,1,128]{2,1,0:T(1,128)S(1)}, u32[]{:S(2)}, u32[]{:S(2)}) collective-permute-start(f32[2,1,128]{2,1,0:T(1,128)S(1)} %add_add_fusion.1), channel_id=1, source_target_pairs={{0,8},{1,9},{2,10},{3,11},{4,12},{5,13},{6,14},{7,15},{8,0},{9,1},... | collective-permute-start | bytes 3080 | tf_op jit(solution)/shard_map/ppermute | solution.py:378
  123.0 5.7 %collective-permute-start.22 = (f32[2,1,128]{2,1,0:T(1,128)S(1)}, f32[2,1,128]{2,1,0:T(1,128)S(1)}, u32[]{:S(2)}, u32[]{:S(2)}) collective-permute-start(f32[2,1,128]{2,1,0:T(1,128)S(1)} %add_add_fusion.1), channel_id=1, source_target_pairs={{0,12},{1,13},{2,14},{3,15},{4,8},{5,9},{6,10},{7,11},{8,4},{9,5},... | collective-permute-start | bytes 3080 | tf_op jit(solution)/shard_map/ppermute | solution.py:378
Sparse Core Ops, SparseCore 0:
  33.1 70.2 all-gather.2

commit v7 on v6

--- a/solution.py
+++ b/solution.py
@@ -12,6 +12,7 @@
 TOGETHER = 8
 LEAST = 1e-33
 CHUNK = 256
+WIDER = 640
 PARAMS = pltpu.CompilerParams(vmem_limit_bytes=56 * 1024 * 1024)
 LESS = pltpu.CompilerParams(vmem_limit_bytes=28 * 1024 * 1024)
 RAW = ((0, 64), (64, 32))
@@ -194,9 +195,9 @@
 
     slot = (example * tiles + tile) % 2
     share = share_ref[0]
-    for at in range(0, width, CHUNK):
-        here = slice(at, at + CHUNK)
-        some = acts[slot, :, :, here].reshape(devices * shard, CHUNK)
+    for at in range(0, width, WIDER):
+        here = slice(at, at + WIDER)
+        some = acts[slot, :, :, here].reshape(devices * shard, WIDER)
         product = jnp.dot(grads[example], some, preferred_element_type=jnp.float32)
         product_ref[0, :, here] = product
         top_ref[0, :, here] = tops(product)
@@ -401,8 +402,9 @@
     raw, exponents, squares = raw_products(order, pieces, masked)
     raw = lax.all_to_all(raw, "dp", 0, 0)
     products, top, share = plain_products(second, masked, squares)
-    share = share + crossed(share, 1) + crossed(share, 2) + crossed(share, 3)
-    share = share + crossed(share, 4) + crossed(share, 8) + crossed(share, 12)
+    share = share + crossed(share, 1)
+    for k in (1, 2, 4):
+        share = share + along_z(share, k)
     clipped = clipped_sums(clip_bound, share, products, top, exponents)
     clipped, raw = lax.optimization_barrier((clipped, raw))
     clipped = lax.all_to_all(clipped, "dp", 0, 0)

time: 184 us -> 188 us (1.022)
  waiting for transfers between devices: 60.3 us -> 63.5 us
    ppermute x15 -> x10, starting transfers between devices: 10.3 us -> 1.45 us  [crossed(): return lax.ppermute(x, 'tensor', [(t, t ^ k) for t in range(devices)])]
    ppermute x8 -> x11, starting transfers between devices: 11.4 us -> 20.1 us  [along_z(): lax.ppermute(x, 'tensor', [(t, (t + 2 * k) % devices) for t in range(devi...]
    ppermute x8 -> x11, waiting for transfers between devices: 29.8 us -> 37.5 us  [along_z(): lax.ppermute(x, 'tensor', [(t, (t + 2 * k) % devices) for t in range(devi...]
    ppermute x15 -> x10, waiting for transfers between devices: 6.99 us -> 2.32 us  [crossed(): return lax.ppermute(x, 'tensor', [(t, t ^ k) for t in range(devices)])]
  transfers between devices with their start and end apart: 25 -> 23, of which waited for: 13 -> 13; matrix products, arithmetic and copies ran while one was open for 4% -> 3% of each run, Pallas kernels for 14% -> 14%
where the time goes in v7:
time: 188 us; the launch traced here: 186 us
  waiting for transfers between devices  63.5 us (34%)
  blocking collectives  39.2 us (21%)
  Pallas kernels  32.6 us (17%)
  starting transfers between devices  28.7 us (15%)
  between operations  14.3 us (8%)
  local copies, waits for them, and re-layouts  4.52 us (2%)
  other arithmetic  3.45 us (2%)
    all_to_all x1, blocking collectives, per_device(): clipped = lax.all_to_all(clipped, 'dp', 0, 0)  39.2 us
    ppermute x11, waiting for transfers between devices, along_z(): lax.ppermute(x, 'tensor', [(t, (t + 2 * k) % devices) for t in range(devi...  37.5 us
    all_gather x1, waiting for transfers between devices, per_device(): second = lax.all_gather(second, 'tensor')  23.7 us
    ppermute x11, starting transfers between devices, along_z(): lax.ppermute(x, 'tensor', [(t, (t + 2 * k) % devices) for t in range(devi...  20.1 us
    pallas_call x1, Pallas kernels, plain_products(): pl.pallas_call(plain_kernel, grid=(examples, features // width), in_specs...  10.8 us
    pallas_call x1, Pallas kernels, raw_products(): pl.pallas_call(raw_kernel, grid=(examples,), in_specs=[pl.BlockSpec(memor...  10 us
    all_to_all x1, starting transfers between devices, per_device(): raw = lax.all_to_all(raw, 'dp', 0, 0)  7.13 us
    pallas_call x1, Pallas kernels, finish(): pl.pallas_call(functools.partial(finish_kernel, scale), grid=(groups // T...  4.6 us
  transfers between devices with their start and end apart: 23, of which 13 were waited for; matrix products, arithmetic and copies ran while one was open for 3% of the time, Pallas kernels for 14%

profile of v7, /device:TPU:32, one launch (start us, length us, event | category | flops | bytes accessed | tf_op | source)
XLA Modules:
  0.0 186.1 jit_solution(10686810280445971082)
XLA Ops:
  6.5 2.0 %shard_map.73 = bf16[128,1536]{1,0:T(8,128)(2,1)} custom-call(bf16[128,4096]{1,0:T(8,128)(2,1)} %bitcast.7), custom_call_target="tpu_custom_call" | custom-call | tf_op jit(solution)/shard_map/pallas_call | solution.py:38
  8.6 1.9 %collective-permute-start = (bf16[2,64,1536]{2,1,0:T(8,128)(2,1)}, bf16[2,64,1536]{2,1,0:T(8,128)(2,1)S(1)}, u32[]{:S(2)}, u32[]{:S(2)}) collective-permute-start(bf16[2,64,1536]{2,1,0:T(8,128)(2,1)} %bitcast.10), channel_id=1, source_target_pairs={{0,2},{1,3},{2,4},{3,5},{4,6},{5,7},{6,8},{7,9},{8,10},{9,11},{10,... | collective-permute-start | bytes 1179656 | tf_op jit(solution)/shard_map/ppermute | solution.py:376
  10.5 0.1 collective-permute-start.2
  10.6 0.7 iota_compare_fusion
  11.3 8.3 %collective-permute-done.refs_2_ = bf16[2,64,1536]{2,1,0:T(8,128)(2,1)S(1)} collective-permute-done((bf16[2,64,1536]{2,1,0:T(8,128)(2,1)}, bf16[2,64,1536]{2,1,0:T(8,128)(2,1)S(1)}, u32[]{:S(2)}, u32[]{:S(2)}) %collective-permute-start) | collective-permute-done | bytes 393248 | tf_op jit(solution)/shard_map/ppermute | solution.py:376
  19.6 1.9 %collective-permute-start.1 = (bf16[2,64,1536]{2,1,0:T(8,128)(2,1)S(1)}, bf16[2,64,1536]{2,1,0:T(8,128)(2,1)}, u32[]{:S(2)}, u32[]{:S(2)}) collective-permute-start(bf16[2,64,1536]{2,1,0:T(8,128)(2,1)S(1)} %collective-permute-done.refs_2_), channel_id=1, source_target_pairs={{0,2},{1,3},{2,4},{3,5},{4,6},{5,7},{6,8},{7,9},{8,10},{9,11},{10,... | collective-permute-start | bytes 1179656 | tf_op jit(solution)/shard_map/ppermute | solution.py:376
  21.6 2.4 %collective-permute-start.3 = (bf16[2,64,1536]{2,1,0:T(8,128)(2,1)S(1)}, bf16[2,64,1536]{2,1,0:T(8,128)(2,1)}, u32[]{:S(2)}, u32[]{:S(2)}) collective-permute-start(bf16[2,64,1536]{2,1,0:T(8,128)(2,1)S(1)} %collective-permute-done.2.refs_4_), channel_id=1, source_target_pairs={{0,14},{1,15},{2,0},{3,1},{4,2},{5,3},{6,4},{7,5},{8,6},{9,7},{10,... | collective-permute-start | bytes 1179656 | tf_op jit(solution)/shard_map/ppermute | solution.py:376
  24.0 1.2 add_and_fusion.order_ref
  25.2 2.0 %shard_map.74 = bf16[128,2560]{1,0:T(8,128)(2,1)} custom-call(bf16[128,4096]{1,0:T(8,128)(2,1)} %bitcast.8), custom_call_target="tpu_custom_call" | custom-call | tf_op jit(solution)/shard_map/pallas_call | solution.py:38
  27.2 3.0 %copy.9 = bf16[2,1024,512]{1,2,0:T(8,128)(2,1)S(1)} copy(bf16[2,1024,512]{2,1,0:T(8,128)(2,1)} %param.8) | data formatting | bytes 4194304 | tf_op args[1]
  30.2 0.0 copy-start.1
  30.2 1.5 select_bitcast_fusion.refs_18_.grads_ref
  31.7 0.8 collective-permute-done.1.refs_6_
  32.5 0.4 collective-permute-done.3.refs_8_
  33.0 0.0 all-gather.3.cloned.1.call-update
  33.0 3.0 %collective-permute-start.9 = (bf16[2,64,1536]{2,1,0:T(8,128)(2,1)}, bf16[2,64,1536]{2,1,0:T(8,128)(2,1)S(1)}, u32[]{:S(2)}, u32[]{:S(2)}) collective-permute-start(bf16[2,64,1536]{2,1,0:T(8,128)(2,1)} %collective-permute-done.1.refs_6_), channel_id=1, source_target_pairs={{0,2},{1,3},{2,4},{3,5},{4,6},{5,7},{6,8},{7,9},{8,10},{9,11},{10,... | collective-permute-start | bytes 1179656 | tf_op jit(solution)/shard_map/ppermute | solution.py:376
  36.0 0.0 collective-permute-start.11
  36.0 0.5 collective-permute-start.5
  36.5 0.1 collective-permute-start.6
  36.6 6.8 %collective-permute-done.9.refs_10_ = bf16[2,64,1536]{2,1,0:T(8,128)(2,1)S(1)} collective-permute-done((bf16[2,64,1536]{2,1,0:T(8,128)(2,1)}, bf16[2,64,1536]{2,1,0:T(8,128)(2,1)S(1)}, u32[]{:S(2)}, u32[]{:S(2)}) %collective-permute-start.9) | collective-permute-done | bytes 393248 | tf_op jit(solution)/shard_map/ppermute | solution.py:376
  43.4 0.0 collective-permute-start.7
  43.5 2.5 %collective-permute-done.11.refs_12_ = bf16[2,64,1536]{2,1,0:T(8,128)(2,1)S(1)} collective-permute-done((bf16[2,64,1536]{2,1,0:T(8,128)(2,1)}, bf16[2,64,1536]{2,1,0:T(8,128)(2,1)S(1)}, u32[]{:S(2)}, u32[]{:S(2)}) %collective-permute-start.11) | collective-permute-done | bytes 393248 | tf_op jit(solution)/shard_map/ppermute | solution.py:376
  46.0 1.8 collective-permute-start.13
  47.8 0.3 collective-permute-start.15
  48.1 0.1 collective-permute-start.10
  48.1 0.5 collective-permute-start.12
  48.6 9.2 %collective-permute-done.13.refs_14_ = bf16[1,64,1536]{2,1,0:T(8,128)(2,1)S(1)} collective-permute-done((bf16[1,64,1536]{2,1,0:T(8,128)(2,1)S(1)}, bf16[1,64,1536]{2,1,0:T(8,128)(2,1)S(1)}, u32[]{:S(2)}, u32[]{:S(2)}) %collective-permute-start.13) | collective-permute-done | bytes 196640 | tf_op jit(solution)/shard_map/ppermute | solution.py:376
  57.8 1.7 collective-permute-done.15.refs_16_
  59.5 0.0 collective-permute-start.16
  59.6 1.4 collective-permute-done.16.refs_17_
  61.1 0.6 copy-done.16
  61.7 0.1 copy-done.11
  61.8 0.7 copy-done.12
  62.5 10.0 %shard_map.75 = (s16[16,2,384,128]{3,2,1,0:T(8,128)(2,1)}, f32[16,2,8,128]{3,2,1,0:T(8,128)}, f32[2,1,128]{2,1,0:T(1,128)}) custom-call(s32[16]{0:T(128)} %add_and_fusion.order_ref, bf16[2,64,1536]{2,1,0:T(8,128)(2,1)} %bitcast.12, bf16[2,64,1536]{2,1,0:T(8,128)(2,1)} %copy-done.6, bf16[2,64,1536]{2,1,0:T(8,128)(2,1)} %copy-done.4, ...), custom_call_target="tpu_custom_call" | custom-call | tf_op jit(solution)/shard_map/pallas_call | solution.py:140
  72.6 7.1 %all-to-all-start = ((s16[16,2,384,128]{3,2,1,0:T(8,128)(2,1)}), s16[16,2,384,128]{3,2,1,0:T(8,128)(2,1)}, u32[]{:S(2)}, u32[]{:S(2)}) async-start(s16[16,2,384,128]{3,2,1,0:T(8,128)(2,1)} %get-tuple-element.28), calls=%async_computation | async-start | bytes 6291456 | tf_op jit(solution)/shard_map/all_to_all | solution.py:403
  79.7 23.7 %all-gather.3.cloned.1.call-done = bf16[32,64,2560]{2,1,0:T(8,128)(2,1)} async-done(((bf16[2,64,2560]{2,1,0:T(8,128)(2,1)}), bf16[32,64,2560]{2,1,0:T(8,128)(2,1)}) %all-gather.3.cloned.1.call-update) | async-done | bytes 10485776 | tf_op jit(solution)/shard_map/all_gather | solution.py:394
  103.4 10.8 %shard_map.76 = (f32[2,512,2560]{2,1,0:T(8,128)S(1)}, f32[2,1,2560]{2,1,0:T(1,128)S(1)}, f32[2,1,128]{2,1,0:T(1,128)S(1)}) custom-call(bf16[16,2,64,2560]{3,2,1,0:T(8,128)(2,1)} %bitcast.6, bf16[2,512,1024]{2,1,0:T(8,128)(2,1)} %select_bitcast_fusion.refs_18_.grads_ref, f32[2,1,128]{2,1,0:T(1,128)} %get-tuple-element.23.squares_ref), custom_call_target="tpu_custom_call" | custom-call | flops 1 | bytes 1 | tf_op jit(solution)/shard_map/pallas_call | solution.py:214
  114.2 0.3 collective-permute-start.17
  114.6 0.9 collective-permute-done.17
  115.5 1.6 collective-permute-start.18
  117.0 2.3 %collective-permute-done.18 = f32[2,1,128]{2,1,0:T(1,128)S(1)} collective-permute-done((f32[2,1,128]{2,1,0:T(1,128)S(1)}, f32[2,1,128]{2,1,0:T(1,128)S(1)}, u32[]{:S(2)}, u32[]{:S(2)}) %collective-permute-start.18) | collective-permute-done | bytes 1056 | tf_op jit(solution)/shard_map/ppermute | solution.py:376
  119.3 3.5 %collective-permute-start.19 = (f32[2,1,128]{2,1,0:T(1,128)S(1)}, f32[2,1,128]{2,1,0:T(1,128)S(1)}, u32[]{:S(2)}, u32[]{:S(2)}) collective-permute-start(f32[2,1,128]{2,1,0:T(1,128)S(1)} %add.25), channel_id=1, source_target_pairs={{0,4},{1,5},{2,6},{3,7},{4,8},{5,9},{6,10},{7,11},{8,12},{9,13},{1... | collective-permute-start | bytes 3080 | tf_op jit(solution)/shard_map/ppermute | solution.py:376
  122.8 2.2 %collective-permute-done.19 = f32[2,1,128]{2,1,0:T(1,128)S(1)} collective-permute-done((f32[2,1,128]{2,1,0:T(1,128)S(1)}, f32[2,1,128]{2,1,0:T(1,128)S(1)}, u32[]{:S(2)}, u32[]{:S(2)}) %collective-permute-start.19) | collective-permute-done | bytes 1056 | tf_op jit(solution)/shard_map/ppermute | solution.py:376
  125.0 3.6 %collective-permute-start.20 = (f32[2,1,128]{2,1,0:T(1,128)S(1)}, f32[2,1,128]{2,1,0:T(1,128)S(1)}, u32[]{:S(2)}, u32[]{:S(2)}) collective-permute-start(f32[2,1,128]{2,1,0:T(1,128)S(1)} %add.26), channel_id=1, source_target_pairs={{0,8},{1,9},{2,10},{3,11},{4,12},{5,13},{6,14},{7,15},{8,0},{9,1},... | collective-permute-start | bytes 3080 | tf_op jit(solution)/shard_map/ppermute | solution.py:376
  129.3 3.2 %collective-permute-done.20 = f32[2,1,128]{2,1,0:T(1,128)S(1)} collective-permute-done((f32[2,1,128]{2,1,0:T(1,128)S(1)}, f32[2,1,128]{2,1,0:T(1,128)S(1)}, u32[]{:S(2)}, u32[]{:S(2)}) %collective-permute-start.20) | collective-permute-done | bytes 1056 | tf_op jit(solution)/shard_map/ppermute | solution.py:376
  132.5 3.0 %shard_map.77 = s16[16,656,128]{2,1,0:T(8,128)(2,1)S(1)} custom-call(f32[1]{0:T(128)S(6)} %copy.10.clip_ref, f32[2,1,128]{2,1,0:T(1,128)S(1)} %add.27.shares_ref, f32[2,512,2560]{2,1,0:T(8,128)S(1)} %get-tuple-element.25.wide_ref.thin_ref, f32[2,512,2560]{2,1,0:T(8,128)S(1)} %get-tuple-element.25.wide_ref.thin_ref, ...), custom_call_target="tpu_custom_call" | custom-call | flops 1 | bytes 1 | tf_op jit(solution)/shard_map/pallas_call | solution.py:281
  135.5 39.2 %all_to_all.10.clipped_ref = s16[16,656,128]{2,1,0:T(8,128)(2,1)} all-to-all(s16[16,656,128]{2,1,0:T(8,128)(2,1)S(1)} %shard_map.77), channel_id=1, replica_groups=mesh['dp'=16,'tensor'=16] {'dp'}, dimensions={0} | all-to-all | bytes 5373952 | tf_op jit(solution)/shard_map/all_to_all | solution.py:410
  174.7 4.6 %shard_map.78 = f32[256,512]{1,0:T(8,128)} custom-call(s16[16,2,384,128]{3,2,1,0:T(8,128)(2,1)} %all-to-all-done.raw_ref, s16[16,656,128]{2,1,0:T(8,128)(2,1)} %all_to_all.10.clipped_ref, f32[256,512]{1,0:T(8,128)} %noise_ref.1), custom_call_target="tpu_custom_call" | custom-call | tf_op jit(solution)/shard_map/pallas_call | solution.py:354
  (50 shorter events, 0.1 us)
Async XLA Ops:
  6.5 96.8 %all-gather.3.cloned.1.call-start = ((), (), s32[]{:S(2)}) async-start(), calls=%async_computation.2 | async-start | bytes 11141120 | tf_op jit(solution)/shard_map/all_gather | solution.py:394
  8.6 11.1 %collective-permute-start = (bf16[2,64,1536]{2,1,0:T(8,128)(2,1)}, bf16[2,64,1536]{2,1,0:T(8,128)(2,1)S(1)}, u32[]{:S(2)}, u32[]{:S(2)}) collective-permute-start(bf16[2,64,1536]{2,1,0:T(8,128)(2,1)} %bitcast.10), channel_id=1, source_target_pairs={{0,2},{1,3},{2,4},{3,5},{4,6},{5,7},{6,8},{7,9},{8,10},{9,11},{10,... | collective-permute-start | bytes 1179656 | tf_op jit(solution)/shard_map/ppermute | solution.py:376
  10.5 11.1 %collective-permute-start.2 = (bf16[2,64,1536]{2,1,0:T(8,128)(2,1)}, bf16[2,64,1536]{2,1,0:T(8,128)(2,1)S(1)}, u32[]{:S(2)}, u32[]{:S(2)}) collective-permute-start(bf16[2,64,1536]{2,1,0:T(8,128)(2,1)} %bitcast.11), channel_id=1, source_target_pairs={{0,14},{1,15},{2,0},{3,1},{4,2},{5,3},{6,4},{7,5},{8,6},{9,7},{10,... | collective-permute-start | bytes 1179656 | tf_op jit(solution)/shard_map/ppermute | solution.py:376
  19.6 16.4 %copy-start.4 = (bf16[2,64,1536]{2,1,0:T(8,128)(2,1)}, bf16[2,64,1536]{2,1,0:T(8,128)(2,1)S(1)}, u32[]{:S(2)}) copy-start(bf16[2,64,1536]{2,1,0:T(8,128)(2,1)S(1)} %collective-permute-done.refs_2_) | copy-start | bytes 1179652
  19.6 12.9 %collective-permute-start.1 = (bf16[2,64,1536]{2,1,0:T(8,128)(2,1)S(1)}, bf16[2,64,1536]{2,1,0:T(8,128)(2,1)}, u32[]{:S(2)}, u32[]{:S(2)}) collective-permute-start(bf16[2,64,1536]{2,1,0:T(8,128)(2,1)S(1)} %collective-permute-done.refs_2_), channel_id=1, source_target_pairs={{0,2},{1,3},{2,4},{3,5},{4,6},{5,7},{6,8},{7,9},{8,10},{9,11},{10,... | collective-permute-start | bytes 1179656 | tf_op jit(solution)/shard_map/ppermute | solution.py:376
  21.6 14.9 %copy-start.5 = (bf16[2,64,1536]{2,1,0:T(8,128)(2,1)}, bf16[2,64,1536]{2,1,0:T(8,128)(2,1)S(1)}, u32[]{:S(2)}) copy-start(bf16[2,64,1536]{2,1,0:T(8,128)(2,1)S(1)} %collective-permute-done.2.refs_4_) | copy-start | bytes 1179652
  21.6 11.4 %collective-permute-start.3 = (bf16[2,64,1536]{2,1,0:T(8,128)(2,1)S(1)}, bf16[2,64,1536]{2,1,0:T(8,128)(2,1)}, u32[]{:S(2)}, u32[]{:S(2)}) collective-permute-start(bf16[2,64,1536]{2,1,0:T(8,128)(2,1)S(1)} %collective-permute-done.2.refs_4_), channel_id=1, source_target_pairs={{0,14},{1,15},{2,0},{3,1},{4,2},{5,3},{6,4},{7,5},{8,6},{9,7},{10,... | collective-permute-start | bytes 1179656 | tf_op jit(solution)/shard_map/ppermute | solution.py:376
  30.2 5.8 %copy-start.1 = (bf16[128,1536]{1,0:T(8,128)(2,1)S(1)}, bf16[128,1536]{1,0:T(8,128)(2,1)}, u32[]{:S(2)}) copy-start(bf16[128,1536]{1,0:T(8,128)(2,1)} %shard_map.73) | copy-start | bytes 1179652
  33.0 10.5 %collective-permute-start.9 = (bf16[2,64,1536]{2,1,0:T(8,128)(2,1)}, bf16[2,64,1536]{2,1,0:T(8,128)(2,1)S(1)}, u32[]{:S(2)}, u32[]{:S(2)}) collective-permute-start(bf16[2,64,1536]{2,1,0:T(8,128)(2,1)} %collective-permute-done.1.refs_6_), channel_id=1, source_target_pairs={{0,2},{1,3},{2,4},{3,5},{4,6},{5,7},{6,8},{7,9},{8,10},{9,11},{10,... | collective-permute-start | bytes 1179656 | tf_op jit(solution)/shard_map/ppermute | solution.py:376
  36.0 9.9 %collective-permute-start.11 = (bf16[2,64,1536]{2,1,0:T(8,128)(2,1)}, bf16[2,64,1536]{2,1,0:T(8,128)(2,1)S(1)}, u32[]{:S(2)}, u32[]{:S(2)}) collective-permute-start(bf16[2,64,1536]{2,1,0:T(8,128)(2,1)} %collective-permute-done.3.refs_8_), channel_id=1, source_target_pairs={{0,14},{1,15},{2,0},{3,1},{4,2},{5,3},{6,4},{7,5},{8,6},{9,7},{10,... | collective-permute-start | bytes 1179656 | tf_op jit(solution)/shard_map/ppermute | solution.py:376
  36.0 9.9 %collective-permute-start.4 = (bf16[2,64,1536]{2,1,0:T(8,128)(2,1)S(1)}, bf16[2,64,1536]{2,1,0:T(8,128)(2,1)S(1)}, u32[]{:S(2)}, u32[]{:S(2)}) collective-permute-start(bf16[2,64,1536]{2,1,0:T(8,128)(2,1)S(1)} %bitcast.13), channel_id=1, source_target_pairs={{0,1},{1,0},{2,3},{3,2},{4,5},{5,4},{6,7},{7,6},{8,9},{9,8},{10,11... | collective-permute-start | bytes 1179656 | tf_op jit(solution)/shard_map/ppermute | solution.py:379
  36.0 11.8 %collective-permute-start.5 = (bf16[2,64,1536]{2,1,0:T(8,128)(2,1)S(1)}, bf16[2,64,1536]{2,1,0:T(8,128)(2,1)S(1)}, u32[]{:S(2)}, u32[]{:S(2)}) collective-permute-start(bf16[2,64,1536]{2,1,0:T(8,128)(2,1)S(1)} %collective-permute-done.refs_2_), channel_id=1, source_target_pairs={{0,1},{1,0},{2,3},{3,2},{4,5},{5,4},{6,7},{7,6},{8,9},{9,8},{10,11... | collective-permute-start | bytes 1179656 | tf_op jit(solution)/shard_map/ppermute | solution.py:379
  36.5 11.6 %collective-permute-start.6 = (bf16[2,64,1536]{2,1,0:T(8,128)(2,1)S(1)}, bf16[2,64,1536]{2,1,0:T(8,128)(2,1)S(1)}, u32[]{:S(2)}, u32[]{:S(2)}) collective-permute-start(bf16[2,64,1536]{2,1,0:T(8,128)(2,1)S(1)} %collective-permute-done.2.refs_4_), channel_id=1, source_target_pairs={{0,1},{1,0},{2,3},{3,2},{4,5},{5,4},{6,7},{7,6},{8,9},{9,8},{10,11... | collective-permute-start | bytes 1179656 | tf_op jit(solution)/shard_map/ppermute | solution.py:379
  43.4 17.5 %copy-start.2 = (bf16[2,64,1536]{2,1,0:T(8,128)(2,1)}, bf16[2,64,1536]{2,1,0:T(8,128)(2,1)S(1)}, u32[]{:S(2)}) copy-start(bf16[2,64,1536]{2,1,0:T(8,128)(2,1)S(1)} %collective-permute-done.9.refs_10_) | copy-start | bytes 1179652
  43.4 4.7 %collective-permute-start.7 = (bf16[2,64,1536]{2,1,0:T(8,128)(2,1)}, bf16[2,64,1536]{2,1,0:T(8,128)(2,1)S(1)}, u32[]{:S(2)}, u32[]{:S(2)}) collective-permute-start(bf16[2,64,1536]{2,1,0:T(8,128)(2,1)} %collective-permute-done.1.refs_6_), channel_id=1, source_target_pairs={{0,1},{1,0},{2,3},{3,2},{4,5},{5,4},{6,7},{7,6},{8,9},{9,8},{10,11... | collective-permute-start | bytes 1179656 | tf_op jit(solution)/shard_map/ppermute | solution.py:379
  45.9 15.1 %copy-start.3 = (bf16[2,64,1536]{2,1,0:T(8,128)(2,1)}, bf16[2,64,1536]{2,1,0:T(8,128)(2,1)S(1)}, u32[]{:S(2)}) copy-start(bf16[2,64,1536]{2,1,0:T(8,128)(2,1)S(1)} %collective-permute-done.11.refs_12_) | copy-start | bytes 1179652
  45.9 13.6 %collective-permute-start.8 = (bf16[2,64,1536]{2,1,0:T(8,128)(2,1)}, bf16[2,64,1536]{2,1,0:T(8,128)(2,1)S(1)}, u32[]{:S(2)}, u32[]{:S(2)}) collective-permute-start(bf16[2,64,1536]{2,1,0:T(8,128)(2,1)} %collective-permute-done.3.refs_8_), channel_id=1, source_target_pairs={{0,1},{1,0},{2,3},{3,2},{4,5},{5,4},{6,7},{7,6},{8,9},{9,8},{10,11... | collective-permute-start | bytes 1179656 | tf_op jit(solution)/shard_map/ppermute | solution.py:379
  46.0 15.0 %copy-start.6 = (bf16[2,64,1536]{2,1,0:T(8,128)(2,1)}, bf16[2,64,1536]{2,1,0:T(8,128)(2,1)S(1)}, u32[]{:S(2)}) copy-start(bf16[2,64,1536]{2,1,0:T(8,128)(2,1)S(1)} %collective-permute-done.4.refs_1_) | copy-start | bytes 1179652
  46.0 11.8 %collective-permute-start.13 = (bf16[1,64,1536]{2,1,0:T(8,128)(2,1)S(1)}, bf16[1,64,1536]{2,1,0:T(8,128)(2,1)S(1)}, u32[]{:S(2)}, u32[]{:S(2)}) collective-permute-start(bf16[1,64,1536]{2,1,0:T(8,128)(2,1)S(1)} %slice.8), channel_id=1, source_target_pairs={{0,2},{1,3},{2,4},{3,5},{4,6},{5,7},{6,8},{7,9},{8,10},{9,11},{10,... | collective-permute-start | bytes 589832 | tf_op jit(solution)/shard_map/ppermute | solution.py:376
  47.8 13.2 %copy-start.7 = (bf16[2,64,1536]{2,1,0:T(8,128)(2,1)}, bf16[2,64,1536]{2,1,0:T(8,128)(2,1)S(1)}, u32[]{:S(2)}) copy-start(bf16[2,64,1536]{2,1,0:T(8,128)(2,1)S(1)} %collective-permute-done.5.refs_3_) | copy-start | bytes 1179652
  47.8 11.7 %collective-permute-start.15 = (bf16[1,64,1536]{2,1,0:T(8,128)(2,1)S(1)}, bf16[1,64,1536]{2,1,0:T(8,128)(2,1)S(1)}, u32[]{:S(2)}, u32[]{:S(2)}) collective-permute-start(bf16[1,64,1536]{2,1,0:T(8,128)(2,1)S(1)} %slice.9), channel_id=1, source_target_pairs={{0,14},{1,15},{2,0},{3,1},{4,2},{5,3},{6,4},{7,5},{8,6},{9,7},{10,... | collective-permute-start | bytes 589832 | tf_op jit(solution)/shard_map/ppermute | solution.py:376
  48.1 12.9 %copy-start.8 = (bf16[2,64,1536]{2,1,0:T(8,128)(2,1)}, bf16[2,64,1536]{2,1,0:T(8,128)(2,1)S(1)}, u32[]{:S(2)}) copy-start(bf16[2,64,1536]{2,1,0:T(8,128)(2,1)S(1)} %collective-permute-done.6.refs_5_) | copy-start | bytes 1179652
  48.1 12.9 %collective-permute-start.10 = (bf16[2,64,1536]{2,1,0:T(8,128)(2,1)S(1)}, bf16[2,64,1536]{2,1,0:T(8,128)(2,1)S(1)}, u32[]{:S(2)}, u32[]{:S(2)}) collective-permute-start(bf16[2,64,1536]{2,1,0:T(8,128)(2,1)S(1)} %collective-permute-done.9.refs_10_), channel_id=1, source_target_pairs={{0,1},{1,0},{2,3},{3,2},{4,5},{5,4},{6,7},{7,6},{8,9},{9,8},{10,11... | collective-permute-start | bytes 1179656 | tf_op jit(solution)/shard_map/ppermute | solution.py:379
  48.1 12.9 %copy-start.9 = (bf16[2,64,1536]{2,1,0:T(8,128)(2,1)}, bf16[2,64,1536]{2,1,0:T(8,128)(2,1)S(1)}, u32[]{:S(2)}) copy-start(bf16[2,64,1536]{2,1,0:T(8,128)(2,1)S(1)} %collective-permute-done.7.refs_7_) | copy-start | bytes 1179652
  48.1 12.8 %collective-permute-start.12 = (bf16[2,64,1536]{2,1,0:T(8,128)(2,1)S(1)}, bf16[2,64,1536]{2,1,0:T(8,128)(2,1)S(1)}, u32[]{:S(2)}, u32[]{:S(2)}) collective-permute-start(bf16[2,64,1536]{2,1,0:T(8,128)(2,1)S(1)} %collective-permute-done.11.refs_12_), channel_id=1, source_target_pairs={{0,1},{1,0},{2,3},{3,2},{4,5},{5,4},{6,7},{7,6},{8,9},{9,8},{10,11... | collective-permute-start | bytes 1179656 | tf_op jit(solution)/shard_map/ppermute | solution.py:379
  57.8 3.2 %copy-start.13 = (bf16[1,64,1536]{2,1,0:T(8,128)(2,1)}, bf16[1,64,1536]{2,1,0:T(8,128)(2,1)S(1)}, u32[]{:S(2)}) copy-start(bf16[1,64,1536]{2,1,0:T(8,128)(2,1)S(1)} %collective-permute-done.13.refs_14_) | copy-start | bytes 589828
  57.8 1.7 collective-permute-start.14
  59.5 1.5 copy-start.14
  59.5 1.4 collective-permute-start.16
  59.5 1.5 copy-start.10
  59.6 1.5 copy-start.15
  61.0 0.7 copy-start.16
  61.0 0.8 copy-start.11
  61.8 0.7 copy-start.12
  72.6 62.9 %all-to-all-start = ((s16[16,2,384,128]{3,2,1,0:T(8,128)(2,1)}), s16[16,2,384,128]{3,2,1,0:T(8,128)(2,1)}, u32[]{:S(2)}, u32[]{:S(2)}) async-start(s16[16,2,384,128]{3,2,1,0:T(8,128)(2,1)} %get-tuple-element.28), calls=%async_computation | async-start | bytes 6291456 | tf_op jit(solution)/shard_map/all_to_all | solution.py:403
  103.4 29.1 %copy-start = (f32[16,2,8,128]{3,2,1,0:T(8,128)S(1)}, f32[16,2,8,128]{3,2,1,0:T(8,128)}, u32[]{:S(2)}) copy-start(f32[16,2,8,128]{3,2,1,0:T(8,128)} %get-tuple-element.27.exponent_ref) | copy-start | bytes 393220
  114.2 1.2 collective-permute-start.17
  115.5 3.9 %collective-permute-start.18 = (f32[2,1,128]{2,1,0:T(1,128)S(1)}, f32[2,1,128]{2,1,0:T(1,128)S(1)}, u32[]{:S(2)}, u32[]{:S(2)}) collective-permute-start(f32[2,1,128]{2,1,0:T(1,128)S(1)} %add.24), channel_id=1, source_target_pairs={{0,2},{1,3},{2,4},{3,5},{4,6},{5,7},{6,8},{7,9},{8,10},{9,11},{10,... | collective-permute-start | bytes 3080 | tf_op jit(solution)/shard_map/ppermute | solution.py:376
  119.3 5.7 %collective-permute-start.19 = (f32[2,1,128]{2,1,0:T(1,128)S(1)}, f32[2,1,128]{2,1,0:T(1,128)S(1)}, u32[]{:S(2)}, u32[]{:S(2)}) collective-permute-start(f32[2,1,128]{2,1,0:T(1,128)S(1)} %add.25), channel_id=1, source_target_pairs={{0,4},{1,5},{2,6},{3,7},{4,8},{5,9},{6,10},{7,11},{8,12},{9,13},{1... | collective-permute-start | bytes 3080 | tf_op jit(solution)/shard_map/ppermute | solution.py:376
  125.0 7.5 %collective-permute-start.20 = (f32[2,1,128]{2,1,0:T(1,128)S(1)}, f32[2,1,128]{2,1,0:T(1,128)S(1)}, u32[]{:S(2)}, u32[]{:S(2)}) collective-permute-start(f32[2,1,128]{2,1,0:T(1,128)S(1)} %add.26), channel_id=1, source_target_pairs={{0,8},{1,9},{2,10},{3,11},{4,12},{5,13},{6,14},{7,15},{8,0},{9,1},... | collective-permute-start | bytes 3080 | tf_op jit(solution)/shard_map/ppermute | solution.py:376
Sparse Core Ops, SparseCore 0:
  33.1 70.2 all-gather.2

commit v8 on v6

--- a/solution.py
+++ b/solution.py
@@ -99,10 +99,12 @@
 
     @pl.when(example == 0)
     def _():
-        for copy in copies(0) + copies(1):
+        for copy in copies(0):
             copy.start()
         for copy in copies(0):
             copy.wait()
+        for copy in copies(1):
+            copy.start()
 
     @pl.when(example == 1)
     def _():
@@ -166,35 +168,51 @@
     tiles = acts_ref.shape[3] // width
     example, tile = pl.program_id(0), pl.program_id(1)
 
-    def acts_copy(step):
-        here = pl.ds(step % tiles * width, width)
-        source = acts_ref.at[:, step // tiles, :, here]
-        return pltpu.make_async_copy(source, acts.at[step % 2], acts_sems.at[step % 2])
+    step = example * tiles + tile
+    halves = ((0, 2 * CHUNK), (2 * CHUNK, width - 2 * CHUNK))
+
+    def acts_copies(e, i):
+        slot = (e * tiles + i) % 2
+        made = []
+        for half, (first, wide) in enumerate(halves):
+            here = pl.ds(pl.multiple_of(i * width + first, LANES), wide)
+            place = acts.at[slot, :, :, pl.ds(first, wide)]
+            made.append(pltpu.make_async_copy(acts_ref.at[:, e, :, here], place, acts_sems.at[slot, half]))
+        return made
 
     def grads_copy(e):
         return pltpu.make_async_copy(grads_ref.at[e], grads.at[e], grads_sems.at[e])
 
-    for step in range(examples * tiles):
-
-        @pl.when(example * tiles + tile == step)
-        def _():
-            if step == 0:
-                acts_copy(0).start()
-                for e in range(examples):
-                    grads_copy(e).start()
-            if step + 1 < examples * tiles:
-                acts_copy(step + 1).start()
-            acts_copy(step).wait()
-            if step % tiles == 0:
-                grads_copy(step // tiles).wait()
+    @pl.when(step == 0)
+    def _():
+        grads_copy(0).start()
+        for copy in acts_copies(0, 0):
+            copy.start()
 
     @pl.when(tile == 0)
     def _():
+        grads_copy(example).wait()
         share_ref[...] = squares_ref[...]
 
-    slot = (example * tiles + tile) % 2
+    now = acts_copies(example, tile)
+    slot = step % 2
     share = share_ref[0]
     for at in range(0, width, CHUNK):
+        if at == halves[0][0]:
+            now[0].wait()
+        if at == halves[1][0]:
+            now[1].wait()
+
+            @pl.when(step + 1 < examples * tiles)
+            def _():
+                for copy in acts_copies((step + 1) // tiles, (step + 1) % tiles):
+                    copy.start()
+
+            @pl.when(step == 0)
+            def _():
+                for e in range(1, examples):
+                    grads_copy(e).start()
+
         here = slice(at, at + CHUNK)
         some = acts[slot, :, :, here].reshape(devices * shard, CHUNK)
         product = jnp.dot(grads[example], some, preferred_element_type=jnp.float32)
@@ -227,7 +245,7 @@
         scratch_shapes=[
             pltpu.VMEM((2, devices, shard, width), acts.dtype),
             pltpu.VMEM(grads.shape, grads.dtype),
-            pltpu.SemaphoreType.DMA((2,)),
+            pltpu.SemaphoreType.DMA((2, 2)),
             pltpu.SemaphoreType.DMA((examples,)),
         ],
         cost_estimate=SMALL,

time: 184 us -> 187 us (1.016)
  Pallas kernels: 31.6 us -> 34 us
    pallas_call x1, Pallas kernels: 9.82 us -> 12.2 us  [plain_products(): pl.pallas_call(plain_kernel, grid=(examples, features // width), in_specs...]
  transfers between devices with their start and end apart: 25 -> 25, of which waited for: 13 -> 13; matrix products, arithmetic and copies ran while one was open for 4% -> 3% of each run, Pallas kernels for 14% -> 15%
where the time goes in v8:
time: 187 us; the launch traced here: 186 us
  waiting for transfers between devices  60.3 us (32%)
  blocking collectives  40.7 us (22%)
  Pallas kernels  34 us (18%)
  starting transfers between devices  28.9 us (15%)
  between operations  14.3 us (8%)
  local copies, waits for them, and re-layouts  4.54 us (2%)
  other arithmetic  3.44 us (2%)
    all_to_all x1, blocking collectives, per_device(): clipped = lax.all_to_all(clipped, 'dp', 0, 0)  40.7 us
    ppermute x8, waiting for transfers between devices, along_z(): lax.ppermute(x, 'tensor', [(t, (t + 2 * k) % devices) for t in range(devi...  29.8 us
    all_gather x1, waiting for transfers between devices, per_device(): second = lax.all_gather(second, 'tensor')  23.6 us
    pallas_call x1, Pallas kernels, plain_products(): pl.pallas_call(plain_kernel, grid=(examples, features // width), in_specs...  12.2 us
    ppermute x8, starting transfers between devices, along_z(): lax.ppermute(x, 'tensor', [(t, (t + 2 * k) % devices) for t in range(devi...  11.4 us
    ppermute x15, starting transfers between devices, crossed(): return lax.ppermute(x, 'tensor', [(t, t ^ k) for t in range(devices)])  10.3 us
    pallas_call x1, Pallas kernels, raw_products(): pl.pallas_call(raw_kernel, grid=(examples,), in_specs=[pl.BlockSpec(memor...  10.1 us
    all_to_all x1, starting transfers between devices, per_device(): raw = lax.all_to_all(raw, 'dp', 0, 0)  7.13 us
  transfers between devices with their start and end apart: 25, of which 13 were waited for; matrix products, arithmetic and copies ran while one was open for 3% of the time, Pallas kernels for 15%

profile of v8, /device:TPU:32, one launch (start us, length us, event | category | flops | bytes accessed | tf_op | source)
XLA Modules:
  0.0 186.2 jit_solution(2590837638266905526)
XLA Ops:
  6.5 2.0 %shard_map.73 = bf16[128,1536]{1,0:T(8,128)(2,1)} custom-call(bf16[128,4096]{1,0:T(8,128)(2,1)} %bitcast.7), custom_call_target="tpu_custom_call" | custom-call | tf_op jit(solution)/shard_map/pallas_call | solution.py:37
  8.6 1.9 %collective-permute-start = (bf16[2,64,1536]{2,1,0:T(8,128)(2,1)}, bf16[2,64,1536]{2,1,0:T(8,128)(2,1)S(1)}, u32[]{:S(2)}, u32[]{:S(2)}) collective-permute-start(bf16[2,64,1536]{2,1,0:T(8,128)(2,1)} %bitcast.10), channel_id=1, source_target_pairs={{0,2},{1,3},{2,4},{3,5},{4,6},{5,7},{6,8},{7,9},{8,10},{9,11},{10,... | collective-permute-start | bytes 1179656 | tf_op jit(solution)/shard_map/ppermute | solution.py:393
  10.5 0.1 collective-permute-start.2
  10.6 0.7 iota_compare_fusion
  11.3 8.3 %collective-permute-done.refs_2_ = bf16[2,64,1536]{2,1,0:T(8,128)(2,1)S(1)} collective-permute-done((bf16[2,64,1536]{2,1,0:T(8,128)(2,1)}, bf16[2,64,1536]{2,1,0:T(8,128)(2,1)S(1)}, u32[]{:S(2)}, u32[]{:S(2)}) %collective-permute-start) | collective-permute-done | bytes 393248 | tf_op jit(solution)/shard_map/ppermute | solution.py:393
  19.6 1.9 %collective-permute-start.1 = (bf16[2,64,1536]{2,1,0:T(8,128)(2,1)S(1)}, bf16[2,64,1536]{2,1,0:T(8,128)(2,1)}, u32[]{:S(2)}, u32[]{:S(2)}) collective-permute-start(bf16[2,64,1536]{2,1,0:T(8,128)(2,1)S(1)} %collective-permute-done.refs_2_), channel_id=1, source_target_pairs={{0,2},{1,3},{2,4},{3,5},{4,6},{5,7},{6,8},{7,9},{8,10},{9,11},{10,... | collective-permute-start | bytes 1179656 | tf_op jit(solution)/shard_map/ppermute | solution.py:393
  21.6 2.4 %collective-permute-start.3 = (bf16[2,64,1536]{2,1,0:T(8,128)(2,1)S(1)}, bf16[2,64,1536]{2,1,0:T(8,128)(2,1)}, u32[]{:S(2)}, u32[]{:S(2)}) collective-permute-start(bf16[2,64,1536]{2,1,0:T(8,128)(2,1)S(1)} %collective-permute-done.2.refs_4_), channel_id=1, source_target_pairs={{0,14},{1,15},{2,0},{3,1},{4,2},{5,3},{6,4},{7,5},{8,6},{9,7},{10,... | collective-permute-start | bytes 1179656 | tf_op jit(solution)/shard_map/ppermute | solution.py:393
  24.0 1.2 add_and_fusion.order_ref
  25.2 2.0 %shard_map.74 = bf16[128,2560]{1,0:T(8,128)(2,1)} custom-call(bf16[128,4096]{1,0:T(8,128)(2,1)} %bitcast.8), custom_call_target="tpu_custom_call" | custom-call | tf_op jit(solution)/shard_map/pallas_call | solution.py:37
  27.2 3.0 %copy.9 = bf16[2,1024,512]{1,2,0:T(8,128)(2,1)S(1)} copy(bf16[2,1024,512]{2,1,0:T(8,128)(2,1)} %param.8) | data formatting | bytes 4194304 | tf_op args[1]
  30.2 0.0 copy-start.1
  30.2 1.5 select_bitcast_fusion.refs_18_.grads_ref
  31.7 0.8 collective-permute-done.1.refs_6_
  32.5 0.4 collective-permute-done.3.refs_8_
  33.0 0.0 all-gather.3.cloned.1.call-update
  33.0 3.0 %collective-permute-start.9 = (bf16[2,64,1536]{2,1,0:T(8,128)(2,1)}, bf16[2,64,1536]{2,1,0:T(8,128)(2,1)S(1)}, u32[]{:S(2)}, u32[]{:S(2)}) collective-permute-start(bf16[2,64,1536]{2,1,0:T(8,128)(2,1)} %collective-permute-done.1.refs_6_), channel_id=1, source_target_pairs={{0,2},{1,3},{2,4},{3,5},{4,6},{5,7},{6,8},{7,9},{8,10},{9,11},{10,... | collective-permute-start | bytes 1179656 | tf_op jit(solution)/shard_map/ppermute | solution.py:393
  36.0 0.0 collective-permute-start.11
  36.0 0.5 collective-permute-start.5
  36.5 0.1 collective-permute-start.6
  36.6 6.8 %collective-permute-done.9.refs_10_ = bf16[2,64,1536]{2,1,0:T(8,128)(2,1)S(1)} collective-permute-done((bf16[2,64,1536]{2,1,0:T(8,128)(2,1)}, bf16[2,64,1536]{2,1,0:T(8,128)(2,1)S(1)}, u32[]{:S(2)}, u32[]{:S(2)}) %collective-permute-start.9) | collective-permute-done | bytes 393248 | tf_op jit(solution)/shard_map/ppermute | solution.py:393
  43.5 2.5 %collective-permute-done.11.refs_12_ = bf16[2,64,1536]{2,1,0:T(8,128)(2,1)S(1)} collective-permute-done((bf16[2,64,1536]{2,1,0:T(8,128)(2,1)}, bf16[2,64,1536]{2,1,0:T(8,128)(2,1)S(1)}, u32[]{:S(2)}, u32[]{:S(2)}) %collective-permute-start.11) | collective-permute-done | bytes 393248 | tf_op jit(solution)/shard_map/ppermute | solution.py:393
  46.0 1.8 collective-permute-start.13
  47.8 0.3 collective-permute-start.15
  48.1 0.1 collective-permute-start.10
  48.1 0.5 collective-permute-start.12
  48.6 9.2 %collective-permute-done.13.refs_14_ = bf16[1,64,1536]{2,1,0:T(8,128)(2,1)S(1)} collective-permute-done((bf16[1,64,1536]{2,1,0:T(8,128)(2,1)S(1)}, bf16[1,64,1536]{2,1,0:T(8,128)(2,1)S(1)}, u32[]{:S(2)}, u32[]{:S(2)}) %collective-permute-start.13) | collective-permute-done | bytes 196640 | tf_op jit(solution)/shard_map/ppermute | solution.py:393
  57.8 1.7 collective-permute-done.15.refs_16_
  59.5 0.0 collective-permute-start.16
  59.6 1.4 collective-permute-done.16.refs_17_
  61.1 0.6 copy-done.16
  61.6 0.2 copy-done.11
  61.8 0.7 copy-done.12
  62.5 10.1 %shard_map.75 = (s16[16,2,384,128]{3,2,1,0:T(8,128)(2,1)}, f32[16,2,8,128]{3,2,1,0:T(8,128)}, f32[2,1,128]{2,1,0:T(1,128)}) custom-call(s32[16]{0:T(128)} %add_and_fusion.order_ref, bf16[2,64,1536]{2,1,0:T(8,128)(2,1)} %bitcast.12, bf16[2,64,1536]{2,1,0:T(8,128)(2,1)} %copy-done.6, bf16[2,64,1536]{2,1,0:T(8,128)(2,1)} %copy-done.4, ...), custom_call_target="tpu_custom_call" | custom-call | tf_op jit(solution)/shard_map/pallas_call | solution.py:141
  72.7 7.1 %all-to-all-start = ((s16[16,2,384,128]{3,2,1,0:T(8,128)(2,1)}), s16[16,2,384,128]{3,2,1,0:T(8,128)(2,1)}, u32[]{:S(2)}, u32[]{:S(2)}) async-start(s16[16,2,384,128]{3,2,1,0:T(8,128)(2,1)} %get-tuple-element.28), calls=%async_computation | async-start | bytes 6291456 | tf_op jit(solution)/shard_map/all_to_all | solution.py:420
  79.8 23.6 %all-gather.3.cloned.1.call-done = bf16[32,64,2560]{2,1,0:T(8,128)(2,1)} async-done(((bf16[2,64,2560]{2,1,0:T(8,128)(2,1)}), bf16[32,64,2560]{2,1,0:T(8,128)(2,1)}) %all-gather.3.cloned.1.call-update) | async-done | bytes 10485776 | tf_op jit(solution)/shard_map/all_gather | solution.py:411
  103.4 12.2 %shard_map.76 = (f32[2,512,2560]{2,1,0:T(8,128)S(1)}, f32[2,1,2560]{2,1,0:T(1,128)S(1)}, f32[2,1,128]{2,1,0:T(1,128)S(1)}) custom-call(bf16[16,2,64,2560]{3,2,1,0:T(8,128)(2,1)} %bitcast.6, bf16[2,512,1024]{2,1,0:T(8,128)(2,1)} %select_bitcast_fusion.refs_18_.grads_ref, f32[2,1,128]{2,1,0:T(1,128)} %get-tuple-element.23.squares_ref), custom_call_target="tpu_custom_call" | custom-call | flops 1 | bytes 1 | tf_op jit(solution)/shard_map/pallas_call | solution.py:231
  115.6 0.3 collective-permute-start.17
  115.9 2.3 %collective-permute-start.18 = (f32[2,1,128]{2,1,0:T(1,128)S(1)}, f32[2,1,128]{2,1,0:T(1,128)S(1)}, u32[]{:S(2)}, u32[]{:S(2)}) collective-permute-start(f32[2,1,128]{2,1,0:T(1,128)S(1)} %get-tuple-element.24), channel_id=1, source_target_pairs={{0,2},{1,3},{2,0},{3,1},{4,6},{5,7},{6,4},{7,5},{8,10},{9,11},{10,... | collective-permute-start | bytes 3080 | tf_op jit(solution)/shard_map/ppermute | solution.py:396
  118.3 1.5 collective-permute-done.18
  119.8 1.4 collective-permute-done.19
  121.3 2.1 %collective-permute-start.20 = (f32[2,1,128]{2,1,0:T(1,128)S(1)}, f32[2,1,128]{2,1,0:T(1,128)S(1)}, u32[]{:S(2)}, u32[]{:S(2)}) collective-permute-start(f32[2,1,128]{2,1,0:T(1,128)S(1)} %add_add_fusion.1), channel_id=1, source_target_pairs={{0,4},{1,5},{2,6},{3,7},{4,0},{5,1},{6,2},{7,3},{8,12},{9,13},{10,... | collective-permute-start | bytes 3080 | tf_op jit(solution)/shard_map/ppermute | solution.py:396
  123.3 2.0 %collective-permute-start.21 = (f32[2,1,128]{2,1,0:T(1,128)S(1)}, f32[2,1,128]{2,1,0:T(1,128)S(1)}, u32[]{:S(2)}, u32[]{:S(2)}) collective-permute-start(f32[2,1,128]{2,1,0:T(1,128)S(1)} %add_add_fusion.1), channel_id=1, source_target_pairs={{0,8},{1,9},{2,10},{3,11},{4,12},{5,13},{6,14},{7,15},{8,0},{9,1},... | collective-permute-start | bytes 3080 | tf_op jit(solution)/shard_map/ppermute | solution.py:396
  125.3 2.4 %collective-permute-start.22 = (f32[2,1,128]{2,1,0:T(1,128)S(1)}, f32[2,1,128]{2,1,0:T(1,128)S(1)}, u32[]{:S(2)}, u32[]{:S(2)}) collective-permute-start(f32[2,1,128]{2,1,0:T(1,128)S(1)} %add_add_fusion.1), channel_id=1, source_target_pairs={{0,12},{1,13},{2,14},{3,15},{4,8},{5,9},{6,10},{7,11},{8,4},{9,5},... | collective-permute-start | bytes 3080 | tf_op jit(solution)/shard_map/ppermute | solution.py:396
  128.4 2.4 %collective-permute-done.21 = f32[2,1,128]{2,1,0:T(1,128)S(1)} collective-permute-done((f32[2,1,128]{2,1,0:T(1,128)S(1)}, f32[2,1,128]{2,1,0:T(1,128)S(1)}, u32[]{:S(2)}, u32[]{:S(2)}) %collective-permute-start.21) | collective-permute-done | bytes 1056 | tf_op jit(solution)/shard_map/ppermute | solution.py:396
  130.8 0.2 collective-permute-done.22
  131.0 3.0 %shard_map.77 = s16[16,656,128]{2,1,0:T(8,128)(2,1)S(1)} custom-call(f32[1]{0:T(128)S(6)} %copy.10.clip_ref, f32[2,1,128]{2,1,0:T(1,128)S(1)} %add_add_fusion.shares_ref, f32[2,512,2560]{2,1,0:T(8,128)S(1)} %get-tuple-element.25.wide_ref.thin_ref, f32[2,512,2560]{2,1,0:T(8,128)S(1)} %get-tuple-element.25.wide_ref.thin_ref, ...), custom_call_target="tpu_custom_call" | custom-call | flops 1 | bytes 1 | tf_op jit(solution)/shard_map/pallas_call | solution.py:298
  134.0 40.7 %all_to_all.10.clipped_ref = s16[16,656,128]{2,1,0:T(8,128)(2,1)} all-to-all(s16[16,656,128]{2,1,0:T(8,128)(2,1)S(1)} %shard_map.77), channel_id=1, replica_groups=mesh['dp'=16,'tensor'=16] {'dp'}, dimensions={0} | all-to-all | bytes 5373952 | tf_op jit(solution)/shard_map/all_to_all | solution.py:426
  174.8 4.6 %shard_map.78 = f32[256,512]{1,0:T(8,128)} custom-call(s16[16,2,384,128]{3,2,1,0:T(8,128)(2,1)} %all-to-all-done.raw_ref, s16[16,656,128]{2,1,0:T(8,128)(2,1)} %all_to_all.10.clipped_ref, f32[256,512]{1,0:T(8,128)} %noise_ref.1), custom_call_target="tpu_custom_call" | custom-call | tf_op jit(solution)/shard_map/pallas_call | solution.py:371
  (52 shorter events, 0.1 us)
Async XLA Ops:
  6.5 96.8 %all-gather.3.cloned.1.call-start = ((), (), s32[]{:S(2)}) async-start(), calls=%async_computation.2 | async-start | bytes 11141120 | tf_op jit(solution)/shard_map/all_gather | solution.py:411
  8.6 11.1 %collective-permute-start = (bf16[2,64,1536]{2,1,0:T(8,128)(2,1)}, bf16[2,64,1536]{2,1,0:T(8,128)(2,1)S(1)}, u32[]{:S(2)}, u32[]{:S(2)}) collective-permute-start(bf16[2,64,1536]{2,1,0:T(8,128)(2,1)} %bitcast.10), channel_id=1, source_target_pairs={{0,2},{1,3},{2,4},{3,5},{4,6},{5,7},{6,8},{7,9},{8,10},{9,11},{10,... | collective-permute-start | bytes 1179656 | tf_op jit(solution)/shard_map/ppermute | solution.py:393
  10.5 11.1 %collective-permute-start.2 = (bf16[2,64,1536]{2,1,0:T(8,128)(2,1)}, bf16[2,64,1536]{2,1,0:T(8,128)(2,1)S(1)}, u32[]{:S(2)}, u32[]{:S(2)}) collective-permute-start(bf16[2,64,1536]{2,1,0:T(8,128)(2,1)} %bitcast.11), channel_id=1, source_target_pairs={{0,14},{1,15},{2,0},{3,1},{4,2},{5,3},{6,4},{7,5},{8,6},{9,7},{10,... | collective-permute-start | bytes 1179656 | tf_op jit(solution)/shard_map/ppermute | solution.py:393
  19.6 16.4 %copy-start.4 = (bf16[2,64,1536]{2,1,0:T(8,128)(2,1)}, bf16[2,64,1536]{2,1,0:T(8,128)(2,1)S(1)}, u32[]{:S(2)}) copy-start(bf16[2,64,1536]{2,1,0:T(8,128)(2,1)S(1)} %collective-permute-done.refs_2_) | copy-start | bytes 1179652
  19.6 12.9 %collective-permute-start.1 = (bf16[2,64,1536]{2,1,0:T(8,128)(2,1)S(1)}, bf16[2,64,1536]{2,1,0:T(8,128)(2,1)}, u32[]{:S(2)}, u32[]{:S(2)}) collective-permute-start(bf16[2,64,1536]{2,1,0:T(8,128)(2,1)S(1)} %collective-permute-done.refs_2_), channel_id=1, source_target_pairs={{0,2},{1,3},{2,4},{3,5},{4,6},{5,7},{6,8},{7,9},{8,10},{9,11},{10,... | collective-permute-start | bytes 1179656 | tf_op jit(solution)/shard_map/ppermute | solution.py:393
  21.6 14.9 %copy-start.5 = (bf16[2,64,1536]{2,1,0:T(8,128)(2,1)}, bf16[2,64,1536]{2,1,0:T(8,128)(2,1)S(1)}, u32[]{:S(2)}) copy-start(bf16[2,64,1536]{2,1,0:T(8,128)(2,1)S(1)} %collective-permute-done.2.refs_4_) | copy-start | bytes 1179652
  21.6 11.4 %collective-permute-start.3 = (bf16[2,64,1536]{2,1,0:T(8,128)(2,1)S(1)}, bf16[2,64,1536]{2,1,0:T(8,128)(2,1)}, u32[]{:S(2)}, u32[]{:S(2)}) collective-permute-start(bf16[2,64,1536]{2,1,0:T(8,128)(2,1)S(1)} %collective-permute-done.2.refs_4_), channel_id=1, source_target_pairs={{0,14},{1,15},{2,0},{3,1},{4,2},{5,3},{6,4},{7,5},{8,6},{9,7},{10,... | collective-permute-start | bytes 1179656 | tf_op jit(solution)/shard_map/ppermute | solution.py:393
  30.2 5.8 %copy-start.1 = (bf16[128,1536]{1,0:T(8,128)(2,1)S(1)}, bf16[128,1536]{1,0:T(8,128)(2,1)}, u32[]{:S(2)}) copy-start(bf16[128,1536]{1,0:T(8,128)(2,1)} %shard_map.73) | copy-start | bytes 1179652
  33.0 10.5 %collective-permute-start.9 = (bf16[2,64,1536]{2,1,0:T(8,128)(2,1)}, bf16[2,64,1536]{2,1,0:T(8,128)(2,1)S(1)}, u32[]{:S(2)}, u32[]{:S(2)}) collective-permute-start(bf16[2,64,1536]{2,1,0:T(8,128)(2,1)} %collective-permute-done.1.refs_6_), channel_id=1, source_target_pairs={{0,2},{1,3},{2,4},{3,5},{4,6},{5,7},{6,8},{7,9},{8,10},{9,11},{10,... | collective-permute-start | bytes 1179656 | tf_op jit(solution)/shard_map/ppermute | solution.py:393
  36.0 9.9 %collective-permute-start.11 = (bf16[2,64,1536]{2,1,0:T(8,128)(2,1)}, bf16[2,64,1536]{2,1,0:T(8,128)(2,1)S(1)}, u32[]{:S(2)}, u32[]{:S(2)}) collective-permute-start(bf16[2,64,1536]{2,1,0:T(8,128)(2,1)} %collective-permute-done.3.refs_8_), channel_id=1, source_target_pairs={{0,14},{1,15},{2,0},{3,1},{4,2},{5,3},{6,4},{7,5},{8,6},{9,7},{10,... | collective-permute-start | bytes 1179656 | tf_op jit(solution)/shard_map/ppermute | solution.py:393
  36.0 9.9 %collective-permute-start.4 = (bf16[2,64,1536]{2,1,0:T(8,128)(2,1)S(1)}, bf16[2,64,1536]{2,1,0:T(8,128)(2,1)S(1)}, u32[]{:S(2)}, u32[]{:S(2)}) collective-permute-start(bf16[2,64,1536]{2,1,0:T(8,128)(2,1)S(1)} %bitcast.13), channel_id=1, source_target_pairs={{0,1},{1,0},{2,3},{3,2},{4,5},{5,4},{6,7},{7,6},{8,9},{9,8},{10,11... | collective-permute-start | bytes 1179656 | tf_op jit(solution)/shard_map/ppermute | solution.py:396
  36.0 11.8 %collective-permute-start.5 = (bf16[2,64,1536]{2,1,0:T(8,128)(2,1)S(1)}, bf16[2,64,1536]{2,1,0:T(8,128)(2,1)S(1)}, u32[]{:S(2)}, u32[]{:S(2)}) collective-permute-start(bf16[2,64,1536]{2,1,0:T(8,128)(2,1)S(1)} %collective-permute-done.refs_2_), channel_id=1, source_target_pairs={{0,1},{1,0},{2,3},{3,2},{4,5},{5,4},{6,7},{7,6},{8,9},{9,8},{10,11... | collective-permute-start | bytes 1179656 | tf_op jit(solution)/shard_map/ppermute | solution.py:396
  36.5 11.6 %collective-permute-start.6 = (bf16[2,64,1536]{2,1,0:T(8,128)(2,1)S(1)}, bf16[2,64,1536]{2,1,0:T(8,128)(2,1)S(1)}, u32[]{:S(2)}, u32[]{:S(2)}) collective-permute-start(bf16[2,64,1536]{2,1,0:T(8,128)(2,1)S(1)} %collective-permute-done.2.refs_4_), channel_id=1, source_target_pairs={{0,1},{1,0},{2,3},{3,2},{4,5},{5,4},{6,7},{7,6},{8,9},{9,8},{10,11... | collective-permute-start | bytes 1179656 | tf_op jit(solution)/shard_map/ppermute | solution.py:396
  43.4 17.5 %copy-start.2 = (bf16[2,64,1536]{2,1,0:T(8,128)(2,1)}, bf16[2,64,1536]{2,1,0:T(8,128)(2,1)S(1)}, u32[]{:S(2)}) copy-start(bf16[2,64,1536]{2,1,0:T(8,128)(2,1)S(1)} %collective-permute-done.9.refs_10_) | copy-start | bytes 1179652
  43.4 4.7 %collective-permute-start.7 = (bf16[2,64,1536]{2,1,0:T(8,128)(2,1)}, bf16[2,64,1536]{2,1,0:T(8,128)(2,1)S(1)}, u32[]{:S(2)}, u32[]{:S(2)}) collective-permute-start(bf16[2,64,1536]{2,1,0:T(8,128)(2,1)} %collective-permute-done.1.refs_6_), channel_id=1, source_target_pairs={{0,1},{1,0},{2,3},{3,2},{4,5},{5,4},{6,7},{7,6},{8,9},{9,8},{10,11... | collective-permute-start | bytes 1179656 | tf_op jit(solution)/shard_map/ppermute | solution.py:396
  45.9 15.1 %copy-start.3 = (bf16[2,64,1536]{2,1,0:T(8,128)(2,1)}, bf16[2,64,1536]{2,1,0:T(8,128)(2,1)S(1)}, u32[]{:S(2)}) copy-start(bf16[2,64,1536]{2,1,0:T(8,128)(2,1)S(1)} %collective-permute-done.11.refs_12_) | copy-start | bytes 1179652
  45.9 13.6 %collective-permute-start.8 = (bf16[2,64,1536]{2,1,0:T(8,128)(2,1)}, bf16[2,64,1536]{2,1,0:T(8,128)(2,1)S(1)}, u32[]{:S(2)}, u32[]{:S(2)}) collective-permute-start(bf16[2,64,1536]{2,1,0:T(8,128)(2,1)} %collective-permute-done.3.refs_8_), channel_id=1, source_target_pairs={{0,1},{1,0},{2,3},{3,2},{4,5},{5,4},{6,7},{7,6},{8,9},{9,8},{10,11... | collective-permute-start | bytes 1179656 | tf_op jit(solution)/shard_map/ppermute | solution.py:396
  46.0 15.0 %copy-start.6 = (bf16[2,64,1536]{2,1,0:T(8,128)(2,1)}, bf16[2,64,1536]{2,1,0:T(8,128)(2,1)S(1)}, u32[]{:S(2)}) copy-start(bf16[2,64,1536]{2,1,0:T(8,128)(2,1)S(1)} %collective-permute-done.4.refs_1_) | copy-start | bytes 1179652
  46.0 11.8 %collective-permute-start.13 = (bf16[1,64,1536]{2,1,0:T(8,128)(2,1)S(1)}, bf16[1,64,1536]{2,1,0:T(8,128)(2,1)S(1)}, u32[]{:S(2)}, u32[]{:S(2)}) collective-permute-start(bf16[1,64,1536]{2,1,0:T(8,128)(2,1)S(1)} %slice.8), channel_id=1, source_target_pairs={{0,2},{1,3},{2,4},{3,5},{4,6},{5,7},{6,8},{7,9},{8,10},{9,11},{10,... | collective-permute-start | bytes 589832 | tf_op jit(solution)/shard_map/ppermute | solution.py:393
  47.8 13.2 %copy-start.7 = (bf16[2,64,1536]{2,1,0:T(8,128)(2,1)}, bf16[2,64,1536]{2,1,0:T(8,128)(2,1)S(1)}, u32[]{:S(2)}) copy-start(bf16[2,64,1536]{2,1,0:T(8,128)(2,1)S(1)} %collective-permute-done.5.refs_3_) | copy-start | bytes 1179652
  47.8 11.7 %collective-permute-start.15 = (bf16[1,64,1536]{2,1,0:T(8,128)(2,1)S(1)}, bf16[1,64,1536]{2,1,0:T(8,128)(2,1)S(1)}, u32[]{:S(2)}, u32[]{:S(2)}) collective-permute-start(bf16[1,64,1536]{2,1,0:T(8,128)(2,1)S(1)} %slice.9), channel_id=1, source_target_pairs={{0,14},{1,15},{2,0},{3,1},{4,2},{5,3},{6,4},{7,5},{8,6},{9,7},{10,... | collective-permute-start | bytes 589832 | tf_op jit(solution)/shard_map/ppermute | solution.py:393
  48.1 12.9 %copy-start.8 = (bf16[2,64,1536]{2,1,0:T(8,128)(2,1)}, bf16[2,64,1536]{2,1,0:T(8,128)(2,1)S(1)}, u32[]{:S(2)}) copy-start(bf16[2,64,1536]{2,1,0:T(8,128)(2,1)S(1)} %collective-permute-done.6.refs_5_) | copy-start | bytes 1179652
  48.1 12.9 %collective-permute-start.10 = (bf16[2,64,1536]{2,1,0:T(8,128)(2,1)S(1)}, bf16[2,64,1536]{2,1,0:T(8,128)(2,1)S(1)}, u32[]{:S(2)}, u32[]{:S(2)}) collective-permute-start(bf16[2,64,1536]{2,1,0:T(8,128)(2,1)S(1)} %collective-permute-done.9.refs_10_), channel_id=1, source_target_pairs={{0,1},{1,0},{2,3},{3,2},{4,5},{5,4},{6,7},{7,6},{8,9},{9,8},{10,11... | collective-permute-start | bytes 1179656 | tf_op jit(solution)/shard_map/ppermute | solution.py:396
  48.1 12.9 %copy-start.9 = (bf16[2,64,1536]{2,1,0:T(8,128)(2,1)}, bf16[2,64,1536]{2,1,0:T(8,128)(2,1)S(1)}, u32[]{:S(2)}) copy-start(bf16[2,64,1536]{2,1,0:T(8,128)(2,1)S(1)} %collective-permute-done.7.refs_7_) | copy-start | bytes 1179652
  48.1 12.8 %collective-permute-start.12 = (bf16[2,64,1536]{2,1,0:T(8,128)(2,1)S(1)}, bf16[2,64,1536]{2,1,0:T(8,128)(2,1)S(1)}, u32[]{:S(2)}, u32[]{:S(2)}) collective-permute-start(bf16[2,64,1536]{2,1,0:T(8,128)(2,1)S(1)} %collective-permute-done.11.refs_12_), channel_id=1, source_target_pairs={{0,1},{1,0},{2,3},{3,2},{4,5},{5,4},{6,7},{7,6},{8,9},{9,8},{10,11... | collective-permute-start | bytes 1179656 | tf_op jit(solution)/shard_map/ppermute | solution.py:396
  57.8 3.2 %copy-start.13 = (bf16[1,64,1536]{2,1,0:T(8,128)(2,1)}, bf16[1,64,1536]{2,1,0:T(8,128)(2,1)S(1)}, u32[]{:S(2)}) copy-start(bf16[1,64,1536]{2,1,0:T(8,128)(2,1)S(1)} %collective-permute-done.13.refs_14_) | copy-start | bytes 589828
  57.8 1.7 collective-permute-start.14
  59.5 1.5 copy-start.14
  59.5 1.4 collective-permute-start.16
  59.5 1.5 copy-start.10
  59.6 1.5 copy-start.15
  61.0 0.7 copy-start.16
  61.0 0.8 copy-start.11
  61.8 0.7 copy-start.12
  72.7 61.3 %all-to-all-start = ((s16[16,2,384,128]{3,2,1,0:T(8,128)(2,1)}), s16[16,2,384,128]{3,2,1,0:T(8,128)(2,1)}, u32[]{:S(2)}, u32[]{:S(2)}) async-start(s16[16,2,384,128]{3,2,1,0:T(8,128)(2,1)} %get-tuple-element.28), calls=%async_computation | async-start | bytes 6291456 | tf_op jit(solution)/shard_map/all_to_all | solution.py:420
  103.4 27.6 %copy-start = (f32[16,2,8,128]{3,2,1,0:T(8,128)S(1)}, f32[16,2,8,128]{3,2,1,0:T(8,128)}, u32[]{:S(2)}) copy-start(f32[16,2,8,128]{3,2,1,0:T(8,128)} %get-tuple-element.27.exponent_ref) | copy-start | bytes 393220
  115.6 2.7 %collective-permute-start.17 = (f32[2,1,128]{2,1,0:T(1,128)S(1)}, f32[2,1,128]{2,1,0:T(1,128)S(1)}, u32[]{:S(2)}, u32[]{:S(2)}) collective-permute-start(f32[2,1,128]{2,1,0:T(1,128)S(1)} %get-tuple-element.24), channel_id=1, source_target_pairs={{0,1},{1,0},{2,3},{3,2},{4,5},{5,4},{6,7},{7,6},{8,9},{9,8},{10,11... | collective-permute-start | bytes 3080 | tf_op jit(solution)/shard_map/ppermute | solution.py:396
  115.9 3.9 %collective-permute-start.18 = (f32[2,1,128]{2,1,0:T(1,128)S(1)}, f32[2,1,128]{2,1,0:T(1,128)S(1)}, u32[]{:S(2)}, u32[]{:S(2)}) collective-permute-start(f32[2,1,128]{2,1,0:T(1,128)S(1)} %get-tuple-element.24), channel_id=1, source_target_pairs={{0,2},{1,3},{2,0},{3,1},{4,6},{5,7},{6,4},{7,5},{8,10},{9,11},{10,... | collective-permute-start | bytes 3080 | tf_op jit(solution)/shard_map/ppermute | solution.py:396
  118.3 3.0 %collective-permute-start.19 = (f32[2,1,128]{2,1,0:T(1,128)S(1)}, f32[2,1,128]{2,1,0:T(1,128)S(1)}, u32[]{:S(2)}, u32[]{:S(2)}) collective-permute-start(f32[2,1,128]{2,1,0:T(1,128)S(1)} %get-tuple-element.24), channel_id=1, source_target_pairs={{0,3},{1,2},{2,1},{3,0},{4,7},{5,6},{6,5},{7,4},{8,11},{9,10},{10,... | collective-permute-start | bytes 3080 | tf_op jit(solution)/shard_map/ppermute | solution.py:396
  121.3 7.2 %collective-permute-start.20 = (f32[2,1,128]{2,1,0:T(1,128)S(1)}, f32[2,1,128]{2,1,0:T(1,128)S(1)}, u32[]{:S(2)}, u32[]{:S(2)}) collective-permute-start(f32[2,1,128]{2,1,0:T(1,128)S(1)} %add_add_fusion.1), channel_id=1, source_target_pairs={{0,4},{1,5},{2,6},{3,7},{4,0},{5,1},{6,2},{7,3},{8,12},{9,13},{10,... | collective-permute-start | bytes 3080 | tf_op jit(solution)/shard_map/ppermute | solution.py:396
  123.3 7.5 %collective-permute-start.21 = (f32[2,1,128]{2,1,0:T(1,128)S(1)}, f32[2,1,128]{2,1,0:T(1,128)S(1)}, u32[]{:S(2)}, u32[]{:S(2)}) collective-permute-start(f32[2,1,128]{2,1,0:T(1,128)S(1)} %add_add_fusion.1), channel_id=1, source_target_pairs={{0,8},{1,9},{2,10},{3,11},{4,12},{5,13},{6,14},{7,15},{8,0},{9,1},... | collective-permute-start | bytes 3080 | tf_op jit(solution)/shard_map/ppermute | solution.py:396
  125.3 5.7 %collective-permute-start.22 = (f32[2,1,128]{2,1,0:T(1,128)S(1)}, f32[2,1,128]{2,1,0:T(1,128)S(1)}, u32[]{:S(2)}, u32[]{:S(2)}) collective-permute-start(f32[2,1,128]{2,1,0:T(1,128)S(1)} %add_add_fusion.1), channel_id=1, source_target_pairs={{0,12},{1,13},{2,14},{3,15},{4,8},{5,9},{6,10},{7,11},{8,4},{9,5},... | collective-permute-start | bytes 3080 | tf_op jit(solution)/shard_map/ppermute | solution.py:396
Sparse Core Ops, SparseCore 0:
  33.1 70.2 all-gather.2

commit v9 on v6

--- a/solution.py
+++ b/solution.py
@@ -179,14 +179,16 @@
         @pl.when(example * tiles + tile == step)
         def _():
             if step == 0:
+                grads_copy(0).start()
                 acts_copy(0).start()
-                for e in range(examples):
-                    grads_copy(e).start()
-            if step + 1 < examples * tiles:
-                acts_copy(step + 1).start()
             acts_copy(step).wait()
             if step % tiles == 0:
                 grads_copy(step // tiles).wait()
+            if step + 1 < examples * tiles:
+                acts_copy(step + 1).start()
+            if step == 0:
+                for e in range(1, examples):
+                    grads_copy(e).start()
 
     @pl.when(tile == 0)
     def _():

time: 184 us -> 184 us (level)
  no operation moved by 1% of the time
where the time goes in v9:
time: 184 us
  waiting for transfers between devices  60.3 us (33%)
  blocking collectives  40.7 us (22%)
  Pallas kernels  31.7 us (17%)
  starting transfers between devices  28.9 us (16%)
  between operations  14.3 us (8%)
  local copies, waits for them, and re-layouts  4.54 us (2%)
  other arithmetic  3.44 us (2%)
    all_to_all x1, blocking collectives, per_device(): clipped = lax.all_to_all(clipped, 'dp', 0, 0)  40.7 us
    ppermute x8, waiting for transfers between devices, along_z(): lax.ppermute(x, 'tensor', [(t, (t + 2 * k) % devices) for t in range(devi...  29.8 us
    all_gather x1, waiting for transfers between devices, per_device(): second = lax.all_gather(second, 'tensor')  23.6 us
    ppermute x8, starting transfers between devices, along_z(): lax.ppermute(x, 'tensor', [(t, (t + 2 * k) % devices) for t in range(devi...  11.4 us
    ppermute x15, starting transfers between devices, crossed(): return lax.ppermute(x, 'tensor', [(t, t ^ k) for t in range(devices)])  10.3 us
    pallas_call x1, Pallas kernels, raw_products(): pl.pallas_call(raw_kernel, grid=(examples,), in_specs=[pl.BlockSpec(memor...  10.1 us
    pallas_call x1, Pallas kernels, plain_products(): pl.pallas_call(plain_kernel, grid=(examples, features // width), in_specs...  9.92 us
    all_to_all x1, starting transfers between devices, per_device(): raw = lax.all_to_all(raw, 'dp', 0, 0)  7.13 us
  transfers between devices with their start and end apart: 25, of which 13 were waited for; matrix products, arithmetic and copies ran while one was open for 4% of the time, Pallas kernels for 14%

profile of v9, /device:TPU:32, one launch (start us, length us, event | category | flops | bytes accessed | tf_op | source)
XLA Modules:
  0.0 183.9 jit_solution(6073856902075287584)
XLA Ops:
  6.5 2.0 %shard_map.73 = bf16[128,1536]{1,0:T(8,128)(2,1)} custom-call(bf16[128,4096]{1,0:T(8,128)(2,1)} %bitcast.7), custom_call_target="tpu_custom_call" | custom-call | tf_op jit(solution)/shard_map/pallas_call | solution.py:37
  8.6 1.9 %collective-permute-start = (bf16[2,64,1536]{2,1,0:T(8,128)(2,1)}, bf16[2,64,1536]{2,1,0:T(8,128)(2,1)S(1)}, u32[]{:S(2)}, u32[]{:S(2)}) collective-permute-start(bf16[2,64,1536]{2,1,0:T(8,128)(2,1)} %bitcast.10), channel_id=1, source_target_pairs={{0,2},{1,3},{2,4},{3,5},{4,6},{5,7},{6,8},{7,9},{8,10},{9,11},{10,... | collective-permute-start | bytes 1179656 | tf_op jit(solution)/shard_map/ppermute | solution.py:377
  10.5 0.1 collective-permute-start.2
  10.6 0.7 iota_compare_fusion
  11.3 8.3 %collective-permute-done.refs_2_ = bf16[2,64,1536]{2,1,0:T(8,128)(2,1)S(1)} collective-permute-done((bf16[2,64,1536]{2,1,0:T(8,128)(2,1)}, bf16[2,64,1536]{2,1,0:T(8,128)(2,1)S(1)}, u32[]{:S(2)}, u32[]{:S(2)}) %collective-permute-start) | collective-permute-done | bytes 393248 | tf_op jit(solution)/shard_map/ppermute | solution.py:377
  19.6 1.9 %collective-permute-start.1 = (bf16[2,64,1536]{2,1,0:T(8,128)(2,1)S(1)}, bf16[2,64,1536]{2,1,0:T(8,128)(2,1)}, u32[]{:S(2)}, u32[]{:S(2)}) collective-permute-start(bf16[2,64,1536]{2,1,0:T(8,128)(2,1)S(1)} %collective-permute-done.refs_2_), channel_id=1, source_target_pairs={{0,2},{1,3},{2,4},{3,5},{4,6},{5,7},{6,8},{7,9},{8,10},{9,11},{10,... | collective-permute-start | bytes 1179656 | tf_op jit(solution)/shard_map/ppermute | solution.py:377
  21.6 2.4 %collective-permute-start.3 = (bf16[2,64,1536]{2,1,0:T(8,128)(2,1)S(1)}, bf16[2,64,1536]{2,1,0:T(8,128)(2,1)}, u32[]{:S(2)}, u32[]{:S(2)}) collective-permute-start(bf16[2,64,1536]{2,1,0:T(8,128)(2,1)S(1)} %collective-permute-done.2.refs_4_), channel_id=1, source_target_pairs={{0,14},{1,15},{2,0},{3,1},{4,2},{5,3},{6,4},{7,5},{8,6},{9,7},{10,... | collective-permute-start | bytes 1179656 | tf_op jit(solution)/shard_map/ppermute | solution.py:377
  24.0 1.2 add_and_fusion.order_ref
  25.2 2.0 %shard_map.74 = bf16[128,2560]{1,0:T(8,128)(2,1)} custom-call(bf16[128,4096]{1,0:T(8,128)(2,1)} %bitcast.8), custom_call_target="tpu_custom_call" | custom-call | tf_op jit(solution)/shard_map/pallas_call | solution.py:37
  27.2 3.0 %copy.9 = bf16[2,1024,512]{1,2,0:T(8,128)(2,1)S(1)} copy(bf16[2,1024,512]{2,1,0:T(8,128)(2,1)} %param.8) | data formatting | bytes 4194304 | tf_op args[1]
  30.2 0.0 copy-start.1
  30.2 1.5 select_bitcast_fusion.refs_18_.grads_ref
  31.7 0.8 collective-permute-done.1.refs_6_
  32.5 0.4 collective-permute-done.3.refs_8_
  33.0 0.0 all-gather.3.cloned.1.call-update
  33.0 3.0 %collective-permute-start.9 = (bf16[2,64,1536]{2,1,0:T(8,128)(2,1)}, bf16[2,64,1536]{2,1,0:T(8,128)(2,1)S(1)}, u32[]{:S(2)}, u32[]{:S(2)}) collective-permute-start(bf16[2,64,1536]{2,1,0:T(8,128)(2,1)} %collective-permute-done.1.refs_6_), channel_id=1, source_target_pairs={{0,2},{1,3},{2,4},{3,5},{4,6},{5,7},{6,8},{7,9},{8,10},{9,11},{10,... | collective-permute-start | bytes 1179656 | tf_op jit(solution)/shard_map/ppermute | solution.py:377
  36.0 0.0 collective-permute-start.11
  36.0 0.5 collective-permute-start.5
  36.5 0.1 collective-permute-start.6
  36.6 6.8 %collective-permute-done.9.refs_10_ = bf16[2,64,1536]{2,1,0:T(8,128)(2,1)S(1)} collective-permute-done((bf16[2,64,1536]{2,1,0:T(8,128)(2,1)}, bf16[2,64,1536]{2,1,0:T(8,128)(2,1)S(1)}, u32[]{:S(2)}, u32[]{:S(2)}) %collective-permute-start.9) | collective-permute-done | bytes 393248 | tf_op jit(solution)/shard_map/ppermute | solution.py:377
  43.5 2.5 %collective-permute-done.11.refs_12_ = bf16[2,64,1536]{2,1,0:T(8,128)(2,1)S(1)} collective-permute-done((bf16[2,64,1536]{2,1,0:T(8,128)(2,1)}, bf16[2,64,1536]{2,1,0:T(8,128)(2,1)S(1)}, u32[]{:S(2)}, u32[]{:S(2)}) %collective-permute-start.11) | collective-permute-done | bytes 393248 | tf_op jit(solution)/shard_map/ppermute | solution.py:377
  46.0 1.8 collective-permute-start.13
  47.8 0.3 collective-permute-start.15
  48.1 0.1 collective-permute-start.10
  48.1 0.5 collective-permute-start.12
  48.6 9.2 %collective-permute-done.13.refs_14_ = bf16[1,64,1536]{2,1,0:T(8,128)(2,1)S(1)} collective-permute-done((bf16[1,64,1536]{2,1,0:T(8,128)(2,1)S(1)}, bf16[1,64,1536]{2,1,0:T(8,128)(2,1)S(1)}, u32[]{:S(2)}, u32[]{:S(2)}) %collective-permute-start.13) | collective-permute-done | bytes 196640 | tf_op jit(solution)/shard_map/ppermute | solution.py:377
  57.8 1.7 collective-permute-done.15.refs_16_
  59.5 0.0 collective-permute-start.16
  59.6 1.4 collective-permute-done.16.refs_17_
  61.1 0.6 copy-done.16
  61.6 0.2 copy-done.11
  61.8 0.7 copy-done.12
  62.5 10.1 %shard_map.75 = (s16[16,2,384,128]{3,2,1,0:T(8,128)(2,1)}, f32[16,2,8,128]{3,2,1,0:T(8,128)}, f32[2,1,128]{2,1,0:T(1,128)}) custom-call(s32[16]{0:T(128)} %add_and_fusion.order_ref, bf16[2,64,1536]{2,1,0:T(8,128)(2,1)} %bitcast.12, bf16[2,64,1536]{2,1,0:T(8,128)(2,1)} %copy-done.6, bf16[2,64,1536]{2,1,0:T(8,128)(2,1)} %copy-done.4, ...), custom_call_target="tpu_custom_call" | custom-call | tf_op jit(solution)/shard_map/pallas_call | solution.py:139
  72.7 7.1 %all-to-all-start = ((s16[16,2,384,128]{3,2,1,0:T(8,128)(2,1)}), s16[16,2,384,128]{3,2,1,0:T(8,128)(2,1)}, u32[]{:S(2)}, u32[]{:S(2)}) async-start(s16[16,2,384,128]{3,2,1,0:T(8,128)(2,1)} %get-tuple-element.28), calls=%async_computation | async-start | bytes 6291456 | tf_op jit(solution)/shard_map/all_to_all | solution.py:404
  79.8 23.6 %all-gather.3.cloned.1.call-done = bf16[32,64,2560]{2,1,0:T(8,128)(2,1)} async-done(((bf16[2,64,2560]{2,1,0:T(8,128)(2,1)}), bf16[32,64,2560]{2,1,0:T(8,128)(2,1)}) %all-gather.3.cloned.1.call-update) | async-done | bytes 10485776 | tf_op jit(solution)/shard_map/all_gather | solution.py:395
  103.4 9.9 %shard_map.76 = (f32[2,512,2560]{2,1,0:T(8,128)S(1)}, f32[2,1,2560]{2,1,0:T(1,128)S(1)}, f32[2,1,128]{2,1,0:T(1,128)S(1)}) custom-call(bf16[16,2,64,2560]{3,2,1,0:T(8,128)(2,1)} %bitcast.6, bf16[2,512,1024]{2,1,0:T(8,128)(2,1)} %select_bitcast_fusion.refs_18_.grads_ref, f32[2,1,128]{2,1,0:T(1,128)} %get-tuple-element.23.squares_ref), custom_call_target="tpu_custom_call" | custom-call | flops 1 | bytes 1 | tf_op jit(solution)/shard_map/pallas_call | solution.py:215
  113.3 0.3 collective-permute-start.17
  113.6 2.3 %collective-permute-start.18 = (f32[2,1,128]{2,1,0:T(1,128)S(1)}, f32[2,1,128]{2,1,0:T(1,128)S(1)}, u32[]{:S(2)}, u32[]{:S(2)}) collective-permute-start(f32[2,1,128]{2,1,0:T(1,128)S(1)} %get-tuple-element.24), channel_id=1, source_target_pairs={{0,2},{1,3},{2,0},{3,1},{4,6},{5,7},{6,4},{7,5},{8,10},{9,11},{10,... | collective-permute-start | bytes 3080 | tf_op jit(solution)/shard_map/ppermute | solution.py:380
  116.0 1.5 collective-permute-done.18
  117.5 1.4 collective-permute-done.19
  119.0 2.1 %collective-permute-start.20 = (f32[2,1,128]{2,1,0:T(1,128)S(1)}, f32[2,1,128]{2,1,0:T(1,128)S(1)}, u32[]{:S(2)}, u32[]{:S(2)}) collective-permute-start(f32[2,1,128]{2,1,0:T(1,128)S(1)} %add_add_fusion.1), channel_id=1, source_target_pairs={{0,4},{1,5},{2,6},{3,7},{4,0},{5,1},{6,2},{7,3},{8,12},{9,13},{10,... | collective-permute-start | bytes 3080 | tf_op jit(solution)/shard_map/ppermute | solution.py:380
  121.1 2.0 %collective-permute-start.21 = (f32[2,1,128]{2,1,0:T(1,128)S(1)}, f32[2,1,128]{2,1,0:T(1,128)S(1)}, u32[]{:S(2)}, u32[]{:S(2)}) collective-permute-start(f32[2,1,128]{2,1,0:T(1,128)S(1)} %add_add_fusion.1), channel_id=1, source_target_pairs={{0,8},{1,9},{2,10},{3,11},{4,12},{5,13},{6,14},{7,15},{8,0},{9,1},... | collective-permute-start | bytes 3080 | tf_op jit(solution)/shard_map/ppermute | solution.py:380
  123.0 2.4 %collective-permute-start.22 = (f32[2,1,128]{2,1,0:T(1,128)S(1)}, f32[2,1,128]{2,1,0:T(1,128)S(1)}, u32[]{:S(2)}, u32[]{:S(2)}) collective-permute-start(f32[2,1,128]{2,1,0:T(1,128)S(1)} %add_add_fusion.1), channel_id=1, source_target_pairs={{0,12},{1,13},{2,14},{3,15},{4,8},{5,9},{6,10},{7,11},{8,4},{9,5},... | collective-permute-start | bytes 3080 | tf_op jit(solution)/shard_map/ppermute | solution.py:380
  126.2 2.4 %collective-permute-done.21 = f32[2,1,128]{2,1,0:T(1,128)S(1)} collective-permute-done((f32[2,1,128]{2,1,0:T(1,128)S(1)}, f32[2,1,128]{2,1,0:T(1,128)S(1)}, u32[]{:S(2)}, u32[]{:S(2)}) %collective-permute-start.21) | collective-permute-done | bytes 1056 | tf_op jit(solution)/shard_map/ppermute | solution.py:380
  128.5 0.2 collective-permute-done.22
  128.7 3.0 %shard_map.77 = s16[16,656,128]{2,1,0:T(8,128)(2,1)S(1)} custom-call(f32[1]{0:T(128)S(6)} %copy.10.clip_ref, f32[2,1,128]{2,1,0:T(1,128)S(1)} %add_add_fusion.shares_ref, f32[2,512,2560]{2,1,0:T(8,128)S(1)} %get-tuple-element.25.wide_ref.thin_ref, f32[2,512,2560]{2,1,0:T(8,128)S(1)} %get-tuple-element.25.wide_ref.thin_ref, ...), custom_call_target="tpu_custom_call" | custom-call | flops 1 | bytes 1 | tf_op jit(solution)/shard_map/pallas_call | solution.py:282
  131.8 40.7 %all_to_all.10.clipped_ref = s16[16,656,128]{2,1,0:T(8,128)(2,1)} all-to-all(s16[16,656,128]{2,1,0:T(8,128)(2,1)S(1)} %shard_map.77), channel_id=1, replica_groups=mesh['dp'=16,'tensor'=16] {'dp'}, dimensions={0} | all-to-all | bytes 5373952 | tf_op jit(solution)/shard_map/all_to_all | solution.py:410
  172.5 4.6 %shard_map.78 = f32[256,512]{1,0:T(8,128)} custom-call(s16[16,2,384,128]{3,2,1,0:T(8,128)(2,1)} %all-to-all-done.raw_ref, s16[16,656,128]{2,1,0:T(8,128)(2,1)} %all_to_all.10.clipped_ref, f32[256,512]{1,0:T(8,128)} %noise_ref.1), custom_call_target="tpu_custom_call" | custom-call | tf_op jit(solution)/shard_map/pallas_call | solution.py:355
  (52 shorter events, 0.1 us)
Async XLA Ops:
  6.5 96.8 %all-gather.3.cloned.1.call-start = ((), (), s32[]{:S(2)}) async-start(), calls=%async_computation.2 | async-start | bytes 11141120 | tf_op jit(solution)/shard_map/all_gather | solution.py:395
  8.6 11.1 %collective-permute-start = (bf16[2,64,1536]{2,1,0:T(8,128)(2,1)}, bf16[2,64,1536]{2,1,0:T(8,128)(2,1)S(1)}, u32[]{:S(2)}, u32[]{:S(2)}) collective-permute-start(bf16[2,64,1536]{2,1,0:T(8,128)(2,1)} %bitcast.10), channel_id=1, source_target_pairs={{0,2},{1,3},{2,4},{3,5},{4,6},{5,7},{6,8},{7,9},{8,10},{9,11},{10,... | collective-permute-start | bytes 1179656 | tf_op jit(solution)/shard_map/ppermute | solution.py:377
  10.5 11.1 %collective-permute-start.2 = (bf16[2,64,1536]{2,1,0:T(8,128)(2,1)}, bf16[2,64,1536]{2,1,0:T(8,128)(2,1)S(1)}, u32[]{:S(2)}, u32[]{:S(2)}) collective-permute-start(bf16[2,64,1536]{2,1,0:T(8,128)(2,1)} %bitcast.11), channel_id=1, source_target_pairs={{0,14},{1,15},{2,0},{3,1},{4,2},{5,3},{6,4},{7,5},{8,6},{9,7},{10,... | collective-permute-start | bytes 1179656 | tf_op jit(solution)/shard_map/ppermute | solution.py:377
  19.6 16.4 %copy-start.4 = (bf16[2,64,1536]{2,1,0:T(8,128)(2,1)}, bf16[2,64,1536]{2,1,0:T(8,128)(2,1)S(1)}, u32[]{:S(2)}) copy-start(bf16[2,64,1536]{2,1,0:T(8,128)(2,1)S(1)} %collective-permute-done.refs_2_) | copy-start | bytes 1179652
  19.6 12.9 %collective-permute-start.1 = (bf16[2,64,1536]{2,1,0:T(8,128)(2,1)S(1)}, bf16[2,64,1536]{2,1,0:T(8,128)(2,1)}, u32[]{:S(2)}, u32[]{:S(2)}) collective-permute-start(bf16[2,64,1536]{2,1,0:T(8,128)(2,1)S(1)} %collective-permute-done.refs_2_), channel_id=1, source_target_pairs={{0,2},{1,3},{2,4},{3,5},{4,6},{5,7},{6,8},{7,9},{8,10},{9,11},{10,... | collective-permute-start | bytes 1179656 | tf_op jit(solution)/shard_map/ppermute | solution.py:377
  21.6 14.9 %copy-start.5 = (bf16[2,64,1536]{2,1,0:T(8,128)(2,1)}, bf16[2,64,1536]{2,1,0:T(8,128)(2,1)S(1)}, u32[]{:S(2)}) copy-start(bf16[2,64,1536]{2,1,0:T(8,128)(2,1)S(1)} %collective-permute-done.2.refs_4_) | copy-start | bytes 1179652
  21.6 11.4 %collective-permute-start.3 = (bf16[2,64,1536]{2,1,0:T(8,128)(2,1)S(1)}, bf16[2,64,1536]{2,1,0:T(8,128)(2,1)}, u32[]{:S(2)}, u32[]{:S(2)}) collective-permute-start(bf16[2,64,1536]{2,1,0:T(8,128)(2,1)S(1)} %collective-permute-done.2.refs_4_), channel_id=1, source_target_pairs={{0,14},{1,15},{2,0},{3,1},{4,2},{5,3},{6,4},{7,5},{8,6},{9,7},{10,... | collective-permute-start | bytes 1179656 | tf_op jit(solution)/shard_map/ppermute | solution.py:377
  30.2 5.8 %copy-start.1 = (bf16[128,1536]{1,0:T(8,128)(2,1)S(1)}, bf16[128,1536]{1,0:T(8,128)(2,1)}, u32[]{:S(2)}) copy-start(bf16[128,1536]{1,0:T(8,128)(2,1)} %shard_map.73) | copy-start | bytes 1179652
  33.0 10.5 %collective-permute-start.9 = (bf16[2,64,1536]{2,1,0:T(8,128)(2,1)}, bf16[2,64,1536]{2,1,0:T(8,128)(2,1)S(1)}, u32[]{:S(2)}, u32[]{:S(2)}) collective-permute-start(bf16[2,64,1536]{2,1,0:T(8,128)(2,1)} %collective-permute-done.1.refs_6_), channel_id=1, source_target_pairs={{0,2},{1,3},{2,4},{3,5},{4,6},{5,7},{6,8},{7,9},{8,10},{9,11},{10,... | collective-permute-start | bytes 1179656 | tf_op jit(solution)/shard_map/ppermute | solution.py:377
  36.0 9.9 %collective-permute-start.11 = (bf16[2,64,1536]{2,1,0:T(8,128)(2,1)}, bf16[2,64,1536]{2,1,0:T(8,128)(2,1)S(1)}, u32[]{:S(2)}, u32[]{:S(2)}) collective-permute-start(bf16[2,64,1536]{2,1,0:T(8,128)(2,1)} %collective-permute-done.3.refs_8_), channel_id=1, source_target_pairs={{0,14},{1,15},{2,0},{3,1},{4,2},{5,3},{6,4},{7,5},{8,6},{9,7},{10,... | collective-permute-start | bytes 1179656 | tf_op jit(solution)/shard_map/ppermute | solution.py:377
  36.0 9.9 %collective-permute-start.4 = (bf16[2,64,1536]{2,1,0:T(8,128)(2,1)S(1)}, bf16[2,64,1536]{2,1,0:T(8,128)(2,1)S(1)}, u32[]{:S(2)}, u32[]{:S(2)}) collective-permute-start(bf16[2,64,1536]{2,1,0:T(8,128)(2,1)S(1)} %bitcast.13), channel_id=1, source_target_pairs={{0,1},{1,0},{2,3},{3,2},{4,5},{5,4},{6,7},{7,6},{8,9},{9,8},{10,11... | collective-permute-start | bytes 1179656 | tf_op jit(solution)/shard_map/ppermute | solution.py:380
  36.0 11.8 %collective-permute-start.5 = (bf16[2,64,1536]{2,1,0:T(8,128)(2,1)S(1)}, bf16[2,64,1536]{2,1,0:T(8,128)(2,1)S(1)}, u32[]{:S(2)}, u32[]{:S(2)}) collective-permute-start(bf16[2,64,1536]{2,1,0:T(8,128)(2,1)S(1)} %collective-permute-done.refs_2_), channel_id=1, source_target_pairs={{0,1},{1,0},{2,3},{3,2},{4,5},{5,4},{6,7},{7,6},{8,9},{9,8},{10,11... | collective-permute-start | bytes 1179656 | tf_op jit(solution)/shard_map/ppermute | solution.py:380
  36.5 11.6 %collective-permute-start.6 = (bf16[2,64,1536]{2,1,0:T(8,128)(2,1)S(1)}, bf16[2,64,1536]{2,1,0:T(8,128)(2,1)S(1)}, u32[]{:S(2)}, u32[]{:S(2)}) collective-permute-start(bf16[2,64,1536]{2,1,0:T(8,128)(2,1)S(1)} %collective-permute-done.2.refs_4_), channel_id=1, source_target_pairs={{0,1},{1,0},{2,3},{3,2},{4,5},{5,4},{6,7},{7,6},{8,9},{9,8},{10,11... | collective-permute-start | bytes 1179656 | tf_op jit(solution)/shard_map/ppermute | solution.py:380
  43.4 17.5 %copy-start.2 = (bf16[2,64,1536]{2,1,0:T(8,128)(2,1)}, bf16[2,64,1536]{2,1,0:T(8,128)(2,1)S(1)}, u32[]{:S(2)}) copy-start(bf16[2,64,1536]{2,1,0:T(8,128)(2,1)S(1)} %collective-permute-done.9.refs_10_) | copy-start | bytes 1179652
  43.4 4.7 %collective-permute-start.7 = (bf16[2,64,1536]{2,1,0:T(8,128)(2,1)}, bf16[2,64,1536]{2,1,0:T(8,128)(2,1)S(1)}, u32[]{:S(2)}, u32[]{:S(2)}) collective-permute-start(bf16[2,64,1536]{2,1,0:T(8,128)(2,1)} %collective-permute-done.1.refs_6_), channel_id=1, source_target_pairs={{0,1},{1,0},{2,3},{3,2},{4,5},{5,4},{6,7},{7,6},{8,9},{9,8},{10,11... | collective-permute-start | bytes 1179656 | tf_op jit(solution)/shard_map/ppermute | solution.py:380
  45.9 15.1 %copy-start.3 = (bf16[2,64,1536]{2,1,0:T(8,128)(2,1)}, bf16[2,64,1536]{2,1,0:T(8,128)(2,1)S(1)}, u32[]{:S(2)}) copy-start(bf16[2,64,1536]{2,1,0:T(8,128)(2,1)S(1)} %collective-permute-done.11.refs_12_) | copy-start | bytes 1179652
  45.9 13.6 %collective-permute-start.8 = (bf16[2,64,1536]{2,1,0:T(8,128)(2,1)}, bf16[2,64,1536]{2,1,0:T(8,128)(2,1)S(1)}, u32[]{:S(2)}, u32[]{:S(2)}) collective-permute-start(bf16[2,64,1536]{2,1,0:T(8,128)(2,1)} %collective-permute-done.3.refs_8_), channel_id=1, source_target_pairs={{0,1},{1,0},{2,3},{3,2},{4,5},{5,4},{6,7},{7,6},{8,9},{9,8},{10,11... | collective-permute-start | bytes 1179656 | tf_op jit(solution)/shard_map/ppermute | solution.py:380
  46.0 15.0 %copy-start.6 = (bf16[2,64,1536]{2,1,0:T(8,128)(2,1)}, bf16[2,64,1536]{2,1,0:T(8,128)(2,1)S(1)}, u32[]{:S(2)}) copy-start(bf16[2,64,1536]{2,1,0:T(8,128)(2,1)S(1)} %collective-permute-done.4.refs_1_) | copy-start | bytes 1179652
  46.0 11.8 %collective-permute-start.13 = (bf16[1,64,1536]{2,1,0:T(8,128)(2,1)S(1)}, bf16[1,64,1536]{2,1,0:T(8,128)(2,1)S(1)}, u32[]{:S(2)}, u32[]{:S(2)}) collective-permute-start(bf16[1,64,1536]{2,1,0:T(8,128)(2,1)S(1)} %slice.8), channel_id=1, source_target_pairs={{0,2},{1,3},{2,4},{3,5},{4,6},{5,7},{6,8},{7,9},{8,10},{9,11},{10,... | collective-permute-start | bytes 589832 | tf_op jit(solution)/shard_map/ppermute | solution.py:377
  47.8 13.2 %copy-start.7 = (bf16[2,64,1536]{2,1,0:T(8,128)(2,1)}, bf16[2,64,1536]{2,1,0:T(8,128)(2,1)S(1)}, u32[]{:S(2)}) copy-start(bf16[2,64,1536]{2,1,0:T(8,128)(2,1)S(1)} %collective-permute-done.5.refs_3_) | copy-start | bytes 1179652
  47.8 11.7 %collective-permute-start.15 = (bf16[1,64,1536]{2,1,0:T(8,128)(2,1)S(1)}, bf16[1,64,1536]{2,1,0:T(8,128)(2,1)S(1)}, u32[]{:S(2)}, u32[]{:S(2)}) collective-permute-start(bf16[1,64,1536]{2,1,0:T(8,128)(2,1)S(1)} %slice.9), channel_id=1, source_target_pairs={{0,14},{1,15},{2,0},{3,1},{4,2},{5,3},{6,4},{7,5},{8,6},{9,7},{10,... | collective-permute-start | bytes 589832 | tf_op jit(solution)/shard_map/ppermute | solution.py:377
  48.1 12.9 %copy-start.8 = (bf16[2,64,1536]{2,1,0:T(8,128)(2,1)}, bf16[2,64,1536]{2,1,0:T(8,128)(2,1)S(1)}, u32[]{:S(2)}) copy-start(bf16[2,64,1536]{2,1,0:T(8,128)(2,1)S(1)} %collective-permute-done.6.refs_5_) | copy-start | bytes 1179652
  48.1 12.9 %collective-permute-start.10 = (bf16[2,64,1536]{2,1,0:T(8,128)(2,1)S(1)}, bf16[2,64,1536]{2,1,0:T(8,128)(2,1)S(1)}, u32[]{:S(2)}, u32[]{:S(2)}) collective-permute-start(bf16[2,64,1536]{2,1,0:T(8,128)(2,1)S(1)} %collective-permute-done.9.refs_10_), channel_id=1, source_target_pairs={{0,1},{1,0},{2,3},{3,2},{4,5},{5,4},{6,7},{7,6},{8,9},{9,8},{10,11... | collective-permute-start | bytes 1179656 | tf_op jit(solution)/shard_map/ppermute | solution.py:380
  48.1 12.9 %copy-start.9 = (bf16[2,64,1536]{2,1,0:T(8,128)(2,1)}, bf16[2,64,1536]{2,1,0:T(8,128)(2,1)S(1)}, u32[]{:S(2)}) copy-start(bf16[2,64,1536]{2,1,0:T(8,128)(2,1)S(1)} %collective-permute-done.7.refs_7_) | copy-start | bytes 1179652
  48.1 12.8 %collective-permute-start.12 = (bf16[2,64,1536]{2,1,0:T(8,128)(2,1)S(1)}, bf16[2,64,1536]{2,1,0:T(8,128)(2,1)S(1)}, u32[]{:S(2)}, u32[]{:S(2)}) collective-permute-start(bf16[2,64,1536]{2,1,0:T(8,128)(2,1)S(1)} %collective-permute-done.11.refs_12_), channel_id=1, source_target_pairs={{0,1},{1,0},{2,3},{3,2},{4,5},{5,4},{6,7},{7,6},{8,9},{9,8},{10,11... | collective-permute-start | bytes 1179656 | tf_op jit(solution)/shard_map/ppermute | solution.py:380
  57.8 3.2 %copy-start.13 = (bf16[1,64,1536]{2,1,0:T(8,128)(2,1)}, bf16[1,64,1536]{2,1,0:T(8,128)(2,1)S(1)}, u32[]{:S(2)}) copy-start(bf16[1,64,1536]{2,1,0:T(8,128)(2,1)S(1)} %collective-permute-done.13.refs_14_) | copy-start | bytes 589828
  57.8 1.7 collective-permute-start.14
  59.5 1.5 copy-start.14
  59.5 1.4 collective-permute-start.16
  59.5 1.5 copy-start.10
  59.6 1.5 copy-start.15
  61.0 0.7 copy-start.16
  61.0 0.8 copy-start.11
  61.8 0.7 copy-start.12
  72.7 59.1 %all-to-all-start = ((s16[16,2,384,128]{3,2,1,0:T(8,128)(2,1)}), s16[16,2,384,128]{3,2,1,0:T(8,128)(2,1)}, u32[]{:S(2)}, u32[]{:S(2)}) async-start(s16[16,2,384,128]{3,2,1,0:T(8,128)(2,1)} %get-tuple-element.28), calls=%async_computation | async-start | bytes 6291456 | tf_op jit(solution)/shard_map/all_to_all | solution.py:404
  103.4 25.4 %copy-start = (f32[16,2,8,128]{3,2,1,0:T(8,128)S(1)}, f32[16,2,8,128]{3,2,1,0:T(8,128)}, u32[]{:S(2)}) copy-start(f32[16,2,8,128]{3,2,1,0:T(8,128)} %get-tuple-element.27.exponent_ref) | copy-start | bytes 393220
  113.3 2.7 %collective-permute-start.17 = (f32[2,1,128]{2,1,0:T(1,128)S(1)}, f32[2,1,128]{2,1,0:T(1,128)S(1)}, u32[]{:S(2)}, u32[]{:S(2)}) collective-permute-start(f32[2,1,128]{2,1,0:T(1,128)S(1)} %get-tuple-element.24), channel_id=1, source_target_pairs={{0,1},{1,0},{2,3},{3,2},{4,5},{5,4},{6,7},{7,6},{8,9},{9,8},{10,11... | collective-permute-start | bytes 3080 | tf_op jit(solution)/shard_map/ppermute | solution.py:380
  113.6 3.9 %collective-permute-start.18 = (f32[2,1,128]{2,1,0:T(1,128)S(1)}, f32[2,1,128]{2,1,0:T(1,128)S(1)}, u32[]{:S(2)}, u32[]{:S(2)}) collective-permute-start(f32[2,1,128]{2,1,0:T(1,128)S(1)} %get-tuple-element.24), channel_id=1, source_target_pairs={{0,2},{1,3},{2,0},{3,1},{4,6},{5,7},{6,4},{7,5},{8,10},{9,11},{10,... | collective-permute-start | bytes 3080 | tf_op jit(solution)/shard_map/ppermute | solution.py:380
  116.0 3.0 %collective-permute-start.19 = (f32[2,1,128]{2,1,0:T(1,128)S(1)}, f32[2,1,128]{2,1,0:T(1,128)S(1)}, u32[]{:S(2)}, u32[]{:S(2)}) collective-permute-start(f32[2,1,128]{2,1,0:T(1,128)S(1)} %get-tuple-element.24), channel_id=1, source_target_pairs={{0,3},{1,2},{2,1},{3,0},{4,7},{5,6},{6,5},{7,4},{8,11},{9,10},{10,... | collective-permute-start | bytes 3080 | tf_op jit(solution)/shard_map/ppermute | solution.py:380
  119.0 7.2 %collective-permute-start.20 = (f32[2,1,128]{2,1,0:T(1,128)S(1)}, f32[2,1,128]{2,1,0:T(1,128)S(1)}, u32[]{:S(2)}, u32[]{:S(2)}) collective-permute-start(f32[2,1,128]{2,1,0:T(1,128)S(1)} %add_add_fusion.1), channel_id=1, source_target_pairs={{0,4},{1,5},{2,6},{3,7},{4,0},{5,1},{6,2},{7,3},{8,12},{9,13},{10,... | collective-permute-start | bytes 3080 | tf_op jit(solution)/shard_map/ppermute | solution.py:380
  121.1 7.5 %collective-permute-start.21 = (f32[2,1,128]{2,1,0:T(1,128)S(1)}, f32[2,1,128]{2,1,0:T(1,128)S(1)}, u32[]{:S(2)}, u32[]{:S(2)}) collective-permute-start(f32[2,1,128]{2,1,0:T(1,128)S(1)} %add_add_fusion.1), channel_id=1, source_target_pairs={{0,8},{1,9},{2,10},{3,11},{4,12},{5,13},{6,14},{7,15},{8,0},{9,1},... | collective-permute-start | bytes 3080 | tf_op jit(solution)/shard_map/ppermute | solution.py:380
  123.0 5.7 %collective-permute-start.22 = (f32[2,1,128]{2,1,0:T(1,128)S(1)}, f32[2,1,128]{2,1,0:T(1,128)S(1)}, u32[]{:S(2)}, u32[]{:S(2)}) collective-permute-start(f32[2,1,128]{2,1,0:T(1,128)S(1)} %add_add_fusion.1), channel_id=1, source_target_pairs={{0,12},{1,13},{2,14},{3,15},{4,8},{5,9},{6,10},{7,11},{8,4},{9,5},... | collective-permute-start | bytes 3080 | tf_op jit(solution)/shard_map/ppermute | solution.py:380
Sparse Core Ops, SparseCore 0:
  33.1 70.2 all-gather.2
